TPU v7x, 512 devices: a whole 4x8x8 slice. The times are simulated.
512 devices in a mesh: member: 16 (over y, x_hi), tile: 32 (over x_lo, z, core).
Axes of the slice: x: 4 (x_hi: 2, x_lo: 2; x = x_hi * 2 + x_lo), y: 8, z: 8, core: 2. Of those that a mesh axis runs over, the one named last changes fastest.
Arguments:
- predictor_inputs: bfloat16 [16, 64, 32, 4096], P('member', None, None, 'tile'), may hold values from -6 to 6
- target: float32 [16, 32, 4096], P(None, None, 'tile'), may hold values from -6 to 6
- depth_one: float32 [64, 9], replicated, may hold values from -2 to 2
- point_one: bfloat16 [64, 64], replicated, may hold values from -0.75 to 0.75
- bias_one: float32 [64], replicated, may hold values from -3 to 3
- depth_two: float32 [64, 9], replicated, may hold values from -2 to 2
- point_two: bfloat16 [16, 64], replicated, may hold values from -0.75 to 0.75
- bias_two: float32 [16], replicated, may hold values from -3 to 3
Outputs:
- corrected_realizations: bfloat16 [16, 16, 32, 4096], P('member', None, None, 'tile')
- grad_depth_one: float32 [64, 9], replicated
- grad_point_one: float32 [64, 64], replicated
- grad_bias_one: float32 [64], replicated
- grad_depth_two: float32 [64, 9], replicated
- grad_point_two: float32 [16, 64], replicated
- grad_bias_two: float32 [16], replicated
All inputs are finite; a program needn't handle non-finite values.
Results may differ from a plain program's by a relative error of at most 0.0042.
The roundings to bfloat16 on the way count: a program that leaves them out, or rounds other values in their place, can miss the bound.
Values may be sent and summed in bfloat16 or wider, within the bound.
No kernel may reach another device: no remote copies, remote signals or barrier semaphores. Data moves between devices by JAX's collectives and lax.ppermute only.
A program may use at most 64 MiB of HBM per device.

v0:
```python
import jax
import jax.numpy as jnp
from jax import lax
from jax.sharding import PartitionSpec as P

smooth_width = 0.25
pair_weight = 0.95


def with_halo(value, sides, width):
    for axis, dim in sides:
        count, length = (lax.axis_size(axis), value.shape[dim])
        up = [(i, (i + 1) % count) for i in range(count)]
        down = [(j, i) for i, j in up]
        last = lax.slice_in_dim(value, length - width, length, axis=dim)
        leading = lax.slice_in_dim(value, 0, width, axis=dim)
        before = lax.ppermute(last, axis, up)
        after = lax.ppermute(leading, axis, down)
        value = jnp.concatenate([before, value, after], axis=dim)
    return value


def pad_poles(field):
    return jnp.pad(field, ((0, 0), (1, 1), (0, 0)))


def depthwise(padded, kernel, rows, cols):
    total = jnp.zeros((padded.shape[0], rows, cols), jnp.float32)
    for row_off in range(3):
        for col_off in range(3):
            tap = kernel[:, 3 * row_off + col_off][:, None, None]
            total = total + tap * padded[
                :, row_off : row_off + rows, col_off : col_off + cols
            ].astype(jnp.float32)
    return total


def depthwise_back(padded, kernel, rows, cols):
    total = jnp.zeros((padded.shape[0], rows, cols), jnp.float32)
    for row_off in range(3):
        for col_off in range(3):
            tap = kernel[:, 3 * row_off + col_off][:, None, None]
            total = total + tap * padded[
                :, 2 - row_off : 2 - row_off + rows, 2 - col_off : 2 - col_off + cols
            ].astype(jnp.float32)
    return total


def kernel_grad(cotan, padded, rows, cols):
    cotan_f = cotan.astype(jnp.float32)
    columns = []
    for row_off in range(3):
        for col_off in range(3):
            window = padded[:, row_off : row_off + rows, col_off : col_off + cols].astype(
                jnp.float32
            )
            columns.append(jnp.sum(cotan_f * window, axis=(1, 2)))
    return jnp.stack(columns, axis=1)


def logistic_derivative(diff):
    return diff / jnp.sqrt(diff * diff + smooth_width * smooth_width)


def contract(left, right, dims):
    return lax.dot_general(
        left, right, ((dims[0], dims[1]), ((), ())), preferred_element_type=jnp.float32
    )


def local(predictor_inputs, target, depth_one, point_one, bias_one, depth_two, point_two, bias_two):
    local_in = predictor_inputs[0]
    chans, rows, cols = local_in.shape
    hidden_n = point_one.shape[0]
    out_n = point_two.shape[0]
    padded_in = pad_poles(with_halo(local_in, (("tile", 2),), 1))
    first_bf = depthwise(padded_in, depth_one, rows, cols).astype(jnp.bfloat16)
    pre_act = (
        jnp.dot(point_one, first_bf.reshape(chans, -1), preferred_element_type=jnp.float32)
        + bias_one[:, None]
    ).reshape(hidden_n, rows, cols)
    hidden_bf = jax.nn.silu(pre_act).astype(jnp.bfloat16)
    hidden_pad = pad_poles(with_halo(hidden_bf, (("tile", 2),), 1))
    second_flat = (
        depthwise(hidden_pad, depth_two, rows, cols).astype(jnp.bfloat16).reshape(hidden_n, -1)
    )
    corrected_realizations = (
        (jnp.dot(point_two, second_flat, preferred_element_type=jnp.float32) + bias_two[:, None])
        .astype(jnp.bfloat16)
        .reshape(out_n, rows, cols)
    )
    members = lax.axis_size("member")
    cells_all = rows * cols * lax.axis_size("tile")
    current_realization = corrected_realizations.astype(jnp.float32)
    pair_sum = jnp.sum(
        logistic_derivative(
            current_realization[None]
            - lax.all_gather(corrected_realizations[None], "member", axis=0, tiled=True).astype(
                jnp.float32
            )
        ),
        axis=0,
    )
    cotan = (
        (logistic_derivative(current_realization - target) - pair_weight / (members - 1) * pair_sum)
        / cells_all
    ).astype(jnp.bfloat16)
    cot_flat = cotan.reshape(out_n, -1)
    g_point_two = contract(cot_flat, second_flat, ((1,), (1,)))
    g_bias_two = jnp.sum(cot_flat.astype(jnp.float32), axis=1)
    back_two = (
        contract(point_two, cot_flat, ((0,), (0,)))
        .astype(jnp.bfloat16)
        .reshape(hidden_n, rows, cols)
    )
    g_depth_two = kernel_grad(back_two, hidden_pad, rows, cols)
    back_pad = pad_poles(with_halo(back_two, (("tile", 2),), 1))
    back_hidden = depthwise_back(back_pad, depth_two, rows, cols)
    gate = jax.nn.sigmoid(pre_act)
    pre_flat = (
        (back_hidden * gate * (1.0 + pre_act * (1.0 - gate)))
        .astype(jnp.bfloat16)
        .reshape(hidden_n, -1)
    )
    g_point_one = contract(pre_flat, first_bf.reshape(chans, -1), ((1,), (1,)))
    g_bias_one = jnp.sum(pre_flat.astype(jnp.float32), axis=1)
    back_first = contract(point_one, pre_flat, ((0,), (0,))).reshape(chans, rows, cols)
    g_depth_one = kernel_grad(back_first, padded_in, rows, cols)
    member_totals = lax.psum(
        (g_depth_one, g_point_one, g_bias_one, g_depth_two, g_point_two, g_bias_two),
        ("member", "tile"),
    )
    return (
        corrected_realizations[None],
        member_totals[0],
        member_totals[1],
        member_totals[2],
        member_totals[3],
        member_totals[4],
        member_totals[5],
    )


def solution(mesh):
    return jax.shard_map(
        local,
        mesh=mesh,
        in_specs=(
            P("member", None, None, "tile"),
            P(None, None, "tile"),
            P(),
            P(),
            P(),
            P(),
            P(),
            P(),
        ),
        out_specs=(P("member", None, None, "tile"), P(), P(), P(), P(), P(), P()),
        check_vma=False,
    )
```

profile of v0, /device:TPU:1, one launch (start us, length us, event | category | flops | bytes accessed | tf_op | source)
XLA Modules:
  0.0 282.3 jit_solution(13439906855430810060)
XLA Ops:
  7.2 1.5 fusion.75
  8.7 5.4 %collective-permute-start = (bf16[64,32,1]{2,1,0:T(8,128)(2,1)S(1)}, bf16[64,32,1]{2,1,0:T(8,128)(2,1)S(1)}, u32[]{:S(2)}, u32[]{:S(2)}) collective-permute-start(bf16[64,32,1]{2,1,0:T(8,128)(2,1)S(1)} %get-tuple-element.41), channel_id=1, source_target_pairs={{0,1},{1,2},{2,3},{3,4},{4,5},{5,6},{6,7},{7,8},{8,9},{9,10},{10,1... | collective-permute-start | bytes 12296 | tf_op jit(solution)/shard_map/ppermute | solution.py:17
  14.1 5.3 %collective-permute-start.1 = (bf16[64,32,1]{2,1,0:T(8,128)(2,1)S(1)}, bf16[64,32,1]{2,1,0:T(8,128)(2,1)S(1)}, u32[]{:S(2)}, u32[]{:S(2)}) collective-permute-start(bf16[64,32,1]{2,1,0:T(8,128)(2,1)S(1)} %get-tuple-element.42), channel_id=1, source_target_pairs={{1,0},{2,1},{3,2},{4,3},{5,4},{6,5},{7,6},{8,7},{9,8},{10,9},{11,1... | collective-permute-start | bytes 12296 | tf_op jit(solution)/shard_map/ppermute | solution.py:18
  20.2 4.7 %collective-permute-done.1 = bf16[64,32,1]{2,1,0:T(8,128)(2,1)S(1)} collective-permute-done((bf16[64,32,1]{2,1,0:T(8,128)(2,1)S(1)}, bf16[64,32,1]{2,1,0:T(8,128)(2,1)S(1)}, u32[]{:S(2)}, u32[]{:S(2)}) %collective-permute-start.1) | collective-permute-done | bytes 4128 | tf_op jit(solution)/shard_map/ppermute | solution.py:18
  24.9 1.1 fusion.6
  26.1 2.7 fusion.15
  30.3 1.0 copy-done.6
  31.8 1.9 collective-permute-start.2
  33.8 7.2 %collective-permute-start.3 = (bf16[64,32,1]{2,1,0:T(8,128)(2,1)S(1)}, bf16[64,32,1]{2,1,0:T(8,128)(2,1)S(1)}, u32[]{:S(2)}, u32[]{:S(2)}) collective-permute-start(bf16[64,32,1]{2,1,0:T(8,128)(2,1)S(1)} %get-tuple-element.40), channel_id=1, source_target_pairs={{1,0},{2,1},{3,2},{4,3},{5,4},{6,5},{7,6},{8,7},{9,8},{10,9},{11,1... | collective-permute-start | bytes 12296 | tf_op jit(solution)/shard_map/ppermute | solution.py:18
  41.0 4.0 %collective-permute-done.3 = bf16[64,32,1]{2,1,0:T(8,128)(2,1)S(1)} collective-permute-done((bf16[64,32,1]{2,1,0:T(8,128)(2,1)S(1)}, bf16[64,32,1]{2,1,0:T(8,128)(2,1)S(1)}, u32[]{:S(2)}, u32[]{:S(2)}) %collective-permute-start.3) | collective-permute-done | bytes 4128 | tf_op jit(solution)/shard_map/ppermute | solution.py:18
  45.0 1.1 select_maximum_fusion.2
  46.2 2.7 fusion.32
  50.7 1.1 convert.2
  51.9 90.9 %all-gather.2.cloned.1.call-done = bf16[16,16,32,128]{3,2,1,0:T(8,128)(2,1)} async-done(((bf16[1,16,32,128]{3,2,1,0:T(8,128)(2,1)}), bf16[16,16,32,128]{3,2,1,0:T(8,128)(2,1)}) %all-gather.2.cloned.1.call-update) | async-done | bytes 2097168 | tf_op jit(solution)/shard_map/all_gather | solution.py:98
  142.9 2.7 multiply_reduce_fusion
  146.5 1.2 fusion.73
  147.6 7.0 %collective-permute-start.4 = (bf16[64,32,1]{2,1,0:T(8,128)(2,1)}, bf16[64,32,1]{2,1,0:T(8,128)(2,1)}, u32[]{:S(2)}, u32[]{:S(2)}) collective-permute-start(bf16[64,32,1]{2,1,0:T(8,128)(2,1)} %get-tuple-element.37), channel_id=1, source_target_pairs={{0,1},{1,2},{2,3},{3,4},{4,5},{5,6},{6,7},{7,8},{8,9},{9,10},{10,1... | collective-permute-start | bytes 12296 | tf_op jit(solution)/shard_map/ppermute | solution.py:17
  154.7 2.2 collective-permute-start.5
  156.9 3.2 %fusion.48 = (f32[64]{0:T(128)S(1)}, f32[64]{0:T(128)S(1)}, f32[64]{0:T(128)S(1)}, f32[64]{0:T(128)S(1)}, f32[64]{0:T(128)S(1)}, /*index=5*/f32[64]{0:T(128)S(1)}, f32[64]{0:T(128)S(1)}, f32[64]{0:T(128)S(1)}) fusion(bf16[64,34,130]{2,1,0:T(8,128)(2,1)S(1)} %select_maximum_fusion.2, bf16[8,8,32,128]{3,2,1,0:T(8,128)(2,1)S(1)} %copy.40, ...), kind=kLoop, calls=%fused_computation.93 | loop fusion | flops 8125952 | bytes 4204544 | tf_op jit(solution)/shard_map/reduce_sum | solution.py:57
  161.1 4.5 %collective-permute-done.5 = bf16[64,32,1]{2,1,0:T(8,128)(2,1)} collective-permute-done((bf16[64,32,1]{2,1,0:T(8,128)(2,1)}, bf16[64,32,1]{2,1,0:T(8,128)(2,1)}, u32[]{:S(2)}, u32[]{:S(2)}) %collective-permute-start.5) | collective-permute-done | bytes 4128 | tf_op jit(solution)/shard_map/ppermute | solution.py:18
  165.6 2.5 select_maximum_fusion
  168.2 4.7 %convert_reduce_fusion = (f32[64]{0:T(128)S(1)}, bf16[64,32,128]{2,1,0:T(8,128)(2,1)S(1)}) fusion(f32[8,8,32,128]{3,2,1,0:T(8,128)S(1)} %copy-done.7, bf16[64,34,130]{2,1,0:T(8,128)(2,1)S(1)} %select_maximum_fusion, f32[64]{0:T(128)S(1)} %get-tuple-element.50, f32[64]{0:T(128)S(1)} %get-tuple-element.51, f32[64]{0:T(128)S(1)} %get-tuple-element.44, ...), kind=kLoop, calls=%fused_computation.111 | loop fusion | flops 11272128 | bytes 5253632 | tf_op jit(solution)/shard_map/reduce_sum | solution.py:126
  174.5 3.2 %fusion.23 = (f32[64]{0:T(128)S(1)}, f32[64]{0:T(128)S(1)}, f32[64]{0:T(128)S(1)}, f32[64]{0:T(128)S(1)}, f32[64]{0:T(128)S(1)}, /*index=5*/f32[64]{0:T(128)S(1)}, f32[64]{0:T(128)S(1)}, f32[64]{0:T(128)S(1)}) fusion(f32[8,8,32,128]{3,2,1,0:T(8,128)S(1)} %copy.42, bf16[64,34,130]{2,1,0:T(8,128)(2,1)S(1)} %fusion.6, bf16[64,32,128]{2,1,0:T(8,128)(2,1)S(1)} %bitcast.165, ...), kind=kLoop, calls=%fused_computation.68 | loop fusion | flops 7863808 | bytes 4728832 | tf_op jit(solution)/shard_map/reduce_sum | solution.py:57
  177.7 97.8 %all-reduce.3 = (f32[64,9]{0,1:T(8,128)}, f32[64,64]{1,0:T(8,128)}, f32[64]{0:T(128)}, f32[64,9]{0,1:T(8,128)}, f32[16,64]{1,0:T(8,128)}, /*index=5*/f32[16]{0:T(128)}) all-reduce(f32[64,9]{0,1:T(8,128)S(1)} %stack.69, f32[64,64]{1,0:T(8,128)S(1)} %convolution_bitcast_fusion, ...), channel_id=1, replica_groups=mesh['member'=16,'tile'=32] {'member','tile'}, use_global_device_ids=true, to_apply=%region_10.11 | all-reduce | flops 6352 | bytes 50816 | tf_op jit(solution)/shard_map/psum | solution.py:129
  (81 shorter events, 8.1 us)
Async XLA Ops:
  7.2 21.7 %copy-start = (bf16[64,64]{1,0:T(8,128)(2,1)S(1)}, bf16[64,64]{1,0:T(8,128)(2,1)}, u32[]{:S(2)}) copy-start(bf16[64,64]{1,0:T(8,128)(2,1)} %param.11) | copy-start | bytes 24580
  7.2 17.7 %copy-start.1 = (bf16[1,64,32,128]{3,2,1,0:T(8,128)(2,1)S(1)}, bf16[1,64,32,128]{3,2,1,0:T(8,128)(2,1)}, u32[]{:S(2)}) copy-start(bf16[1,64,32,128]{3,2,1,0:T(8,128)(2,1)} %param.8) | copy-start | bytes 1572868
  7.2 12.2 %copy-start.25 = (f32[64,9]{0,1:T(8,128)S(1)}, f32[64,9]{0,1:T(8,128)}, u32[]{:S(2)}) copy-start(f32[64,9]{0,1:T(8,128)} %param.10) | copy-start | bytes 6916
  7.2 135.7 %all-gather.2.cloned.1.call-start = ((), (), s32[]{:S(2)}) async-start(), calls=%async_computation | async-start | bytes 2228224 | tf_op jit(solution)/shard_map/all_gather | solution.py:98
  8.7 11.5 %collective-permute-start = (bf16[64,32,1]{2,1,0:T(8,128)(2,1)S(1)}, bf16[64,32,1]{2,1,0:T(8,128)(2,1)S(1)}, u32[]{:S(2)}, u32[]{:S(2)}) collective-permute-start(bf16[64,32,1]{2,1,0:T(8,128)(2,1)S(1)} %get-tuple-element.41), channel_id=1, source_target_pairs={{0,1},{1,2},{2,3},{3,4},{4,5},{5,6},{6,7},{7,8},{8,9},{9,10},{10,1... | collective-permute-start | bytes 12296 | tf_op jit(solution)/shard_map/ppermute | solution.py:17
  14.1 10.8 %collective-permute-start.1 = (bf16[64,32,1]{2,1,0:T(8,128)(2,1)S(1)}, bf16[64,32,1]{2,1,0:T(8,128)(2,1)S(1)}, u32[]{:S(2)}, u32[]{:S(2)}) collective-permute-start(bf16[64,32,1]{2,1,0:T(8,128)(2,1)S(1)} %get-tuple-element.42), channel_id=1, source_target_pairs={{1,0},{2,1},{3,2},{4,3},{5,4},{6,5},{7,6},{8,7},{9,8},{10,9},{11,1... | collective-permute-start | bytes 12296 | tf_op jit(solution)/shard_map/ppermute | solution.py:18
  20.2 8.6 %copy-start.8 = (bf16[64,32,1]{2,1,0:T(8,128)(2,1)}, bf16[64,32,1]{2,1,0:T(8,128)(2,1)S(1)}, u32[]{:S(2)}) copy-start(bf16[64,32,1]{2,1,0:T(8,128)(2,1)S(1)} %collective-permute-done) | copy-start | bytes 12292
  31.3 9.6 %copy-start.26 = (f32[64,9]{0,1:T(8,128)S(1)}, f32[64,9]{0,1:T(8,128)}, u32[]{:S(2)}) copy-start(f32[64,9]{0,1:T(8,128)} %param.13) | copy-start | bytes 6916
  31.6 14.6 %copy-start.2 = (bf16[64,32,128]{2,1,0:T(8,128)(2,1)}, bf16[64,32,128]{2,1,0:T(8,128)(2,1)S(1)}, u32[]{:S(2)}) copy-start(bf16[64,32,128]{2,1,0:T(8,128)(2,1)S(1)} %fusion.53) | copy-start | bytes 1572868
  31.8 9.1 %collective-permute-start.2 = (bf16[64,32,1]{2,1,0:T(8,128)(2,1)S(1)}, bf16[64,32,1]{2,1,0:T(8,128)(2,1)S(1)}, u32[]{:S(2)}, u32[]{:S(2)}) collective-permute-start(bf16[64,32,1]{2,1,0:T(8,128)(2,1)S(1)} %get-tuple-element.39), channel_id=1, source_target_pairs={{0,1},{1,2},{2,3},{3,4},{4,5},{5,6},{6,7},{7,8},{8,9},{9,10},{10,1... | collective-permute-start | bytes 12296 | tf_op jit(solution)/shard_map/ppermute | solution.py:17
  33.8 11.2 %collective-permute-start.3 = (bf16[64,32,1]{2,1,0:T(8,128)(2,1)S(1)}, bf16[64,32,1]{2,1,0:T(8,128)(2,1)S(1)}, u32[]{:S(2)}, u32[]{:S(2)}) collective-permute-start(bf16[64,32,1]{2,1,0:T(8,128)(2,1)S(1)} %get-tuple-element.40), channel_id=1, source_target_pairs={{1,0},{2,1},{3,2},{4,3},{5,4},{6,5},{7,6},{8,7},{9,8},{10,9},{11,1... | collective-permute-start | bytes 12296 | tf_op jit(solution)/shard_map/ppermute | solution.py:18
  41.0 8.0 %copy-start.12 = (bf16[64,32,1]{2,1,0:T(8,128)(2,1)}, bf16[64,32,1]{2,1,0:T(8,128)(2,1)S(1)}, u32[]{:S(2)}) copy-start(bf16[64,32,1]{2,1,0:T(8,128)(2,1)S(1)} %collective-permute-done.2) | copy-start | bytes 12292
  45.0 3.9 %copy-start.14 = (bf16[64,32,1]{2,1,0:T(8,128)(2,1)}, bf16[64,32,1]{2,1,0:T(8,128)(2,1)S(1)}, u32[]{:S(2)}) copy-start(bf16[64,32,1]{2,1,0:T(8,128)(2,1)S(1)} %collective-permute-done.3) | copy-start | bytes 12292
  146.3 10.6 %copy-start.3 = (bf16[64,32,128]{2,1,0:T(8,128)(2,1)S(1)}, bf16[64,32,128]{2,1,0:T(8,128)(2,1)}, u32[]{:S(2)}) copy-start(bf16[64,32,128]{2,1,0:T(8,128)(2,1)} %copy-done.2) | copy-start | bytes 1572868
  146.3 10.6 %copy-start.13 = (bf16[64,32,1]{2,1,0:T(8,128)(2,1)S(1)}, bf16[64,32,1]{2,1,0:T(8,128)(2,1)}, u32[]{:S(2)}) copy-start(bf16[64,32,1]{2,1,0:T(8,128)(2,1)} %copy-done.12) | copy-start | bytes 12292
  146.3 10.6 %copy-start.15 = (bf16[64,32,1]{2,1,0:T(8,128)(2,1)S(1)}, bf16[64,32,1]{2,1,0:T(8,128)(2,1)}, u32[]{:S(2)}) copy-start(bf16[64,32,1]{2,1,0:T(8,128)(2,1)} %copy-done.14) | copy-start | bytes 12292
  146.5 13.7 %copy-start.4 = (bf16[8,8,32,128]{3,2,1,0:T(8,128)(2,1)}, bf16[8,8,32,128]{3,2,1,0:T(8,128)(2,1)S(1)}, u32[]{:S(2)}) copy-start(bf16[8,8,32,128]{3,2,1,0:T(8,128)(2,1)S(1)} %copy.40) | copy-start | bytes 1572868
  147.6 13.4 %collective-permute-start.4 = (bf16[64,32,1]{2,1,0:T(8,128)(2,1)}, bf16[64,32,1]{2,1,0:T(8,128)(2,1)}, u32[]{:S(2)}, u32[]{:S(2)}) collective-permute-start(bf16[64,32,1]{2,1,0:T(8,128)(2,1)} %get-tuple-element.37), channel_id=1, source_target_pairs={{0,1},{1,2},{2,3},{3,4},{4,5},{5,6},{6,7},{7,8},{8,9},{9,10},{10,1... | collective-permute-start | bytes 12296 | tf_op jit(solution)/shard_map/ppermute | solution.py:17
  154.7 5.5 %copy-start.22 = (bf16[64,32,128]{2,1,0:T(8,128)(2,1)S(1)}, bf16[64,32,128]{2,1,0:T(8,128)(2,1)}, u32[]{:S(2)}) copy-start(bf16[64,32,128]{2,1,0:T(8,128)(2,1)} %copy-done.21) | copy-start | bytes 1572868
  154.7 10.9 %collective-permute-start.5 = (bf16[64,32,1]{2,1,0:T(8,128)(2,1)}, bf16[64,32,1]{2,1,0:T(8,128)(2,1)}, u32[]{:S(2)}, u32[]{:S(2)}) collective-permute-start(bf16[64,32,1]{2,1,0:T(8,128)(2,1)} %get-tuple-element.38), channel_id=1, source_target_pairs={{1,0},{2,1},{3,2},{4,3},{5,4},{6,5},{7,6},{8,7},{9,8},{10,9},{11,1... | collective-permute-start | bytes 12296 | tf_op jit(solution)/shard_map/ppermute | solution.py:18
  160.2 8.0 %copy-start.7 = (f32[8,8,32,128]{3,2,1,0:T(8,128)S(1)}, f32[8,8,32,128]{3,2,1,0:T(8,128)}, u32[]{:S(2)}) copy-start(f32[8,8,32,128]{3,2,1,0:T(8,128)} %copy-done.6) | copy-start | bytes 3145732
  160.5 7.7 %copy-start.5 = (bf16[8,8,32,128]{3,2,1,0:T(8,128)(2,1)S(1)}, bf16[8,8,32,128]{3,2,1,0:T(8,128)(2,1)}, u32[]{:S(2)}) copy-start(bf16[8,8,32,128]{3,2,1,0:T(8,128)(2,1)} %copy-done.4) | copy-start | bytes 1572868
  168.2 4.7 %copy-start.20 = (bf16[64,32,128]{2,1,0:T(8,128)(2,1)S(1)}, bf16[64,32,128]{2,1,0:T(8,128)(2,1)}, u32[]{:S(2)}) copy-start(bf16[64,32,128]{2,1,0:T(8,128)(2,1)} %copy-done.19) | copy-start | bytes 1572868
  168.2 5.1 %copy-start.16 = (f32[8,8,32,128]{3,2,1,0:T(8,128)S(1)}, f32[8,8,32,128]{3,2,1,0:T(8,128)}, u32[]{:S(2)}) copy-start(f32[8,8,32,128]{3,2,1,0:T(8,128)} %convert.2) | copy-start | bytes 3145732
  (12 other events, 27.4 us)
Sparse Core Ops, SparseCore 0:
  50.9 91.9 all-gather.1
where the time goes:
time: 283 us; the launch traced here: 282 us
  waiting for transfers between devices  106 us (37%)
  blocking collectives  97.8 us (35%)
  starting transfers between devices  29.1 us (10%)
  other arithmetic  25.6 us (9%)
  between operations  14.5 us (5%)
  local copies, waits for them, and re-layouts  7.11 us (3%)
    psum x1, blocking collectives, local(): lax.psum((g_depth_one, g_point_one, g_bias_one, g_depth_two, g_point_two,...  97.8 us
    all_gather x1, waiting for transfers between devices, local(): lax.all_gather(corrected_realizations[None], 'member', axis=0, tiled=True)  90.9 us
    ppermute x3, starting transfers between devices, with_halo(): after = lax.ppermute(leading, axis, down)  14.7 us
    ppermute x3, starting transfers between devices, with_halo(): before = lax.ppermute(last, axis, up)  14.3 us
    ppermute x3, waiting for transfers between devices, with_halo(): after = lax.ppermute(leading, axis, down)  13.3 us
    reduce_sum x2, other arithmetic, kernel_grad(): columns.append(jnp.sum(cotan_f * window, axis=(1, 2)))  6.38 us
  transfers between devices with their start and end apart: 7, of which 6 were waited for; matrix products, arithmetic and copies ran while one was open for 2% of the time, Pallas kernels for 0%

commit v1 on v0

v1 whole, which is shorter than its diff:
```python
import functools

import jax
import jax.numpy as jnp
from jax import lax
from jax.experimental import pallas as pl
from jax.experimental.pallas import tpu as pltpu
from jax.sharding import PartitionSpec as P

smooth_width = 0.25
pair_weight = 0.95

slabs = 16
pitch = 160
own = 16
wide = 144
chunk = 48
edge_rows = 56

f32 = jnp.float32
bf16 = jnp.bfloat16


def lanes_of(shape):
    return lax.broadcasted_iota(jnp.int32, shape, len(shape) - 1)


def dot(left, right, left_dim, right_dim):
    return lax.dot_general(
        left, right, (((left_dim,), (right_dim,)), ((), ())), preferred_element_type=f32
    )


def rounded(value):
    return value.astype(bf16).astype(f32)


def wrap_slabs(ref):
    last = pltpu.roll(ref[slabs], 64, 1)
    ref[0] = jnp.where(lanes_of(last.shape) >= 64, last, 0.0)
    first = pltpu.roll(ref[1], 64, 1)
    ref[slabs + 1] = jnp.where(lanes_of(first.shape) < 64, first, 0.0)


def both_halves(row):
    return jnp.concatenate([row, row], axis=1)


def edge_kernel(x_ref, target_ref, xt_ref, first_ref, last_ref, rows_scr):
    rows_scr[...] = x_ref[...].reshape(64 * 32, 128).astype(f32)

    def body(p, _):
        here = jnp.concatenate(
            [rows_scr[pl.ds(p, 64, stride=32), :], rows_scr[pl.ds(p + 16, 64, stride=32), :]],
            axis=0,
        )
        turned = here.T
        xt_ref[p] = turned
        for j in range(3):
            first_ref[pl.ds(16 * j + p, 1), :] = turned[j : j + 1]
            last_ref[pl.ds(16 * j + p, 1), :] = turned[125 + j : 126 + j]
        return 0

    lax.fori_loop(0, slabs, body, 0)
    for k in range(4):
        turned = target_ref[4 * k : 4 * k + 4].reshape(128, 128).T
        first_ref[48 + k : 49 + k, :] = turned[0:1]
        last_ref[48 + k : 49 + k, :] = turned[127:128]
    first_ref[52:56, :] = jnp.zeros((4, 128), f32)
    last_ref[52:56, :] = jnp.zeros((4, 128), f32)


def forward_kernel(
    xt_ref, left_ref, right_ref, depth_one_ref, point_one_ref, bias_one_ref,
    depth_two_ref, point_two_ref, bias_two_ref,
    out_ref, send_ref, xs_ref, first_ref, gate_ref, hidden_ref, second_ref,
    one_ref, two_ref, taps_two_ref,
    hs_ref, y_ref, edge_ref, taps_one_ref, turn_ref, bias_ref,
):
    turn_ref[...] = jnp.zeros((128, 128), f32)
    turn_ref[0:64, 0:9] = depth_one_ref[...]
    taps = turn_ref[...].T[0:16]
    taps_one_ref[...] = taps + pltpu.roll(taps, 64, 1)
    turn_ref[0:64, 0:9] = depth_two_ref[...]
    taps = turn_ref[...].T[0:16]
    taps_two_ref[...] = taps + pltpu.roll(taps, 64, 1)
    turn_ref[...] = jnp.zeros((128, 128), f32)
    turn_ref[0:1, 0:16] = bias_two_ref[...]
    column = jnp.broadcast_to(turn_ref[...].T[0:16, 0:1], (16, 128))
    bias_ref[0:16] = column
    bias_ref[16:32] = column
    turn_ref[...] = jnp.zeros((128, 128), f32)
    weight = point_one_ref[...].astype(f32)
    turn_ref[0:64, 0:64] = weight
    turn_ref[64:128, 64:128] = weight
    one_ref[...] = turn_ref[...].astype(bf16)
    one_turned = turn_ref[...].T.astype(bf16)
    weight = point_two_ref[...].astype(f32)
    zero = jnp.zeros((16, 64), f32)
    two = jnp.concatenate(
        [jnp.concatenate([weight, zero], axis=1), jnp.concatenate([zero, weight], axis=1)], axis=0
    ).astype(bf16)
    two_ref[...] = two
    bias_one = both_halves(bias_one_ref[...])

    for k in range(slabs + 2):
        xs_ref[k, 0:16, :] = jnp.zeros((16, 128), f32)
        xs_ref[k, 144:160, :] = jnp.zeros((16, 128), f32)
    for p in range(slabs):
        xs_ref[p + 1, own : own + 128, :] = xt_ref[p]
        for j in range(3):
            xs_ref[p + 1, 13 + j : 14 + j, :] = left_ref[16 * j + p : 16 * j + p + 1, :]
            xs_ref[p + 1, 144 + j : 145 + j, :] = right_ref[16 * j + p : 16 * j + p + 1, :]
    wrap_slabs(xs_ref)

    def first_body(p, _):
        total = jnp.zeros((wide, 128), f32)
        for a in range(3):
            for b in range(3):
                tap = taps_one_ref[3 * a + b : 3 * a + b + 1, :]
                total = total + tap * xs_ref[p + a, 7 + b : 7 + b + wide, :]
        first_ref[p] = total[8:136].astype(bf16)
        pre = dot(total.astype(bf16), one_turned, 1, 0) + bias_one
        gate = 1.0 / (1.0 + jnp.exp(-pre))
        hidden = rounded(pre * gate)
        hs_ref[p + 1, 8 : 8 + wide, :] = hidden
        hidden_ref[p] = hidden[8:136].astype(bf16)
        gate_ref[p] = (gate * (1.0 + pre * (1.0 - gate)))[8:136]
        return 0

    for k in range(slabs + 2):
        hs_ref[k, 0:8, :] = jnp.zeros((8, 128), f32)
        hs_ref[k, 152:160, :] = jnp.zeros((8, 128), f32)
    lax.fori_loop(0, slabs, first_body, 0)
    wrap_slabs(hs_ref)
    y_ref[...] = jnp.zeros(y_ref.shape, f32)
    edge_ref[...] = jnp.zeros(edge_ref.shape, f32)

    def second_body(p, _):
        total = jnp.zeros((wide, 128), f32)
        for a in range(3):
            for b in range(3):
                tap = taps_two_ref[3 * a + b : 3 * a + b + 1, :]
                total = total + tap * hs_ref[p + a, 7 + b : 7 + b + wide, :]
        second = total[8:136].astype(bf16)
        second_ref[p] = second
        edge_ref[pl.ds(p, 1), :] = total[7:8]
        edge_ref[pl.ds(16 + p, 1), :] = total[136:137]
        y = dot(two, second, 1, 1) + bias_ref[...]
        y_ref[pl.ds(p, 16, stride=chunk), :] = y[0:16]
        y_ref[pl.ds(16 + p, 16, stride=chunk), :] = y[16:32]
        return 0

    lax.fori_loop(0, slabs, second_body, 0)
    y = dot(two, edge_ref[...].astype(bf16), 1, 1) + bias_ref[...]
    lane = lanes_of((16, 128))
    y = jnp.where(lane < 32, y[0:16], jnp.where(lane < 64, pltpu.roll(y[16:32], 32, 1), 0.0))
    y_ref[pl.ds(32, 16, stride=chunk), :] = y
    send = y_ref[...].astype(bf16).reshape(16, chunk, 128)
    send_ref[...] = send
    out_ref[0] = send[:, 0:32]


def slope(diff):
    return diff * lax.rsqrt(diff * diff + smooth_width * smooth_width)


def crps_kernel(cells_all, x_ref, target_ref, left_ref, right_ref, out_ref):
    members = x_ref.shape[0]
    me = lax.axis_index("member")
    turn = lax.rem(4 - lax.rem(me, 4), 4) * 32
    left = left_ref[pl.ds(48 + me // 4, 1), :]
    right = right_ref[pl.ds(48 + me // 4, 1), :]
    left = pltpu.roll(jnp.broadcast_to(left, (16, 128)), turn, 1)
    right = pltpu.roll(jnp.broadcast_to(right, (16, 128)), turn, 1)
    lane = lanes_of((16, 128))
    halo = jnp.where(
        lane < 16,
        left,
        jnp.where(
            lane < 32,
            pltpu.roll(right, 16, 1),
            jnp.where(lane < 48, pltpu.roll(left, 16, 1), pltpu.roll(right, 32, 1)),
        ),
    )
    for part in range(3):
        rows = slice(16 * part, 16 * part + 16)
        x = [x_ref[i, rows, :].astype(f32) for i in range(members)]
        total = [None] * members
        for i in range(members):
            for j in range(i + 1, members):
                s = slope(x[i] - x[j])
                total[i] = s if total[i] is None else total[i] + s
                total[j] = -s if total[j] is None else total[j] - s
        aim = halo if part == 2 else target_ref[me, rows, :]
        for i in range(members):
            value = slope(x[i] - aim) - pair_weight / (members - 1) * total[i]
            out_ref[i, rows, :] = (value / cells_all).astype(bf16)


def tap_sum(value):
    return jnp.sum(value.reshape(16, 8, 128), axis=0)


def backward_kernel(
    cot_ref, xs_ref, first_ref, gate_ref, hidden_ref, second_ref, one_ref, two_ref, taps_two_ref,
    out_ref,
    cf_ref, bs_ref, sums_ref, cot_sum_ref, point_two_ref, point_one_ref, other_ref,
):
    cf_ref[...] = cot_ref[...].reshape(16 * chunk, 128).astype(f32)
    two = two_ref[...]
    one = one_ref[...]
    sums_ref[...] = jnp.zeros(sums_ref.shape, f32)
    cot_sum_ref[...] = jnp.zeros(cot_sum_ref.shape, f32)
    point_two_ref[...] = jnp.zeros(point_two_ref.shape, f32)
    point_one_ref[...] = jnp.zeros(point_one_ref.shape, f32)
    other_ref[...] = jnp.zeros(other_ref.shape, f32)

    def cot_body(p, _):
        cot = jnp.concatenate(
            [cf_ref[pl.ds(p, 16, stride=chunk), :], cf_ref[pl.ds(16 + p, 16, stride=chunk), :]], axis=0
        )
        cot_sum_ref[...] += cot
        cot = cot.astype(bf16)
        bs_ref[p + 1, own : own + 128, :] = rounded(dot(cot, two, 0, 0))
        point_two_ref[...] += dot(cot, second_ref[p], 1, 0)
        return 0

    lax.fori_loop(0, slabs, cot_body, 0)
    halo = cf_ref[pl.ds(32, 16, stride=chunk), :]
    halo = jnp.concatenate([halo, pltpu.roll(halo, 96, 1)], axis=0).astype(bf16)
    halo = rounded(dot(halo, two, 0, 0))
    for p in range(slabs):
        bs_ref[p + 1, 15:16, :] = halo[p : p + 1]
        bs_ref[p + 1, 144:145, :] = halo[16 + p : 17 + p]
    wrap_slabs(bs_ref)

    def body(p, _):
        total = jnp.zeros((128, 128), f32)
        hidden = hidden_ref[p].astype(f32)
        for a in range(3):
            for b in range(3):
                t = 3 * a + b
                back = bs_ref[p + 2 - a, 17 - b : 145 - b, :]
                total = total + taps_two_ref[t : t + 1, :] * back
                sums_ref[9 + t] += tap_sum(back * hidden)
        back_pre = (total * gate_ref[p]).astype(bf16)
        sums_ref[18] += tap_sum(back_pre.astype(f32))
        point_one_ref[...] += dot(back_pre, first_ref[p], 0, 0)
        back_first = dot(back_pre, one, 1, 0)
        for a in range(3):
            for b in range(3):
                sums_ref[3 * a + b] += tap_sum(back_first * xs_ref[p + a, 15 + b : 143 + b, :])
        return 0

    lax.fori_loop(0, slabs, body, 0)
    for t in range(19):
        total = jnp.sum(sums_ref[t], axis=0, keepdims=True)
        other_ref[t : t + 1, :] = total + pltpu.roll(total, 64, 1)
    other_ref[24:40, :] = pltpu.roll(point_two_ref[0:16], 64, 1) + point_two_ref[16:32]
    bias_two = jnp.sum(cot_sum_ref[0:16] + cot_sum_ref[16:32], axis=1, keepdims=True)
    other_ref[40:56, :] = jnp.broadcast_to(bias_two, (16, 128))
    point_one = point_one_ref[0:64] + pltpu.roll(point_one_ref[64:128], 64, 1)
    packed = jnp.where(lanes_of((64, 128)) < 64, point_one, other_ref[...])
    out_ref[...] = packed.reshape(out_ref.shape)


def call(kernel, out_shape, scratch, flops):
    return pl.pallas_call(
        kernel,
        out_shape=out_shape,
        scratch_shapes=scratch,
        compiler_params=pltpu.CompilerParams(vmem_limit_bytes=24 * 1024 * 1024),
        cost_estimate=pl.CostEstimate(flops=flops, bytes_accessed=4 << 20, transcendentals=0),
    )


def shape(dims, dtype):
    return jax.ShapeDtypeStruct(dims, dtype)


def local(predictor_inputs, target, depth_one, point_one, bias_one, depth_two, point_two, bias_two):
    members = lax.axis_size("member")
    tiles = lax.axis_size("tile")
    _, chans, rows, cols = predictor_inputs.shape
    slab = (slabs, cols, 128)
    xt, first_cols, last_cols = call(
        edge_kernel,
        (shape(slab, f32), shape((edge_rows, 128), f32), shape((edge_rows, 128), f32)),
        [pltpu.VMEM((chans * rows, 128), f32)],
        1 << 20,
    )(predictor_inputs[0], target)
    up = [(i, (i + 1) % tiles) for i in range(tiles)]
    left = lax.ppermute(last_cols, "tile", up)
    right = lax.ppermute(first_cols, "tile", [(j, i) for i, j in up])
    out, send, xs, first, gate, hidden, second, one, two, taps_two = call(
        forward_kernel,
        (
            shape((1, 16, rows, cols), bf16),
            shape((16, chunk, 128), bf16),
            shape((slabs + 2, pitch, 128), f32),
            shape(slab, bf16),
            shape(slab, f32),
            shape(slab, bf16),
            shape(slab, bf16),
            shape((128, 128), bf16),
            shape((32, 128), bf16),
            shape((16, 128), f32),
        ),
        [
            pltpu.VMEM((slabs + 2, pitch, 128), f32),
            pltpu.VMEM((16 * chunk, 128), f32),
            pltpu.VMEM((128, 128), f32),
            pltpu.VMEM((16, 128), f32),
            pltpu.VMEM((128, 128), f32),
            pltpu.VMEM((32, 128), f32),
        ],
        1 << 28,
    )(xt, left, right, depth_one, point_one, bias_one[None], depth_two, point_two, bias_two[None])
    seen = lax.all_to_all(send, "member", 0, 0, tiled=True)
    cot = call(
        functools.partial(crps_kernel, rows * cols * tiles),
        shape((members, chunk, 128), bf16),
        [],
        1 << 24,
    )(seen, target, left, right)
    cot = lax.all_to_all(cot, "member", 0, 0, tiled=True)
    packed = call(
        backward_kernel,
        shape((members, 64 // members, 128), f32),
        [
            pltpu.VMEM((16 * chunk, 128), f32),
            pltpu.VMEM((slabs + 2, pitch, 128), f32),
            pltpu.VMEM((19, 8, 128), f32),
            pltpu.VMEM((32, 128), f32),
            pltpu.VMEM((32, 128), f32),
            pltpu.VMEM((128, 128), f32),
            pltpu.VMEM((64, 128), f32),
        ],
        1 << 28,
    )(cot, xs, first, gate, hidden, second, one, two, taps_two)
    part = jnp.sum(lax.all_to_all(packed, "member", 0, 0, tiled=True), axis=0)
    part = jnp.broadcast_to(part[None], (tiles,) + part.shape)
    part = jnp.sum(lax.all_to_all(part, "tile", 0, 0, tiled=True), axis=0)
    part = jnp.broadcast_to(part[None], (members,) + part.shape)
    total = lax.all_to_all(part, "member", 0, 0, tiled=True).reshape(64, 128)
    other = total[:, 64:]
    return (
        out,
        other[0:9].T,
        total[:, :64],
        other[18],
        other[9:18].T,
        other[24:40],
        other[40:56, 0],
    )


def solution(mesh):
    return jax.shard_map(
        local,
        mesh=mesh,
        in_specs=(
            P("member", None, None, "tile"),
            P(None, None, "tile"),
            P(),
            P(),
            P(),
            P(),
            P(),
            P(),
        ),
        out_specs=(P("member", None, None, "tile"), P(), P(), P(), P(), P(), P()),
        check_vma=False,
    )
```

time: 283 us -> 118 us (0.42)
  waiting for transfers between devices: 106 us -> 0.01 us
  other arithmetic: 25.6 us -> 0.07 us
  blocking collectives: 97.8 us -> 78.1 us
  starting transfers between devices: 29.1 us -> 10.7 us
  Pallas kernels: 0 us -> 18 us
  between operations: 14.5 us -> 0.7 us
    psum x1 -> x0, blocking collectives: 97.8 us -> none  [local(): lax.psum((g_depth_one, g_point_one, g_bias_one, g_depth_two, g_point_two,...]
    all_gather x1 -> x0, waiting for transfers between devices: 90.9 us -> none  [local(): lax.all_gather(corrected_realizations[None], 'member', axis=0, tiled=True)]
    all_to_all x0 -> x5, blocking collectives: none -> 78.1 us  [the longest x1 23.6 us: local(): part = jnp.sum(lax.all_to_all(part, 'tile', 0, 0, tiled=True), axis=0)]
    ppermute x6 -> x2, starting transfers between devices: 29 us -> 10.7 us  [the longest x1 5.39 us: local(): left = lax.ppermute(last_cols, 'tile', up)]
    pallas_call x0 -> x4, Pallas kernels: none -> 18 us  [the longest x1 7.96 us: local(): call(backward_kernel, shape((members, 64 // members, 128), f32), [pltpu.V...]
    ppermute x6 -> x2, waiting for transfers between devices: 14.6 us -> 0.01 us  [the longest x1 0.01 us: local(): left = lax.ppermute(last_cols, 'tile', up)]
    reduce_sum x5 -> x2, other arithmetic: 14 us -> 0.07 us  [the longest x1 0.04 us: local(): part = jnp.sum(lax.all_to_all(part, 'tile', 0, 0, tiled=True), axis=0)]
    convert_element_type x3 -> x0, other arithmetic: 5.71 us -> none  [the longest x1 2.71 us: local(): first_bf = depthwise(padded_in, depth_one, rows, cols).astype(jnp.bfloat16)]
  transfers between devices with their start and end apart: 7 -> 2, of which waited for: 6 -> 0; matrix products, arithmetic and copies ran while one was open for 2% -> 1% of each run, Pallas kernels for 0% -> 0%
where the time goes in v1:
time: 118 us; the launch traced here: 117 us
  blocking collectives  78.1 us (66%)
  Pallas kernels  18 us (15%)
  starting transfers between devices  10.7 us (9%)
  local copies, waits for them, and re-layouts  9.52 us (8%)
    all_to_all x1, blocking collectives, local(): part = jnp.sum(lax.all_to_all(part, 'tile', 0, 0, tiled=True), axis=0)  23.6 us
    all_to_all x1, blocking collectives, local(): seen = lax.all_to_all(send, 'member', 0, 0, tiled=True)  18 us
    all_to_all x1, blocking collectives, local(): cot = lax.all_to_all(cot, 'member', 0, 0, tiled=True)  13.2 us
    all_to_all x1, blocking collectives, local(): part = jnp.sum(lax.all_to_all(packed, 'member', 0, 0, tiled=True), axis=0)  11.7 us
    all_to_all x1, blocking collectives, local(): total = lax.all_to_all(part, 'member', 0, 0, tiled=True).reshape(64, 128)  11.7 us
    pallas_call x1, Pallas kernels, local(): call(backward_kernel, shape((members, 64 // members, 128), f32), [pltpu.V...  7.96 us
    pallas_call x1, Pallas kernels, local(): call(forward_kernel, (shape((1, 16, rows, cols), bf16), shape((16, chunk,...  7.09 us
    unnamed x17, local copies, waits for them, and re-layouts  6.88 us
  transfers between devices with their start and end apart: 2, of which 0 were waited for; matrix products, arithmetic and copies ran while one was open for 1% of the time, Pallas kernels for 0%

profile of v1, /device:TPU:1, one launch (start us, length us, event | category | flops | bytes accessed | tf_op | source)
XLA Modules:
  0.0 117.1 jit_solution(2741162806682249457)
XLA Ops:
  0.6 0.9 copy-done
  1.6 1.0 copy-done.2
  2.6 2.1 %shard_map.135 = (f32[16,128,128]{2,1,0:T(8,128)S(1)}, f32[56,128]{1,0:T(8,128)S(1)}, f32[56,128]{1,0:T(8,128)S(1)}) custom-call(bf16[64,32,128]{2,1,0:T(8,128)(2,1)S(1)} %bitcast.11, f32[16,32,128]{2,1,0:T(8,128)S(1)} %copy-done), custom_call_target="tpu_custom_call" | custom-call | flops 1048576 | bytes 4194304 | tf_op jit(solution)/shard_map/pallas_call | solution.py:287
  4.7 5.4 %collective-permute-start = (f32[56,128]{1,0:T(8,128)S(1)}, f32[56,128]{1,0:T(8,128)S(1)}, u32[]{:S(2)}, u32[]{:S(2)}) collective-permute-start(f32[56,128]{1,0:T(8,128)S(1)} %get-tuple-element.21), channel_id=1, source_target_pairs={{0,1},{1,2},{2,3},{3,4},{4,5},{5,6},{6,7},{7,8},{8,9},{9,10},{10,1... | collective-permute-start | bytes 86024 | tf_op jit(solution)/shard_map/ppermute | solution.py:294
  10.1 5.3 %collective-permute-start.1 = (f32[56,128]{1,0:T(8,128)S(1)}, f32[56,128]{1,0:T(8,128)S(1)}, u32[]{:S(2)}, u32[]{:S(2)}) collective-permute-start(f32[56,128]{1,0:T(8,128)S(1)} %get-tuple-element.22), channel_id=1, source_target_pairs={{1,0},{2,1},{3,2},{4,3},{5,4},{6,5},{7,6},{8,7},{9,8},{10,9},{11,1... | collective-permute-start | bytes 86024 | tf_op jit(solution)/shard_map/ppermute | solution.py:295
  15.4 0.8 copy.21.depth_one_ref
  16.2 0.8 copy.22.depth_two_ref
  17.0 0.7 copy-done.3
  17.7 0.7 copy-done.4
  18.4 0.7 copy-done.5
  19.1 0.7 copy-done.6
  19.7 7.1 %shard_map.136 = (bf16[1,16,32,128]{3,2,1,0:T(8,128)(2,1)}, bf16[16,48,128]{2,1,0:T(8,128)(2,1)S(1)}, f32[18,160,128]{2,1,0:T(8,128)S(1)}, bf16[16,128,128]{2,1,...) custom-call(f32[16,128,128]{2,1,0:T(8,128)S(1)} %get-tuple-element.2, ...), custom_call_target="tpu_custom_call" | custom-call | flops 268435456 | bytes 4194304 | tf_op jit(solution)/shard_map/pallas_call | solution.py:296
  26.8 18.0 %all_to_all.25.x_ref = bf16[16,48,128]{2,1,0:T(8,128)(2,1)S(1)} all-to-all(bf16[16,48,128]{2,1,0:T(8,128)(2,1)S(1)} %get-tuple-element.24), channel_id=1, replica_groups=mesh['member'=16,'tile'=32] {'member'}, dimensions={0} | all-to-all | bytes 393216 | tf_op jit(solution)/shard_map/all_to_all | solution.py:320
  44.8 0.9 shard_map.137
  45.7 13.2 %all_to_all.26.cot_ref = bf16[16,48,128]{2,1,0:T(8,128)(2,1)S(1)} all-to-all(bf16[16,48,128]{2,1,0:T(8,128)(2,1)S(1)} %shard_map.137), channel_id=1, replica_groups=mesh['member'=16,'tile'=32] {'member'}, dimensions={0} | all-to-all | bytes 393216 | tf_op jit(solution)/shard_map/all_to_all | solution.py:327
  58.9 8.0 %shard_map.138 = f32[16,4,128]{2,1,0:T(4,128)S(1)} custom-call(bf16[16,48,128]{2,1,0:T(8,128)(2,1)S(1)} %all_to_all.26.cot_ref, f32[18,160,128]{2,1,0:T(8,128)S(1)} %get-tuple-element.25.xs_ref, bf16[16,128,128]{2,1,0:T(8,128)(2,1)S(1)} %get-tuple-element.26.first_ref, f32[16,128,128]{2,1,0:T(8,128)S(1)} %get-tuple-element.27.gate_ref, ...), custom_call_target="tpu_custom_call" | custom-call | flops 268435456 | bytes 4194304 | tf_op jit(solution)/shard_map/pallas_call | solution.py:328
  66.8 11.7 %all_to_all.27 = f32[16,4,128]{2,1,0:T(4,128)S(1)} all-to-all(f32[16,4,128]{2,1,0:T(4,128)S(1)} %shard_map.138), channel_id=1, replica_groups=mesh['member'=16,'tile'=32] {'member'}, dimensions={0} | all-to-all | bytes 65536 | tf_op jit(solution)/shard_map/all_to_all | solution.py:342
  78.6 23.6 %all_to_all.28 = f32[32,4,128]{2,1,0:T(4,128)S(1)} all-to-all(f32[32,4,128]{2,1,0:T(4,128)S(1)} %broadcast_in_dim.20), channel_id=1, replica_groups=mesh['member'=16,'tile'=32] {'tile'}, dimensions={0} | all-to-all | bytes 131072 | tf_op jit(solution)/shard_map/all_to_all | solution.py:344
  102.2 11.7 %all_to_all.29 = f32[16,4,128]{2,1,0:T(4,128)S(1)} all-to-all(f32[16,4,128]{2,1,0:T(4,128)S(1)} %broadcast_in_dim.21), channel_id=1, replica_groups=mesh['member'=16,'tile'=32] {'member'}, dimensions={0} | all-to-all | bytes 65536 | tf_op jit(solution)/shard_map/all_to_all | solution.py:346
  113.9 0.6 slice_bitcast_fusion.2
  114.5 0.7 slice_reduce_fusion
  115.2 0.7 slice.34
  115.9 0.7 slice_bitcast_fusion
  116.5 0.6 copy.26
  (14 shorter events, 0.1 us)
Async XLA Ops:
  0.6 1.0 copy-start
  1.6 1.0 copy-start.2
  2.6 42.2 %copy-start.1 = (f32[16,32,128]{2,1,0:T(8,128)S(1)}, f32[16,32,128]{2,1,0:T(8,128)}, u32[]{:S(2)}) copy-start(f32[16,32,128]{2,1,0:T(8,128)} %target_ref.3) | copy-start | bytes 786436
  4.7 12.3 %collective-permute-start = (f32[56,128]{1,0:T(8,128)S(1)}, f32[56,128]{1,0:T(8,128)S(1)}, u32[]{:S(2)}, u32[]{:S(2)}) collective-permute-start(f32[56,128]{1,0:T(8,128)S(1)} %get-tuple-element.21), channel_id=1, source_target_pairs={{0,1},{1,2},{2,3},{3,4},{4,5},{5,6},{6,7},{7,8},{8,9},{9,10},{10,1... | collective-permute-start | bytes 86024 | tf_op jit(solution)/shard_map/ppermute | solution.py:294
  10.1 6.9 %collective-permute-start.1 = (f32[56,128]{1,0:T(8,128)S(1)}, f32[56,128]{1,0:T(8,128)S(1)}, u32[]{:S(2)}, u32[]{:S(2)}) collective-permute-start(f32[56,128]{1,0:T(8,128)S(1)} %get-tuple-element.22), channel_id=1, source_target_pairs={{1,0},{2,1},{3,2},{4,3},{5,4},{6,5},{7,6},{8,7},{9,8},{10,9},{11,1... | collective-permute-start | bytes 86024 | tf_op jit(solution)/shard_map/ppermute | solution.py:295
  17.0 0.7 copy-start.3
  17.7 0.7 copy-start.4
  18.4 0.7 copy-start.5
  19.1 0.7 copy-start.6

commit v2 on v1

--- a/solution.py
+++ b/solution.py
@@ -46,10 +46,30 @@
     return jnp.concatenate([row, row], axis=1)
 
 
-def edge_kernel(x_ref, target_ref, xt_ref, first_ref, last_ref, rows_scr):
+def each_slab(body):
+    def step(p, carry):
+        body(p)
+        return carry
+
+    lax.fori_loop(0, slabs, step, 0, unroll=True)
+
+
+def fetch(sources, places, sems):
+    copies = [
+        pltpu.make_async_copy(source, place, sems.at[k])
+        for k, (source, place) in enumerate(zip(sources, places))
+    ]
+    for copy in copies:
+        copy.start()
+    return copies
+
+
+def edge_kernel(x_hbm, target_hbm, xt_ref, first_ref, last_ref, x_ref, target_ref, rows_scr, sems):
+    x_copy, target_copy = fetch((x_hbm.at[0], target_hbm), (x_ref, target_ref), sems)
+    x_copy.wait()
     rows_scr[...] = x_ref[...].reshape(64 * 32, 128).astype(f32)
 
-    def body(p, _):
+    def body(p):
         here = jnp.concatenate(
             [rows_scr[pl.ds(p, 64, stride=32), :], rows_scr[pl.ds(p + 16, 64, stride=32), :]],
             axis=0,
@@ -59,9 +79,9 @@
         for j in range(3):
             first_ref[pl.ds(16 * j + p, 1), :] = turned[j : j + 1]
             last_ref[pl.ds(16 * j + p, 1), :] = turned[125 + j : 126 + j]
-        return 0
-
-    lax.fori_loop(0, slabs, body, 0)
+
+    each_slab(body)
+    target_copy.wait()
     for k in range(4):
         turned = target_ref[4 * k : 4 * k + 4].reshape(128, 128).T
         first_ref[48 + k : 49 + k, :] = turned[0:1]
@@ -70,38 +90,49 @@
     last_ref[52:56, :] = jnp.zeros((4, 128), f32)
 
 
-def forward_kernel(
-    xt_ref, left_ref, right_ref, depth_one_ref, point_one_ref, bias_one_ref,
-    depth_two_ref, point_two_ref, bias_two_ref,
-    out_ref, send_ref, xs_ref, first_ref, gate_ref, hidden_ref, second_ref,
-    one_ref, two_ref, taps_two_ref,
-    hs_ref, y_ref, edge_ref, taps_one_ref, turn_ref, bias_ref,
+def weight_kernel(
+    depth_one_hbm, point_one_hbm, bias_one_hbm, depth_two_hbm, point_two_hbm, bias_two_hbm,
+    taps_one_ref, one_ref, one_turned_ref, bias_one_ref, taps_two_ref, two_ref, bias_two_ref,
+    d1_ref, p1_ref, b1_ref, d2_ref, p2_ref, b2_ref, turn_ref, sems,
 ):
+    places = (d1_ref, p1_ref, b1_ref, d2_ref, p2_ref, b2_ref)
+    sources = (
+        depth_one_hbm, point_one_hbm, bias_one_hbm, depth_two_hbm, point_two_hbm, bias_two_hbm
+    )
+    copies = fetch(sources, places, sems)
     turn_ref[...] = jnp.zeros((128, 128), f32)
-    turn_ref[0:64, 0:9] = depth_one_ref[...]
-    taps = turn_ref[...].T[0:16]
-    taps_one_ref[...] = taps + pltpu.roll(taps, 64, 1)
-    turn_ref[0:64, 0:9] = depth_two_ref[...]
-    taps = turn_ref[...].T[0:16]
-    taps_two_ref[...] = taps + pltpu.roll(taps, 64, 1)
-    turn_ref[...] = jnp.zeros((128, 128), f32)
-    turn_ref[0:1, 0:16] = bias_two_ref[...]
+    for copy in copies:
+        copy.wait()
+    zero = jnp.zeros((7, 128), f32)
+    taps_one_ref[...] = jnp.concatenate([both_halves(d1_ref[...]), zero], axis=0)
+    taps_two_ref[...] = jnp.concatenate([both_halves(d2_ref[...]), zero], axis=0)
+    bias_one_ref[...] = jnp.broadcast_to(both_halves(b1_ref[...]), (8, 128))
+    turn_ref[0:1, 0:16] = b2_ref[...]
     column = jnp.broadcast_to(turn_ref[...].T[0:16, 0:1], (16, 128))
-    bias_ref[0:16] = column
-    bias_ref[16:32] = column
-    turn_ref[...] = jnp.zeros((128, 128), f32)
-    weight = point_one_ref[...].astype(f32)
+    bias_two_ref[0:16] = column
+    bias_two_ref[16:32] = column
+    turn_ref[0:1, :] = jnp.zeros((1, 128), f32)
+    weight = p1_ref[...].astype(f32)
     turn_ref[0:64, 0:64] = weight
     turn_ref[64:128, 64:128] = weight
     one_ref[...] = turn_ref[...].astype(bf16)
-    one_turned = turn_ref[...].T.astype(bf16)
-    weight = point_two_ref[...].astype(f32)
+    one_turned_ref[...] = turn_ref[...].T.astype(bf16)
+    weight = p2_ref[...].astype(f32)
     zero = jnp.zeros((16, 64), f32)
-    two = jnp.concatenate(
+    two_ref[...] = jnp.concatenate(
         [jnp.concatenate([weight, zero], axis=1), jnp.concatenate([zero, weight], axis=1)], axis=0
     ).astype(bf16)
-    two_ref[...] = two
-    bias_one = both_halves(bias_one_ref[...])
+
+
+def forward_kernel(
+    xt_ref, left_ref, right_ref,
+    taps_one_ref, one_turned_ref, bias_one_ref, taps_two_ref, two_ref, bias_ref,
+    out_ref, send_ref, xs_ref, first_ref, gate_ref, hidden_ref, second_ref,
+    hs_ref, y_ref, edge_ref,
+):
+    one_turned = one_turned_ref[...]
+    two = two_ref[...]
+    bias_one = bias_one_ref[0:1]
 
     for k in range(slabs + 2):
         xs_ref[k, 0:16, :] = jnp.zeros((16, 128), f32)
@@ -113,7 +144,7 @@
             xs_ref[p + 1, 144 + j : 145 + j, :] = right_ref[16 * j + p : 16 * j + p + 1, :]
     wrap_slabs(xs_ref)
 
-    def first_body(p, _):
+    def first_body(p):
         total = jnp.zeros((wide, 128), f32)
         for a in range(3):
             for b in range(3):
@@ -126,17 +157,16 @@
         hs_ref[p + 1, 8 : 8 + wide, :] = hidden
         hidden_ref[p] = hidden[8:136].astype(bf16)
         gate_ref[p] = (gate * (1.0 + pre * (1.0 - gate)))[8:136]
-        return 0
 
     for k in range(slabs + 2):
         hs_ref[k, 0:8, :] = jnp.zeros((8, 128), f32)
         hs_ref[k, 152:160, :] = jnp.zeros((8, 128), f32)
-    lax.fori_loop(0, slabs, first_body, 0)
+    each_slab(first_body)
     wrap_slabs(hs_ref)
     y_ref[...] = jnp.zeros(y_ref.shape, f32)
     edge_ref[...] = jnp.zeros(edge_ref.shape, f32)
 
-    def second_body(p, _):
+    def second_body(p):
         total = jnp.zeros((wide, 128), f32)
         for a in range(3):
             for b in range(3):
@@ -149,9 +179,8 @@
         y = dot(two, second, 1, 1) + bias_ref[...]
         y_ref[pl.ds(p, 16, stride=chunk), :] = y[0:16]
         y_ref[pl.ds(16 + p, 16, stride=chunk), :] = y[16:32]
-        return 0
-
-    lax.fori_loop(0, slabs, second_body, 0)
+
+    each_slab(second_body)
     y = dot(two, edge_ref[...].astype(bf16), 1, 1) + bias_ref[...]
     lane = lanes_of((16, 128))
     y = jnp.where(lane < 32, y[0:16], jnp.where(lane < 64, pltpu.roll(y[16:32], 32, 1), 0.0))
@@ -216,17 +245,16 @@
     point_one_ref[...] = jnp.zeros(point_one_ref.shape, f32)
     other_ref[...] = jnp.zeros(other_ref.shape, f32)
 
-    def cot_body(p, _):
+    def cot_body(p):
         cot = jnp.concatenate(
             [cf_ref[pl.ds(p, 16, stride=chunk), :], cf_ref[pl.ds(16 + p, 16, stride=chunk), :]], axis=0
         )
-        cot_sum_ref[...] += cot
+        cot_sum_ref[0:32] += cot
         cot = cot.astype(bf16)
         bs_ref[p + 1, own : own + 128, :] = rounded(dot(cot, two, 0, 0))
         point_two_ref[...] += dot(cot, second_ref[p], 1, 0)
-        return 0
-
-    lax.fori_loop(0, slabs, cot_body, 0)
+
+    each_slab(cot_body)
     halo = cf_ref[pl.ds(32, 16, stride=chunk), :]
     halo = jnp.concatenate([halo, pltpu.roll(halo, 96, 1)], axis=0).astype(bf16)
     halo = rounded(dot(halo, two, 0, 0))
@@ -235,7 +263,7 @@
         bs_ref[p + 1, 144:145, :] = halo[16 + p : 17 + p]
     wrap_slabs(bs_ref)
 
-    def body(p, _):
+    def body(p):
         total = jnp.zeros((128, 128), f32)
         hidden = hidden_ref[p].astype(f32)
         for a in range(3):
@@ -251,28 +279,45 @@
         for a in range(3):
             for b in range(3):
                 sums_ref[3 * a + b] += tap_sum(back_first * xs_ref[p + a, 15 + b : 143 + b, :])
-        return 0
-
-    lax.fori_loop(0, slabs, body, 0)
+
+    each_slab(body)
     for t in range(19):
         total = jnp.sum(sums_ref[t], axis=0, keepdims=True)
         other_ref[t : t + 1, :] = total + pltpu.roll(total, 64, 1)
     other_ref[24:40, :] = pltpu.roll(point_two_ref[0:16], 64, 1) + point_two_ref[16:32]
-    bias_two = jnp.sum(cot_sum_ref[0:16] + cot_sum_ref[16:32], axis=1, keepdims=True)
-    other_ref[40:56, :] = jnp.broadcast_to(bias_two, (16, 128))
+    bias_two = jnp.sum(cot_sum_ref[...].T, axis=0, keepdims=True)
+    bias_two = bias_two + pltpu.roll(bias_two, 112, 1)
+    other_ref[19:20, :] = pltpu.roll(bias_two, 64, 1)
     point_one = point_one_ref[0:64] + pltpu.roll(point_one_ref[64:128], 64, 1)
     packed = jnp.where(lanes_of((64, 128)) < 64, point_one, other_ref[...])
     out_ref[...] = packed.reshape(out_ref.shape)
 
 
-def call(kernel, out_shape, scratch, flops):
+def output_kernel(total_ref, depth_one_ref, point_one_ref, bias_one_ref, depth_two_ref, point_two_ref, bias_two_ref, rows_ref):
+    rows_ref[...] = total_ref[...].reshape(64, 128)
+    point_one_ref[...] = rows_ref[:, 0:64]
+    depth_one_ref[...] = rows_ref[0:9, 64:128]
+    depth_two_ref[...] = rows_ref[9:18, 64:128]
+    bias_one_ref[...] = rows_ref[18:19, 64:128]
+    bias_two_ref[...] = rows_ref[19:20, 64:80]
+    point_two_ref[...] = rows_ref[24:40, 64:128]
+
+
+def call(kernel, out_shape, scratch, flops, fetched=0, passed=0):
+    hbm = pl.BlockSpec(memory_space=pltpu.HBM)
+    vmem = pl.BlockSpec(memory_space=pltpu.VMEM)
     return pl.pallas_call(
         kernel,
         out_shape=out_shape,
+        in_specs=[hbm] * fetched + [vmem] * passed,
         scratch_shapes=scratch,
         compiler_params=pltpu.CompilerParams(vmem_limit_bytes=24 * 1024 * 1024),
         cost_estimate=pl.CostEstimate(flops=flops, bytes_accessed=4 << 20, transcendentals=0),
     )
+
+
+def in_hbm(*arrays):
+    return [pltpu.with_memory_space_constraint(array, pltpu.HBM) for array in arrays]
 
 
 def shape(dims, dtype):
@@ -287,13 +332,47 @@
     xt, first_cols, last_cols = call(
         edge_kernel,
         (shape(slab, f32), shape((edge_rows, 128), f32), shape((edge_rows, 128), f32)),
-        [pltpu.VMEM((chans * rows, 128), f32)],
+        [
+            pltpu.VMEM((chans, rows, cols), bf16),
+            pltpu.VMEM((16, rows, cols), f32),
+            pltpu.VMEM((chans * rows, 128), f32),
+            pltpu.SemaphoreType.DMA((2,)),
+        ],
         1 << 20,
-    )(predictor_inputs[0], target)
+        fetched=2,
+    )(*in_hbm(predictor_inputs, target))
     up = [(i, (i + 1) % tiles) for i in range(tiles)]
     left = lax.ppermute(last_cols, "tile", up)
     right = lax.ppermute(first_cols, "tile", [(j, i) for i, j in up])
-    out, send, xs, first, gate, hidden, second, one, two, taps_two = call(
+    taps_one, one, one_turned, bias_one, taps_two, two, bias_two = call(
+        weight_kernel,
+        (
+            shape((16, 128), f32),
+            shape((128, 128), bf16),
+            shape((128, 128), bf16),
+            shape((8, 128), f32),
+            shape((16, 128), f32),
+            shape((32, 128), bf16),
+            shape((32, 128), f32),
+        ),
+        [
+            pltpu.VMEM((9, 64), f32),
+            pltpu.VMEM((64, 64), bf16),
+            pltpu.VMEM((1, 64), f32),
+            pltpu.VMEM((9, 64), f32),
+            pltpu.VMEM((16, 64), bf16),
+            pltpu.VMEM((1, 16), f32),
+            pltpu.VMEM((128, 128), f32),
+            pltpu.SemaphoreType.DMA((6,)),
+        ],
+        1 << 20,
+        fetched=6,
+    )(
+        *in_hbm(
+            depth_one.T, point_one, bias_one[None], depth_two.T, point_two, bias_two[None]
+        )
+    )
+    out, send, xs, first, gate, hidden, second = call(
         forward_kernel,
         (
             shape((1, 16, rows, cols), bf16),
@@ -303,56 +382,71 @@
             shape(slab, f32),
             shape(slab, bf16),
             shape(slab, bf16),
-            shape((128, 128), bf16),
-            shape((32, 128), bf16),
-            shape((16, 128), f32),
         ),
         [
             pltpu.VMEM((slabs + 2, pitch, 128), f32),
             pltpu.VMEM((16 * chunk, 128), f32),
             pltpu.VMEM((128, 128), f32),
-            pltpu.VMEM((16, 128), f32),
-            pltpu.VMEM((128, 128), f32),
-            pltpu.VMEM((32, 128), f32),
         ],
         1 << 28,
-    )(xt, left, right, depth_one, point_one, bias_one[None], depth_two, point_two, bias_two[None])
+        passed=9,
+    )(xt, left, right, taps_one, one_turned, bias_one, taps_two, two, bias_two)
     seen = lax.all_to_all(send, "member", 0, 0, tiled=True)
     cot = call(
         functools.partial(crps_kernel, rows * cols * tiles),
         shape((members, chunk, 128), bf16),
         [],
         1 << 24,
+        passed=4,
     )(seen, target, left, right)
     cot = lax.all_to_all(cot, "member", 0, 0, tiled=True)
     packed = call(
         backward_kernel,
-        shape((members, 64 // members, 128), f32),
+        shape((16, 4, 128), f32),
         [
             pltpu.VMEM((16 * chunk, 128), f32),
             pltpu.VMEM((slabs + 2, pitch, 128), f32),
             pltpu.VMEM((19, 8, 128), f32),
-            pltpu.VMEM((32, 128), f32),
+            pltpu.VMEM((128, 128), f32),
             pltpu.VMEM((32, 128), f32),
             pltpu.VMEM((128, 128), f32),
             pltpu.VMEM((64, 128), f32),
         ],
         1 << 28,
+        passed=9,
     )(cot, xs, first, gate, hidden, second, one, two, taps_two)
-    part = jnp.sum(lax.all_to_all(packed, "member", 0, 0, tiled=True), axis=0)
-    part = jnp.broadcast_to(part[None], (tiles,) + part.shape)
-    part = jnp.sum(lax.all_to_all(part, "tile", 0, 0, tiled=True), axis=0)
-    part = jnp.broadcast_to(part[None], (members,) + part.shape)
-    total = lax.all_to_all(part, "member", 0, 0, tiled=True).reshape(64, 128)
-    other = total[:, 64:]
+    axes = ("member", "tile")
+    near = [[16 * g + k for k in range(16)] for g in range(members * tiles // 16)]
+    far = [list(group) for group in zip(*near)]
+    part = lax.all_to_all(packed, axes, 0, 0, tiled=True, axis_index_groups=near)
+    part = jnp.sum(part, axis=0)
+    part = jnp.broadcast_to(part[None], (len(near),) + part.shape)
+    part = lax.all_to_all(part, axes, 0, 0, tiled=True, axis_index_groups=far)
+    part = jnp.sum(part, axis=0)
+    part = jnp.broadcast_to(part[None], (len(far),) + part.shape)
+    total = lax.all_to_all(part, axes, 0, 0, tiled=True, axis_index_groups=near)
+    g_depth_one, g_point_one, g_bias_one, g_depth_two, g_point_two, g_bias_two = call(
+        output_kernel,
+        (
+            shape((9, 64), f32),
+            shape((64, 64), f32),
+            shape((1, 64), f32),
+            shape((9, 64), f32),
+            shape((16, 64), f32),
+            shape((1, 16), f32),
+        ),
+        [pltpu.VMEM((64, 128), f32)],
+        1 << 20,
+        passed=1,
+    )(total)
     return (
         out,
-        other[0:9].T,
-        total[:, :64],
-        other[18],
-        other[9:18].T,
-        other[24:40],
-        other[40:56, 0],
+        g_depth_one.T,
+        g_point_one,
+        g_bias_one[0],
+        g_depth_two.T,
+        g_point_two,
+        g_bias_two[0],
     )
 
 

time: 118 us -> 98.8 us (0.84)
  local copies, waits for them, and re-layouts: 9.52 us -> 0.03 us
  Pallas kernels: 18 us -> 10.5 us
  blocking collectives: 78.1 us -> 76.5 us
    unnamed x17 -> x2, local copies, waits for them, and re-layouts: 6.88 us -> 0.01 us
    pallas_call x1, Pallas kernels: 7.09 us -> 3.12 us  [local(): call(forward_kernel, (shape((1, 16, rows, cols), bf16), shape((16, chunk,...]
    pallas_call x1 -> x3, Pallas kernels: 7.96 us -> 4.51 us  [the longest x1 2.79 us: local(): call(backward_kernel, shape((16, 4, 128), f32), [pltpu.VMEM((16 * chunk,...]
    all_to_all x3, blocking collectives: 47 us -> 44.8 us  [the longest x1 21.5 us: local(): lax.all_to_all(packed, axes, 0, 0, tiled=True, axis_index_groups=near)]
    slice x2 -> x0, local copies, waits for them, and re-layouts: 1.36 us -> none  [the longest x1 0.69 us: local(): other[40:56, 0]]
  transfers between devices with their start and end apart: 2 -> 2, of which waited for: 0 -> 0; matrix products, arithmetic and copies ran while one was open for 1% -> 0% of each run, Pallas kernels for 0% -> 1%
where the time goes in v2:
time: 98.8 us; the launch traced here: 98.4 us
  blocking collectives  76.5 us (77%)
  starting transfers between devices  10.7 us (11%)
  Pallas kernels  10.5 us (11%)
    all_to_all x1, blocking collectives, local(): lax.all_to_all(packed, axes, 0, 0, tiled=True, axis_index_groups=near)  21.5 us
    all_to_all x1, blocking collectives, local(): seen = lax.all_to_all(send, 'member', 0, 0, tiled=True)  18.5 us
    all_to_all x1, blocking collectives, local(): cot = lax.all_to_all(cot, 'member', 0, 0, tiled=True)  13.2 us
    all_to_all x1, blocking collectives, local(): part = lax.all_to_all(part, axes, 0, 0, tiled=True, axis_index_groups=far)  11.8 us
    all_to_all x1, blocking collectives, local(): total = lax.all_to_all(part, axes, 0, 0, tiled=True, axis_index_groups=near)  11.4 us
    ppermute x1, starting transfers between devices, local(): left = lax.ppermute(last_cols, 'tile', up)  5.39 us
    ppermute x1, starting transfers between devices, local(): right = lax.ppermute(first_cols, 'tile', [(j, i) for i, j in up])  5.32 us
    pallas_call x1, Pallas kernels, local(): call(forward_kernel, (shape((1, 16, rows, cols), bf16), shape((16, chunk,...  3.12 us
  transfers between devices with their start and end apart: 2, of which 0 were waited for; matrix products, arithmetic and copies ran while one was open for 0% of the time, Pallas kernels for 1%

profile of v2, /device:TPU:1, one launch (start us, length us, event | category | flops | bytes accessed | tf_op | source)
XLA Modules:
  0.0 98.4 jit_solution(9563976814823542531)
XLA Ops:
  0.6 0.0 copy-start
  0.6 2.0 %shard_map.135 = (f32[16,128,128]{2,1,0:T(8,128)S(1)}, f32[56,128]{1,0:T(8,128)S(1)}, f32[56,128]{1,0:T(8,128)S(1)}) custom-call(bf16[1,64,32,128]{3,2,1,0:T(8,128)(2,1)} %x_hbm.1, f32[16,32,128]{2,1,0:T(8,128)} %target_ref.1), custom_call_target="tpu_custom_call" | custom-call | flops 1048576 | bytes 4194304 | tf_op jit(solution)/shard_map/pallas_call | solution.py:332
  2.6 5.4 %collective-permute-start = (f32[56,128]{1,0:T(8,128)S(1)}, f32[56,128]{1,0:T(8,128)S(1)}, u32[]{:S(2)}, u32[]{:S(2)}) collective-permute-start(f32[56,128]{1,0:T(8,128)S(1)} %get-tuple-element.31), channel_id=1, source_target_pairs={{0,1},{1,2},{2,3},{3,4},{4,5},{5,6},{6,7},{7,8},{8,9},{9,10},{10,1... | collective-permute-start | bytes 86024 | tf_op jit(solution)/shard_map/ppermute | solution.py:345
  8.0 5.3 %collective-permute-start.1 = (f32[56,128]{1,0:T(8,128)S(1)}, f32[56,128]{1,0:T(8,128)S(1)}, u32[]{:S(2)}, u32[]{:S(2)}) collective-permute-start(f32[56,128]{1,0:T(8,128)S(1)} %get-tuple-element.32), channel_id=1, source_target_pairs={{1,0},{2,1},{3,2},{4,3},{5,4},{6,5},{7,6},{8,7},{9,8},{10,9},{11,1... | collective-permute-start | bytes 86024 | tf_op jit(solution)/shard_map/ppermute | solution.py:346
  13.3 1.0 %shard_map.136 = (f32[16,128]{1,0:T(8,128)S(1)}, bf16[128,128]{1,0:T(8,128)(2,1)S(1)}, bf16[128,128]{1,0:T(8,128)(2,1)S(1)}, f32[8,128]{1,0:T(8,128)S(1)}, f32[1...) custom-call(f32[9,64]{1,0:T(8,128)} %bitcast.8, bf16[64,64]{1,0:T(8,128)(2,1)} %point_one_hbm.1, ...), custom_call_target="tpu_custom_call" | custom-call | flops 1048576 | bytes 4194304 | tf_op jit(solution)/shard_map/pallas_call | solution.py:347
  14.4 0.0 collective-permute-done.left_ref
  14.4 0.0 collective-permute-done.1.right_ref
  14.4 3.1 %shard_map.137 = (bf16[1,16,32,128]{3,2,1,0:T(8,128)(2,1)}, bf16[16,48,128]{2,1,0:T(8,128)(2,1)S(1)}, f32[18,160,128]{2,1,0:T(8,128)S(1)}, bf16[16,128,128]{2,1,...) custom-call(f32[16,128,128]{2,1,0:T(8,128)S(1)} %get-tuple-element.3, ...), custom_call_target="tpu_custom_call" | custom-call | flops 268435456 | bytes 4194304 | tf_op jit(solution)/shard_map/pallas_call | solution.py:375
  17.5 18.5 %all_to_all.25.x_ref = bf16[16,48,128]{2,1,0:T(8,128)(2,1)S(1)} all-to-all(bf16[16,48,128]{2,1,0:T(8,128)(2,1)S(1)} %get-tuple-element.40), channel_id=1, replica_groups=mesh['member'=16,'tile'=32] {'member'}, dimensions={0} | all-to-all | bytes 393216 | tf_op jit(solution)/shard_map/all_to_all | solution.py:394
  36.0 0.0 copy-done
  36.0 0.9 shard_map.138
  36.9 13.2 %all_to_all.26.cot_ref = bf16[16,48,128]{2,1,0:T(8,128)(2,1)S(1)} all-to-all(bf16[16,48,128]{2,1,0:T(8,128)(2,1)S(1)} %shard_map.138), channel_id=1, replica_groups=mesh['member'=16,'tile'=32] {'member'}, dimensions={0} | all-to-all | bytes 393216 | tf_op jit(solution)/shard_map/all_to_all | solution.py:402
  50.1 2.8 %shard_map.139 = f32[16,4,128]{2,1,0:T(4,128)S(1)} custom-call(bf16[16,48,128]{2,1,0:T(8,128)(2,1)S(1)} %all_to_all.26.cot_ref, f32[18,160,128]{2,1,0:T(8,128)S(1)} %get-tuple-element.41.xs_ref, bf16[16,128,128]{2,1,0:T(8,128)(2,1)S(1)} %get-tuple-element.42.first_ref, f32[16,128,128]{2,1,0:T(8,128)S(1)} %get-tuple-element.43.gate_ref, ...), custom_call_target="tpu_custom_call" | custom-call | flops 268435456 | bytes 4194304 | tf_op jit(solution)/shard_map/pallas_call | solution.py:403
  52.9 21.5 %all_to_all.27 = f32[16,4,128]{2,1,0:T(4,128)S(1)} all-to-all(f32[16,4,128]{2,1,0:T(4,128)S(1)} %shard_map.139), channel_id=1, replica_groups={{0,1,2,3,4,5,6,7,8,9,10,11,12,13,14,15},{16,17,18,19,20,21,22,23,24,25,..., dimensions={0} | all-to-all | bytes 65536 | tf_op jit(solution)/shard_map/all_to_all | solution.py:421
  74.4 11.8 %all_to_all.28 = f32[32,4,128]{2,1,0:T(4,128)S(1)} all-to-all(f32[32,4,128]{2,1,0:T(4,128)S(1)} %broadcast_in_dim.20), channel_id=1, replica_groups={{0,16,32,48,64,80,96,112,128,144,160,176,192,208,224,240,256,272,288,30..., dimensions={0} | all-to-all | bytes 131072 | tf_op jit(solution)/shard_map/all_to_all | solution.py:424
  86.3 11.4 %all_to_all.29.total_ref = f32[16,4,128]{2,1,0:T(4,128)S(1)} all-to-all(f32[16,4,128]{2,1,0:T(4,128)S(1)} %broadcast_in_dim.21), channel_id=1, replica_groups={{0,1,2,3,4,5,6,7,8,9,10,11,12,13,14,15},{16,17,18,19,20,21,22,23,24,25,..., dimensions={0} | all-to-all | bytes 65536 | tf_op jit(solution)/shard_map/all_to_all | solution.py:427
  97.7 0.7 shard_map.140
  (4 shorter events, 0.1 us)
Async XLA Ops:
  0.6 35.4 %copy-start = (f32[16,32,128]{2,1,0:T(8,128)S(1)}, f32[16,32,128]{2,1,0:T(8,128)}, u32[]{:S(2)}) copy-start(f32[16,32,128]{2,1,0:T(8,128)} %target_ref.1) | copy-start | bytes 786436
  2.6 11.8 %collective-permute-start = (f32[56,128]{1,0:T(8,128)S(1)}, f32[56,128]{1,0:T(8,128)S(1)}, u32[]{:S(2)}, u32[]{:S(2)}) collective-permute-start(f32[56,128]{1,0:T(8,128)S(1)} %get-tuple-element.31), channel_id=1, source_target_pairs={{0,1},{1,2},{2,3},{3,4},{4,5},{5,6},{6,7},{7,8},{8,9},{9,10},{10,1... | collective-permute-start | bytes 86024 | tf_op jit(solution)/shard_map/ppermute | solution.py:345
  8.0 6.4 %collective-permute-start.1 = (f32[56,128]{1,0:T(8,128)S(1)}, f32[56,128]{1,0:T(8,128)S(1)}, u32[]{:S(2)}, u32[]{:S(2)}) collective-permute-start(f32[56,128]{1,0:T(8,128)S(1)} %get-tuple-element.32), channel_id=1, source_target_pairs={{1,0},{2,1},{3,2},{4,3},{5,4},{6,5},{7,6},{8,7},{9,8},{10,9},{11,1... | collective-permute-start | bytes 86024 | tf_op jit(solution)/shard_map/ppermute | solution.py:346

commit v3 on v2

--- a/solution.py
+++ b/solution.py
@@ -90,10 +90,11 @@
     last_ref[52:56, :] = jnp.zeros((4, 128), f32)
 
 
-def weight_kernel(
-    depth_one_hbm, point_one_hbm, bias_one_hbm, depth_two_hbm, point_two_hbm, bias_two_hbm,
+def main_kernel(
+    depth_one_hbm, point_one_hbm, bias_one_hbm, depth_two_hbm, point_two_hbm, bias_two_hbm, xt_ref,
     taps_one_ref, one_ref, one_turned_ref, bias_one_ref, taps_two_ref, two_ref, bias_two_ref,
-    d1_ref, p1_ref, b1_ref, d2_ref, p2_ref, b2_ref, turn_ref, sems,
+    first_ref, gate_ref, hidden_ref, second_ref,
+    d1_ref, p1_ref, b1_ref, d2_ref, p2_ref, b2_ref, turn_ref, xs_ref, hs_ref, sems,
 ):
     places = (d1_ref, p1_ref, b1_ref, d2_ref, p2_ref, b2_ref)
     sources = (
@@ -101,6 +102,13 @@
     )
     copies = fetch(sources, places, sems)
     turn_ref[...] = jnp.zeros((128, 128), f32)
+    for ref in (xs_ref, hs_ref):
+        for k in range(slabs + 2):
+            ref[k, 0:8, :] = jnp.zeros((8, 128), f32)
+            ref[k, 136:144, :] = jnp.zeros((8, 128), f32)
+    for p in range(slabs):
+        xs_ref[p + 1, 8:136, :] = xt_ref[p]
+    wrap_slabs(xs_ref)
     for copy in copies:
         copy.wait()
     zero = jnp.zeros((7, 128), f32)
@@ -116,23 +124,56 @@
     turn_ref[0:64, 0:64] = weight
     turn_ref[64:128, 64:128] = weight
     one_ref[...] = turn_ref[...].astype(bf16)
-    one_turned_ref[...] = turn_ref[...].T.astype(bf16)
+    one_turned = turn_ref[...].T.astype(bf16)
+    one_turned_ref[...] = one_turned
     weight = p2_ref[...].astype(f32)
     zero = jnp.zeros((16, 64), f32)
     two_ref[...] = jnp.concatenate(
         [jnp.concatenate([weight, zero], axis=1), jnp.concatenate([zero, weight], axis=1)], axis=0
     ).astype(bf16)
 
-
-def forward_kernel(
-    xt_ref, left_ref, right_ref,
+    def first_body(p):
+        first = rounded(depthwise(taps_one_ref, xs_ref, p, 7, 128))
+        first_ref[p] = first
+        hidden, gate = activation(first, one_turned, bias_one_ref)
+        hidden_ref[p] = hidden
+        hs_ref[p + 1, 8:136, :] = hidden
+        gate_ref[p] = gate
+
+    def second_body(p):
+        second_ref[p] = depthwise(taps_two_ref, hs_ref, p, 7, 128)
+
+    each_slab(first_body)
+    wrap_slabs(hs_ref)
+    each_slab(second_body)
+
+
+def depthwise(taps_ref, ref, p, row, count):
+    total = jnp.zeros((count, 128), f32)
+    for a in range(3):
+        for b in range(3):
+            tap = taps_ref[3 * a + b : 3 * a + b + 1, :]
+            total = total + tap * ref[p + a, row + b : row + b + count, :]
+    return total
+
+
+def activation(first, one_turned, bias_ref):
+    pre = dot(first.astype(bf16), one_turned, 1, 0) + bias_ref[0:1]
+    gate = 1.0 / (1.0 + jnp.exp(-pre))
+    return rounded(pre * gate), gate * (1.0 + pre * (1.0 - gate))
+
+
+def with_edges(main, edge):
+    return jnp.concatenate([edge[0:8], main[8:120], edge[8:16]], axis=0)
+
+
+def halo_kernel(
+    xt_ref, left_ref, right_ref, hidden_ref, main_second_ref,
     taps_one_ref, one_turned_ref, bias_one_ref, taps_two_ref, two_ref, bias_ref,
-    out_ref, send_ref, xs_ref, first_ref, gate_ref, hidden_ref, second_ref,
-    hs_ref, y_ref, edge_ref,
+    out_ref, send_ref, xs_ref, first_ref, gate_ref, edge_hidden_ref, second_ref,
+    hs_ref, first_scr, y_ref, edge_ref,
 ):
-    one_turned = one_turned_ref[...]
     two = two_ref[...]
-    bias_one = bias_one_ref[0:1]
 
     for k in range(slabs + 2):
         xs_ref[k, 0:16, :] = jnp.zeros((16, 128), f32)
@@ -145,37 +186,38 @@
     wrap_slabs(xs_ref)
 
     def first_body(p):
-        total = jnp.zeros((wide, 128), f32)
-        for a in range(3):
-            for b in range(3):
-                tap = taps_one_ref[3 * a + b : 3 * a + b + 1, :]
-                total = total + tap * xs_ref[p + a, 7 + b : 7 + b + wide, :]
-        first_ref[p] = total[8:136].astype(bf16)
-        pre = dot(total.astype(bf16), one_turned, 1, 0) + bias_one
-        gate = 1.0 / (1.0 + jnp.exp(-pre))
-        hidden = rounded(pre * gate)
-        hs_ref[p + 1, 8 : 8 + wide, :] = hidden
-        hidden_ref[p] = hidden[8:136].astype(bf16)
-        gate_ref[p] = (gate * (1.0 + pre * (1.0 - gate)))[8:136]
-
-    for k in range(slabs + 2):
-        hs_ref[k, 0:8, :] = jnp.zeros((8, 128), f32)
-        hs_ref[k, 152:160, :] = jnp.zeros((8, 128), f32)
+        first = jnp.concatenate(
+            [depthwise(taps_one_ref, xs_ref, p, 7, 16), depthwise(taps_one_ref, xs_ref, p, 135, 16)],
+            axis=0,
+        )
+        first_scr[pl.ds(32 * p, 32), :] = rounded(first)
+
     each_slab(first_body)
+    first = first_scr[...]
+    hidden, gate = activation(first, one_turned_ref[...], bias_one_ref)
+    for p in range(slabs):
+        rows = slice(32 * p + 8, 32 * p + 24)
+        first_ref[p] = first[rows]
+        gate_ref[p] = gate[rows]
+        edge_hidden_ref[p] = hidden[rows]
+        hs_ref[p + 1, 0:8, :] = jnp.zeros((8, 128), f32)
+        hs_ref[p + 1, 8:24, :] = hidden[32 * p : 32 * p + 16]
+        hs_ref[p + 1, 24:32, :] = hidden_ref[p, 8:16, :]
+        hs_ref[p + 1, 32:40, :] = hidden_ref[p, 112:120, :]
+        hs_ref[p + 1, 40:56, :] = hidden[32 * p + 16 : 32 * p + 32]
+        hs_ref[p + 1, 56:64, :] = jnp.zeros((8, 128), f32)
     wrap_slabs(hs_ref)
     y_ref[...] = jnp.zeros(y_ref.shape, f32)
     edge_ref[...] = jnp.zeros(edge_ref.shape, f32)
 
     def second_body(p):
-        total = jnp.zeros((wide, 128), f32)
-        for a in range(3):
-            for b in range(3):
-                tap = taps_two_ref[3 * a + b : 3 * a + b + 1, :]
-                total = total + tap * hs_ref[p + a, 7 + b : 7 + b + wide, :]
-        second = total[8:136].astype(bf16)
+        before = depthwise(taps_two_ref, hs_ref, p, 7, 16)
+        after = depthwise(taps_two_ref, hs_ref, p, 39, 16)
+        edge_ref[pl.ds(p, 1), :] = before[7:8]
+        edge_ref[pl.ds(16 + p, 1), :] = after[8:9]
+        edge = jnp.concatenate([before[8:16], after[0:8]], axis=0)
+        second = with_edges(main_second_ref[p], edge).astype(bf16)
         second_ref[p] = second
-        edge_ref[pl.ds(p, 1), :] = total[7:8]
-        edge_ref[pl.ds(16 + p, 1), :] = total[136:137]
         y = dot(two, second, 1, 1) + bias_ref[...]
         y_ref[pl.ds(p, 16, stride=chunk), :] = y[0:16]
         y_ref[pl.ds(16 + p, 16, stride=chunk), :] = y[16:32]
@@ -214,16 +256,19 @@
     )
     for part in range(3):
         rows = slice(16 * part, 16 * part + 16)
-        x = [x_ref[i, rows, :].astype(f32) for i in range(members)]
+        used = 8 if part == 2 else 16
+        x = [x_ref[i, rows, :].astype(f32)[0:used] for i in range(members)]
         total = [None] * members
         for i in range(members):
             for j in range(i + 1, members):
                 s = slope(x[i] - x[j])
                 total[i] = s if total[i] is None else total[i] + s
                 total[j] = -s if total[j] is None else total[j] - s
-        aim = halo if part == 2 else target_ref[me, rows, :]
+        aim = halo[0:8] if part == 2 else target_ref[me, rows, :]
         for i in range(members):
             value = slope(x[i] - aim) - pair_weight / (members - 1) * total[i]
+            if part == 2:
+                value = jnp.concatenate([value, jnp.zeros((8, 128), f32)], axis=0)
             out_ref[i, rows, :] = (value / cells_all).astype(bf16)
 
 
@@ -232,7 +277,8 @@
 
 
 def backward_kernel(
-    cot_ref, xs_ref, first_ref, gate_ref, hidden_ref, second_ref, one_ref, two_ref, taps_two_ref,
+    cot_ref, xs_ref, first_ref, gate_ref, hidden_ref, edge_first_ref, edge_gate_ref, edge_hidden_ref,
+    second_ref, one_ref, two_ref, taps_two_ref,
     out_ref,
     cf_ref, bs_ref, sums_ref, cot_sum_ref, point_two_ref, point_one_ref, other_ref,
 ):
@@ -265,16 +311,17 @@
 
     def body(p):
         total = jnp.zeros((128, 128), f32)
-        hidden = hidden_ref[p].astype(f32)
+        hidden = with_edges(hidden_ref[p], edge_hidden_ref[p])
         for a in range(3):
             for b in range(3):
                 t = 3 * a + b
                 back = bs_ref[p + 2 - a, 17 - b : 145 - b, :]
                 total = total + taps_two_ref[t : t + 1, :] * back
                 sums_ref[9 + t] += tap_sum(back * hidden)
-        back_pre = (total * gate_ref[p]).astype(bf16)
+        back_pre = (total * with_edges(gate_ref[p], edge_gate_ref[p])).astype(bf16)
         sums_ref[18] += tap_sum(back_pre.astype(f32))
-        point_one_ref[...] += dot(back_pre, first_ref[p], 0, 0)
+        first = with_edges(first_ref[p], edge_first_ref[p]).astype(bf16)
+        point_one_ref[...] += dot(back_pre, first, 0, 0)
         back_first = dot(back_pre, one, 1, 0)
         for a in range(3):
             for b in range(3):
@@ -344,8 +391,11 @@
     up = [(i, (i + 1) % tiles) for i in range(tiles)]
     left = lax.ppermute(last_cols, "tile", up)
     right = lax.ppermute(first_cols, "tile", [(j, i) for i, j in up])
-    taps_one, one, one_turned, bias_one, taps_two, two, bias_two = call(
-        weight_kernel,
+    (
+        taps_one, one, one_turned, bias_one, taps_two, two, bias_two,
+        first, gate, hidden, main_second,
+    ) = call(
+        main_kernel,
         (
             shape((16, 128), f32),
             shape((128, 128), bf16),
@@ -354,6 +404,10 @@
             shape((16, 128), f32),
             shape((32, 128), bf16),
             shape((32, 128), f32),
+            shape(slab, f32),
+            shape(slab, f32),
+            shape(slab, f32),
+            shape(slab, f32),
         ),
         [
             pltpu.VMEM((9, 64), f32),
@@ -363,34 +417,42 @@
             pltpu.VMEM((16, 64), bf16),
             pltpu.VMEM((1, 16), f32),
             pltpu.VMEM((128, 128), f32),
+            pltpu.VMEM((slabs + 2, wide, 128), f32),
+            pltpu.VMEM((slabs + 2, wide, 128), f32),
             pltpu.SemaphoreType.DMA((6,)),
         ],
-        1 << 20,
+        1 << 28,
         fetched=6,
+        passed=1,
     )(
         *in_hbm(
             depth_one.T, point_one, bias_one[None], depth_two.T, point_two, bias_two[None]
-        )
-    )
-    out, send, xs, first, gate, hidden, second = call(
-        forward_kernel,
+        ),
+        xt,
+    )
+    edge = (slabs, 16, 128)
+    out, send, xs, edge_first, edge_gate, edge_hidden, second = call(
+        halo_kernel,
         (
             shape((1, 16, rows, cols), bf16),
             shape((16, chunk, 128), bf16),
             shape((slabs + 2, pitch, 128), f32),
-            shape(slab, bf16),
-            shape(slab, f32),
-            shape(slab, bf16),
+            shape(edge, f32),
+            shape(edge, f32),
+            shape(edge, f32),
             shape(slab, bf16),
         ),
         [
-            pltpu.VMEM((slabs + 2, pitch, 128), f32),
+            pltpu.VMEM((slabs + 2, 64, 128), f32),
+            pltpu.VMEM((32 * slabs, 128), f32),
             pltpu.VMEM((16 * chunk, 128), f32),
             pltpu.VMEM((128, 128), f32),
         ],
-        1 << 28,
-        passed=9,
-    )(xt, left, right, taps_one, one_turned, bias_one, taps_two, two, bias_two)
+        1 << 27,
+        passed=11,
+    )(
+        xt, left, right, hidden, main_second, taps_one, one_turned, bias_one, taps_two, two, bias_two
+    )
     seen = lax.all_to_all(send, "member", 0, 0, tiled=True)
     cot = call(
         functools.partial(crps_kernel, rows * cols * tiles),
@@ -413,8 +475,10 @@
             pltpu.VMEM((64, 128), f32),
         ],
         1 << 28,
-        passed=9,
-    )(cot, xs, first, gate, hidden, second, one, two, taps_two)
+        passed=12,
+    )(
+        cot, xs, first, gate, hidden, edge_first, edge_gate, edge_hidden, second, one, two, taps_two
+    )
     axes = ("member", "tile")
     near = [[16 * g + k for k in range(16)] for g in range(members * tiles // 16)]
     far = [list(group) for group in zip(*near)]

time: 98.8 us -> 97.1 us (0.983)
  blocking collectives: 76.5 us -> 74.4 us
    all_to_all x1, blocking collectives: 18.5 us -> 16.7 us  [local(): seen = lax.all_to_all(send, 'member', 0, 0, tiled=True)]
  transfers between devices with their start and end apart: 2 -> 2, of which waited for: 0 -> 0; matrix products, arithmetic and copies ran while one was open for 0% -> 0% of each run, Pallas kernels for 1% -> 3%
where the time goes in v3:
time: 97.1 us; the launch traced here: 96.7 us
  blocking collectives  74.4 us (77%)
  Pallas kernels  10.8 us (11%)
  starting transfers between devices  10.7 us (11%)
    all_to_all x1, blocking collectives, local(): lax.all_to_all(packed, axes, 0, 0, tiled=True, axis_index_groups=near)  21.3 us
    all_to_all x1, blocking collectives, local(): seen = lax.all_to_all(send, 'member', 0, 0, tiled=True)  16.7 us
    all_to_all x1, blocking collectives, local(): cot = lax.all_to_all(cot, 'member', 0, 0, tiled=True)  13.2 us
    all_to_all x1, blocking collectives, local(): part = lax.all_to_all(part, axes, 0, 0, tiled=True, axis_index_groups=far)  11.8 us
    all_to_all x1, blocking collectives, local(): total = lax.all_to_all(part, axes, 0, 0, tiled=True, axis_index_groups=near)  11.4 us
    ppermute x1, starting transfers between devices, local(): left = lax.ppermute(last_cols, 'tile', up)  5.39 us
    ppermute x1, starting transfers between devices, local(): right = lax.ppermute(first_cols, 'tile', [(j, i) for i, j in up])  5.32 us
    pallas_call x1, Pallas kernels, local(): call(backward_kernel, shape((16, 4, 128), f32), [pltpu.VMEM((16 * chunk,...  2.87 us
  transfers between devices with their start and end apart: 2, of which 0 were waited for; matrix products, arithmetic and copies ran while one was open for 0% of the time, Pallas kernels for 3%

profile of v3, /device:TPU:1, one launch (start us, length us, event | category | flops | bytes accessed | tf_op | source)
XLA Modules:
  0.0 96.7 jit_solution(15578023451193216760)
XLA Ops:
  0.6 1.9 %shard_map.135 = (f32[16,128,128]{2,1,0:T(8,128)S(1)}, f32[56,128]{1,0:T(8,128)S(1)}, f32[56,128]{1,0:T(8,128)S(1)}) custom-call(bf16[1,64,32,128]{3,2,1,0:T(8,128)(2,1)} %x_hbm.1, f32[16,32,128]{2,1,0:T(8,128)} %target_ref.1), custom_call_target="tpu_custom_call" | custom-call | flops 1048576 | bytes 4194304 | tf_op jit(solution)/shard_map/pallas_call | solution.py:379
  2.6 5.4 %collective-permute-start = (f32[56,128]{1,0:T(8,128)S(1)}, f32[56,128]{1,0:T(8,128)S(1)}, u32[]{:S(2)}, u32[]{:S(2)}) collective-permute-start(f32[56,128]{1,0:T(8,128)S(1)} %get-tuple-element.35), channel_id=1, source_target_pairs={{0,1},{1,2},{2,3},{3,4},{4,5},{5,6},{6,7},{7,8},{8,9},{9,10},{10,1... | collective-permute-start | bytes 86024 | tf_op jit(solution)/shard_map/ppermute | solution.py:392
  8.0 5.3 %collective-permute-start.1 = (f32[56,128]{1,0:T(8,128)S(1)}, f32[56,128]{1,0:T(8,128)S(1)}, u32[]{:S(2)}, u32[]{:S(2)}) collective-permute-start(f32[56,128]{1,0:T(8,128)S(1)} %get-tuple-element.36), channel_id=1, source_target_pairs={{1,0},{2,1},{3,2},{4,3},{5,4},{6,5},{7,6},{8,7},{9,8},{10,9},{11,1... | collective-permute-start | bytes 86024 | tf_op jit(solution)/shard_map/ppermute | solution.py:393
  13.3 2.8 %shard_map.136 = (f32[16,128]{1,0:T(8,128)S(1)}, bf16[128,128]{1,0:T(8,128)(2,1)S(1)}, bf16[128,128]{1,0:T(8,128)(2,1)S(1)}, f32[8,128]{1,0:T(8,128)S(1)}, f32[1...) custom-call(f32[9,64]{1,0:T(8,128)} %bitcast.8, ...), custom_call_target="tpu_custom_call" | custom-call | flops 268435456 | bytes 4194304 | tf_op jit(solution)/shard_map/pallas_call | solution.py:397
  16.1 0.0 collective-permute-done.left_ref
  16.1 0.0 collective-permute-done.1.right_ref
  16.1 0.0 copy-start
  16.2 1.7 %shard_map.137 = (bf16[1,16,32,128]{3,2,1,0:T(8,128)(2,1)}, bf16[16,48,128]{2,1,0:T(8,128)(2,1)S(1)}, f32[18,160,128]{2,1,0:T(8,128)S(1)}, f32[16,16,128]{2,1,0:...) custom-call(f32[16,128,128]{2,1,0:T(8,128)S(1)} %get-tuple-element.34.xt_ref, ...), custom_call_target="tpu_custom_call" | custom-call | flops 134217728 | bytes 4194304 | tf_op jit(solution)/shard_map/pallas_call | solution.py:434
  17.9 16.7 %all_to_all.25.x_ref = bf16[16,48,128]{2,1,0:T(8,128)(2,1)S(1)} all-to-all(bf16[16,48,128]{2,1,0:T(8,128)(2,1)S(1)} %get-tuple-element.46), channel_id=1, replica_groups=mesh['member'=16,'tile'=32] {'member'}, dimensions={0} | all-to-all | bytes 393216 | tf_op jit(solution)/shard_map/all_to_all | solution.py:456
  34.6 0.0 copy-done
  34.6 0.7 shard_map.138
  35.3 13.2 %all_to_all.26.cot_ref = bf16[16,48,128]{2,1,0:T(8,128)(2,1)S(1)} all-to-all(bf16[16,48,128]{2,1,0:T(8,128)(2,1)S(1)} %shard_map.138), channel_id=1, replica_groups=mesh['member'=16,'tile'=32] {'member'}, dimensions={0} | all-to-all | bytes 393216 | tf_op jit(solution)/shard_map/all_to_all | solution.py:464
  48.5 2.9 %shard_map.139 = f32[16,4,128]{2,1,0:T(4,128)S(1)} custom-call(bf16[16,48,128]{2,1,0:T(8,128)(2,1)S(1)} %all_to_all.26.cot_ref, f32[18,160,128]{2,1,0:T(8,128)S(1)} %get-tuple-element.47.xs_ref, f32[16,128,128]{2,1,0:T(8,128)S(1)} %get-tuple-element.48.first_ref, f32[16,128,128]{2,1,0:T(8,128)S(1)} %get-tuple-element.49.gate_ref, ...), custom_call_target="tpu_custom_call" | custom-call | flops 268435456 | bytes 4194304 | tf_op jit(solution)/shard_map/pallas_call | solution.py:465
  51.4 21.3 %all_to_all.27 = f32[16,4,128]{2,1,0:T(4,128)S(1)} all-to-all(f32[16,4,128]{2,1,0:T(4,128)S(1)} %shard_map.139), channel_id=1, replica_groups={{0,1,2,3,4,5,6,7,8,9,10,11,12,13,14,15},{16,17,18,19,20,21,22,23,24,25,..., dimensions={0} | all-to-all | bytes 65536 | tf_op jit(solution)/shard_map/all_to_all | solution.py:485
  72.7 11.8 %all_to_all.28 = f32[32,4,128]{2,1,0:T(4,128)S(1)} all-to-all(f32[32,4,128]{2,1,0:T(4,128)S(1)} %broadcast_in_dim.20), channel_id=1, replica_groups={{0,16,32,48,64,80,96,112,128,144,160,176,192,208,224,240,256,272,288,30..., dimensions={0} | all-to-all | bytes 131072 | tf_op jit(solution)/shard_map/all_to_all | solution.py:488
  84.6 11.4 %all_to_all.29.total_ref = f32[16,4,128]{2,1,0:T(4,128)S(1)} all-to-all(f32[16,4,128]{2,1,0:T(4,128)S(1)} %broadcast_in_dim.21), channel_id=1, replica_groups={{0,1,2,3,4,5,6,7,8,9,10,11,12,13,14,15},{16,17,18,19,20,21,22,23,24,25,..., dimensions={0} | all-to-all | bytes 65536 | tf_op jit(solution)/shard_map/all_to_all | solution.py:491
  96.0 0.7 shard_map.140
  (4 shorter events, 0.1 us)
Async XLA Ops:
  2.6 13.6 %collective-permute-start = (f32[56,128]{1,0:T(8,128)S(1)}, f32[56,128]{1,0:T(8,128)S(1)}, u32[]{:S(2)}, u32[]{:S(2)}) collective-permute-start(f32[56,128]{1,0:T(8,128)S(1)} %get-tuple-element.35), channel_id=1, source_target_pairs={{0,1},{1,2},{2,3},{3,4},{4,5},{5,6},{6,7},{7,8},{8,9},{9,10},{10,1... | collective-permute-start | bytes 86024 | tf_op jit(solution)/shard_map/ppermute | solution.py:392
  8.0 8.2 %collective-permute-start.1 = (f32[56,128]{1,0:T(8,128)S(1)}, f32[56,128]{1,0:T(8,128)S(1)}, u32[]{:S(2)}, u32[]{:S(2)}) collective-permute-start(f32[56,128]{1,0:T(8,128)S(1)} %get-tuple-element.36), channel_id=1, source_target_pairs={{1,0},{2,1},{3,2},{4,3},{5,4},{6,5},{7,6},{8,7},{9,8},{10,9},{11,1... | collective-permute-start | bytes 86024 | tf_op jit(solution)/shard_map/ppermute | solution.py:393
  16.1 18.4 %copy-start = (f32[16,32,128]{2,1,0:T(8,128)S(1)}, f32[16,32,128]{2,1,0:T(8,128)}, u32[]{:S(2)}) copy-start(f32[16,32,128]{2,1,0:T(8,128)} %target_ref.1) | copy-start | bytes 786436

commit v4 on v3

--- a/solution.py
+++ b/solution.py
@@ -14,7 +14,9 @@
 pitch = 160
 own = 16
 wide = 144
-chunk = 48
+chunk = 40
+chunk_pitch = 50
+lat_pitch = 34
 edge_rows = 56
 
 f32 = jnp.float32
@@ -65,13 +67,21 @@
 
 
 def edge_kernel(x_hbm, target_hbm, xt_ref, first_ref, last_ref, x_ref, target_ref, rows_scr, sems):
-    x_copy, target_copy = fetch((x_hbm.at[0], target_hbm), (x_ref, target_ref), sems)
+    target_copy, x_copy = fetch((target_hbm, x_hbm.at[0]), (target_ref, x_ref), sems)
+    target_copy.wait()
+    for k in range(4):
+        turned = target_ref[4 * k : 4 * k + 4].reshape(128, 128).T
+        first_ref[48 + k : 49 + k, :] = turned[0:1]
+        last_ref[48 + k : 49 + k, :] = turned[127:128]
+    first_ref[52:56, :] = jnp.zeros((4, 128), f32)
+    last_ref[52:56, :] = jnp.zeros((4, 128), f32)
     x_copy.wait()
-    rows_scr[...] = x_ref[...].reshape(64 * 32, 128).astype(f32)
+    for c in range(64):
+        rows_scr[lat_pitch * c : lat_pitch * c + 32, :] = x_ref[c].astype(f32)
 
     def body(p):
         here = jnp.concatenate(
-            [rows_scr[pl.ds(p, 64, stride=32), :], rows_scr[pl.ds(p + 16, 64, stride=32), :]],
+            [rows_scr[pl.ds(p, 64, stride=lat_pitch), :], rows_scr[pl.ds(p + 16, 64, stride=lat_pitch), :]],
             axis=0,
         )
         turned = here.T
@@ -81,13 +91,6 @@
             last_ref[pl.ds(16 * j + p, 1), :] = turned[125 + j : 126 + j]
 
     each_slab(body)
-    target_copy.wait()
-    for k in range(4):
-        turned = target_ref[4 * k : 4 * k + 4].reshape(128, 128).T
-        first_ref[48 + k : 49 + k, :] = turned[0:1]
-        last_ref[48 + k : 49 + k, :] = turned[127:128]
-    first_ref[52:56, :] = jnp.zeros((4, 128), f32)
-    last_ref[52:56, :] = jnp.zeros((4, 128), f32)
 
 
 def main_kernel(
@@ -149,11 +152,12 @@
 
 
 def depthwise(taps_ref, ref, p, row, count):
-    total = jnp.zeros((count, 128), f32)
+    total = None
     for a in range(3):
         for b in range(3):
             tap = taps_ref[3 * a + b : 3 * a + b + 1, :]
-            total = total + tap * ref[p + a, row + b : row + b + count, :]
+            term = tap * ref[p + a, row + b : row + b + count, :]
+            total = term if total is None else total + term
     return total
 
 
@@ -219,17 +223,18 @@
         second = with_edges(main_second_ref[p], edge).astype(bf16)
         second_ref[p] = second
         y = dot(two, second, 1, 1) + bias_ref[...]
-        y_ref[pl.ds(p, 16, stride=chunk), :] = y[0:16]
-        y_ref[pl.ds(16 + p, 16, stride=chunk), :] = y[16:32]
+        y_ref[pl.ds(p, 16, stride=chunk_pitch), :] = y[0:16]
+        y_ref[pl.ds(16 + p, 16, stride=chunk_pitch), :] = y[16:32]
 
     each_slab(second_body)
     y = dot(two, edge_ref[...].astype(bf16), 1, 1) + bias_ref[...]
     lane = lanes_of((16, 128))
     y = jnp.where(lane < 32, y[0:16], jnp.where(lane < 64, pltpu.roll(y[16:32], 32, 1), 0.0))
-    y_ref[pl.ds(32, 16, stride=chunk), :] = y
-    send = y_ref[...].astype(bf16).reshape(16, chunk, 128)
-    send_ref[...] = send
-    out_ref[0] = send[:, 0:32]
+    y_ref[pl.ds(32, 16, stride=chunk_pitch), :] = y
+    for o in range(16):
+        send = y_ref[chunk_pitch * o : chunk_pitch * o + chunk, :].astype(bf16)
+        send_ref[o] = send
+        out_ref[0, o] = send[0:32]
 
 
 def slope(diff):
@@ -242,9 +247,9 @@
     turn = lax.rem(4 - lax.rem(me, 4), 4) * 32
     left = left_ref[pl.ds(48 + me // 4, 1), :]
     right = right_ref[pl.ds(48 + me // 4, 1), :]
-    left = pltpu.roll(jnp.broadcast_to(left, (16, 128)), turn, 1)
-    right = pltpu.roll(jnp.broadcast_to(right, (16, 128)), turn, 1)
-    lane = lanes_of((16, 128))
+    left = pltpu.roll(jnp.broadcast_to(left, (8, 128)), turn, 1)
+    right = pltpu.roll(jnp.broadcast_to(right, (8, 128)), turn, 1)
+    lane = lanes_of((8, 128))
     halo = jnp.where(
         lane < 16,
         left,
@@ -254,21 +259,17 @@
             jnp.where(lane < 48, pltpu.roll(left, 16, 1), pltpu.roll(right, 32, 1)),
         ),
     )
-    for part in range(3):
-        rows = slice(16 * part, 16 * part + 16)
-        used = 8 if part == 2 else 16
-        x = [x_ref[i, rows, :].astype(f32)[0:used] for i in range(members)]
+    for rows in (slice(0, 16), slice(16, 32), slice(32, 40)):
+        x = [x_ref[i, rows, :].astype(f32) for i in range(members)]
         total = [None] * members
         for i in range(members):
             for j in range(i + 1, members):
                 s = slope(x[i] - x[j])
                 total[i] = s if total[i] is None else total[i] + s
                 total[j] = -s if total[j] is None else total[j] - s
-        aim = halo[0:8] if part == 2 else target_ref[me, rows, :]
+        aim = halo if rows.start == 32 else target_ref[me, rows, :]
         for i in range(members):
             value = slope(x[i] - aim) - pair_weight / (members - 1) * total[i]
-            if part == 2:
-                value = jnp.concatenate([value, jnp.zeros((8, 128), f32)], axis=0)
             out_ref[i, rows, :] = (value / cells_all).astype(bf16)
 
 
@@ -282,7 +283,8 @@
     out_ref,
     cf_ref, bs_ref, sums_ref, cot_sum_ref, point_two_ref, point_one_ref, other_ref,
 ):
-    cf_ref[...] = cot_ref[...].reshape(16 * chunk, 128).astype(f32)
+    for o in range(16):
+        cf_ref[chunk_pitch * o : chunk_pitch * o + chunk, :] = cot_ref[o].astype(f32)
     two = two_ref[...]
     one = one_ref[...]
     sums_ref[...] = jnp.zeros(sums_ref.shape, f32)
@@ -293,7 +295,7 @@
 
     def cot_body(p):
         cot = jnp.concatenate(
-            [cf_ref[pl.ds(p, 16, stride=chunk), :], cf_ref[pl.ds(16 + p, 16, stride=chunk), :]], axis=0
+            [cf_ref[pl.ds(p, 16, stride=chunk_pitch), :], cf_ref[pl.ds(16 + p, 16, stride=chunk_pitch), :]], axis=0
         )
         cot_sum_ref[0:32] += cot
         cot = cot.astype(bf16)
@@ -301,7 +303,7 @@
         point_two_ref[...] += dot(cot, second_ref[p], 1, 0)
 
     each_slab(cot_body)
-    halo = cf_ref[pl.ds(32, 16, stride=chunk), :]
+    halo = cf_ref[pl.ds(32, 16, stride=chunk_pitch), :]
     halo = jnp.concatenate([halo, pltpu.roll(halo, 96, 1)], axis=0).astype(bf16)
     halo = rounded(dot(halo, two, 0, 0))
     for p in range(slabs):
@@ -310,13 +312,14 @@
     wrap_slabs(bs_ref)
 
     def body(p):
-        total = jnp.zeros((128, 128), f32)
+        total = None
         hidden = with_edges(hidden_ref[p], edge_hidden_ref[p])
         for a in range(3):
             for b in range(3):
                 t = 3 * a + b
                 back = bs_ref[p + 2 - a, 17 - b : 145 - b, :]
-                total = total + taps_two_ref[t : t + 1, :] * back
+                term = taps_two_ref[t : t + 1, :] * back
+                total = term if total is None else total + term
                 sums_ref[9 + t] += tap_sum(back * hidden)
         back_pre = (total * with_edges(gate_ref[p], edge_gate_ref[p])).astype(bf16)
         sums_ref[18] += tap_sum(back_pre.astype(f32))
@@ -382,7 +385,7 @@
         [
             pltpu.VMEM((chans, rows, cols), bf16),
             pltpu.VMEM((16, rows, cols), f32),
-            pltpu.VMEM((chans * rows, 128), f32),
+            pltpu.VMEM((chans * lat_pitch, 128), f32),
             pltpu.SemaphoreType.DMA((2,)),
         ],
         1 << 20,
@@ -445,7 +448,7 @@
         [
             pltpu.VMEM((slabs + 2, 64, 128), f32),
             pltpu.VMEM((32 * slabs, 128), f32),
-            pltpu.VMEM((16 * chunk, 128), f32),
+            pltpu.VMEM((16 * chunk_pitch, 128), f32),
             pltpu.VMEM((128, 128), f32),
         ],
         1 << 27,
@@ -466,7 +469,7 @@
         backward_kernel,
         shape((16, 4, 128), f32),
         [
-            pltpu.VMEM((16 * chunk, 128), f32),
+            pltpu.VMEM((16 * chunk_pitch, 128), f32),
             pltpu.VMEM((slabs + 2, pitch, 128), f32),
             pltpu.VMEM((19, 8, 128), f32),
             pltpu.VMEM((128, 128), f32),

time: 97.1 us -> 95.7 us (0.986)
  blocking collectives: 74.4 us -> 73.4 us
where the time goes in v4:
time: 95.7 us; the launch traced here: 95.3 us
  blocking collectives  73.4 us (77%)
  starting transfers between devices  10.7 us (11%)
  Pallas kernels  10.4 us (11%)
    all_to_all x1, blocking collectives, local(): lax.all_to_all(packed, axes, 0, 0, tiled=True, axis_index_groups=near)  20.9 us
    all_to_all x1, blocking collectives, local(): seen = lax.all_to_all(send, 'member', 0, 0, tiled=True)  16.4 us
    all_to_all x1, blocking collectives, local(): cot = lax.all_to_all(cot, 'member', 0, 0, tiled=True)  12.9 us
    all_to_all x1, blocking collectives, local(): part = lax.all_to_all(part, axes, 0, 0, tiled=True, axis_index_groups=far)  11.8 us
    all_to_all x1, blocking collectives, local(): total = lax.all_to_all(part, axes, 0, 0, tiled=True, axis_index_groups=near)  11.4 us
    ppermute x1, starting transfers between devices, local(): left = lax.ppermute(last_cols, 'tile', up)  5.39 us
    ppermute x1, starting transfers between devices, local(): right = lax.ppermute(first_cols, 'tile', [(j, i) for i, j in up])  5.32 us
    pallas_call x1, Pallas kernels, local(): call(main_kernel, (shape((16, 128), f32), shape((128, 128), bf16), shape(...  2.85 us
  transfers between devices with their start and end apart: 2, of which 0 were waited for; matrix products, arithmetic and copies ran while one was open for 0% of the time, Pallas kernels for 3%

profile of v4, /device:TPU:1, one launch (start us, length us, event | category | flops | bytes accessed | tf_op | source)
XLA Modules:
  0.0 95.3 jit_solution(5436510762545834448)
XLA Ops:
  0.6 1.5 %shard_map.135 = (f32[16,128,128]{2,1,0:T(8,128)S(1)}, f32[56,128]{1,0:T(8,128)S(1)}, f32[56,128]{1,0:T(8,128)S(1)}) custom-call(bf16[1,64,32,128]{3,2,1,0:T(8,128)(2,1)} %x_hbm.1, f32[16,32,128]{2,1,0:T(8,128)} %target_ref.1), custom_call_target="tpu_custom_call" | custom-call | flops 1048576 | bytes 4194304 | tf_op jit(solution)/shard_map/pallas_call | solution.py:382
  2.2 5.4 %collective-permute-start = (f32[56,128]{1,0:T(8,128)S(1)}, f32[56,128]{1,0:T(8,128)S(1)}, u32[]{:S(2)}, u32[]{:S(2)}) collective-permute-start(f32[56,128]{1,0:T(8,128)S(1)} %get-tuple-element.35), channel_id=1, source_target_pairs={{0,1},{1,2},{2,3},{3,4},{4,5},{5,6},{6,7},{7,8},{8,9},{9,10},{10,1... | collective-permute-start | bytes 86024 | tf_op jit(solution)/shard_map/ppermute | solution.py:395
  7.6 5.3 %collective-permute-start.1 = (f32[56,128]{1,0:T(8,128)S(1)}, f32[56,128]{1,0:T(8,128)S(1)}, u32[]{:S(2)}, u32[]{:S(2)}) collective-permute-start(f32[56,128]{1,0:T(8,128)S(1)} %get-tuple-element.36), channel_id=1, source_target_pairs={{1,0},{2,1},{3,2},{4,3},{5,4},{6,5},{7,6},{8,7},{9,8},{10,9},{11,1... | collective-permute-start | bytes 86024 | tf_op jit(solution)/shard_map/ppermute | solution.py:396
  12.9 2.9 %shard_map.136 = (f32[16,128]{1,0:T(8,128)S(1)}, bf16[128,128]{1,0:T(8,128)(2,1)S(1)}, bf16[128,128]{1,0:T(8,128)(2,1)S(1)}, f32[8,128]{1,0:T(8,128)S(1)}, f32[1...) custom-call(f32[9,64]{1,0:T(8,128)} %bitcast.8, ...), custom_call_target="tpu_custom_call" | custom-call | flops 268435456 | bytes 4194304 | tf_op jit(solution)/shard_map/pallas_call | solution.py:400
  15.7 0.0 collective-permute-done.left_ref
  15.7 0.0 collective-permute-done.1.right_ref
  15.8 0.0 copy-start
  15.8 1.7 %shard_map.137 = (bf16[1,16,32,128]{3,2,1,0:T(8,128)(2,1)}, bf16[16,40,128]{2,1,0:T(8,128)(2,1)S(1)}, f32[18,160,128]{2,1,0:T(8,128)S(1)}, f32[16,16,128]{2,1,0:...) custom-call(f32[16,128,128]{2,1,0:T(8,128)S(1)} %get-tuple-element.34.xt_ref, ...), custom_call_target="tpu_custom_call" | custom-call | flops 134217728 | bytes 4194304 | tf_op jit(solution)/shard_map/pallas_call | solution.py:437
  17.5 16.4 %all_to_all.25.x_ref = bf16[16,40,128]{2,1,0:T(8,128)(2,1)S(1)} all-to-all(bf16[16,40,128]{2,1,0:T(8,128)(2,1)S(1)} %get-tuple-element.46), channel_id=1, replica_groups=mesh['member'=16,'tile'=32] {'member'}, dimensions={0} | all-to-all | bytes 327680 | tf_op jit(solution)/shard_map/all_to_all | solution.py:459
  33.9 0.0 copy-done
  33.9 0.7 shard_map.138
  34.6 12.9 %all_to_all.26.cot_ref = bf16[16,40,128]{2,1,0:T(8,128)(2,1)S(1)} all-to-all(bf16[16,40,128]{2,1,0:T(8,128)(2,1)S(1)} %shard_map.138), channel_id=1, replica_groups=mesh['member'=16,'tile'=32] {'member'}, dimensions={0} | all-to-all | bytes 327680 | tf_op jit(solution)/shard_map/all_to_all | solution.py:467
  47.5 2.9 %shard_map.139 = f32[16,4,128]{2,1,0:T(4,128)S(1)} custom-call(bf16[16,40,128]{2,1,0:T(8,128)(2,1)S(1)} %all_to_all.26.cot_ref, f32[18,160,128]{2,1,0:T(8,128)S(1)} %get-tuple-element.47.xs_ref, f32[16,128,128]{2,1,0:T(8,128)S(1)} %get-tuple-element.48.first_ref, f32[16,128,128]{2,1,0:T(8,128)S(1)} %get-tuple-element.49.gate_ref, ...), custom_call_target="tpu_custom_call" | custom-call | flops 268435456 | bytes 4194304 | tf_op jit(solution)/shard_map/pallas_call | solution.py:468
  50.4 20.9 %all_to_all.27 = f32[16,4,128]{2,1,0:T(4,128)S(1)} all-to-all(f32[16,4,128]{2,1,0:T(4,128)S(1)} %shard_map.139), channel_id=1, replica_groups={{0,1,2,3,4,5,6,7,8,9,10,11,12,13,14,15},{16,17,18,19,20,21,22,23,24,25,..., dimensions={0} | all-to-all | bytes 65536 | tf_op jit(solution)/shard_map/all_to_all | solution.py:488
  71.3 11.8 %all_to_all.28 = f32[32,4,128]{2,1,0:T(4,128)S(1)} all-to-all(f32[32,4,128]{2,1,0:T(4,128)S(1)} %broadcast_in_dim.20), channel_id=1, replica_groups={{0,16,32,48,64,80,96,112,128,144,160,176,192,208,224,240,256,272,288,30..., dimensions={0} | all-to-all | bytes 131072 | tf_op jit(solution)/shard_map/all_to_all | solution.py:491
  83.2 11.4 %all_to_all.29.total_ref = f32[16,4,128]{2,1,0:T(4,128)S(1)} all-to-all(f32[16,4,128]{2,1,0:T(4,128)S(1)} %broadcast_in_dim.21), channel_id=1, replica_groups={{0,1,2,3,4,5,6,7,8,9,10,11,12,13,14,15},{16,17,18,19,20,21,22,23,24,25,..., dimensions={0} | all-to-all | bytes 65536 | tf_op jit(solution)/shard_map/all_to_all | solution.py:494
  94.6 0.7 shard_map.140
  (4 shorter events, 0.1 us)
Async XLA Ops:
  2.2 13.6 %collective-permute-start = (f32[56,128]{1,0:T(8,128)S(1)}, f32[56,128]{1,0:T(8,128)S(1)}, u32[]{:S(2)}, u32[]{:S(2)}) collective-permute-start(f32[56,128]{1,0:T(8,128)S(1)} %get-tuple-element.35), channel_id=1, source_target_pairs={{0,1},{1,2},{2,3},{3,4},{4,5},{5,6},{6,7},{7,8},{8,9},{9,10},{10,1... | collective-permute-start | bytes 86024 | tf_op jit(solution)/shard_map/ppermute | solution.py:395
  7.6 8.2 %collective-permute-start.1 = (f32[56,128]{1,0:T(8,128)S(1)}, f32[56,128]{1,0:T(8,128)S(1)}, u32[]{:S(2)}, u32[]{:S(2)}) collective-permute-start(f32[56,128]{1,0:T(8,128)S(1)} %get-tuple-element.36), channel_id=1, source_target_pairs={{1,0},{2,1},{3,2},{4,3},{5,4},{6,5},{7,6},{8,7},{9,8},{10,9},{11,1... | collective-permute-start | bytes 86024 | tf_op jit(solution)/shard_map/ppermute | solution.py:396
  15.8 18.1 %copy-start = (f32[16,32,128]{2,1,0:T(8,128)S(1)}, f32[16,32,128]{2,1,0:T(8,128)}, u32[]{:S(2)}) copy-start(f32[16,32,128]{2,1,0:T(8,128)} %target_ref.1) | copy-start | bytes 786436

commit v5 on v4

--- a/solution.py
+++ b/solution.py
@@ -95,10 +95,12 @@
 
 def main_kernel(
     depth_one_hbm, point_one_hbm, bias_one_hbm, depth_two_hbm, point_two_hbm, bias_two_hbm, xt_ref,
+    columns_ref,
     taps_one_ref, one_ref, one_turned_ref, bias_one_ref, taps_two_ref, two_ref, bias_two_ref,
-    first_ref, gate_ref, hidden_ref, second_ref,
-    d1_ref, p1_ref, b1_ref, d2_ref, p2_ref, b2_ref, turn_ref, xs_ref, hs_ref, sems,
+    first_ref, gate_ref, hidden_ref, hs_ref, columns_out_ref,
+    d1_ref, p1_ref, b1_ref, d2_ref, p2_ref, b2_ref, turn_ref, xs_ref, sems,
 ):
+    columns_out_ref[...] = columns_ref[...]
     places = (d1_ref, p1_ref, b1_ref, d2_ref, p2_ref, b2_ref)
     sources = (
         depth_one_hbm, point_one_hbm, bias_one_hbm, depth_two_hbm, point_two_hbm, bias_two_hbm
@@ -143,12 +145,15 @@
         hs_ref[p + 1, 8:136, :] = hidden
         gate_ref[p] = gate
 
-    def second_body(p):
-        second_ref[p] = depthwise(taps_two_ref, hs_ref, p, 7, 128)
-
     each_slab(first_body)
     wrap_slabs(hs_ref)
-    each_slab(second_body)
+
+
+def second_kernel(hs_ref, taps_ref, second_ref):
+    def body(p):
+        second_ref[p] = depthwise(taps_ref, hs_ref, p, 7, 128)
+
+    each_slab(body)
 
 
 def depthwise(taps_ref, ref, p, row, count):
@@ -393,10 +398,9 @@
     )(*in_hbm(predictor_inputs, target))
     up = [(i, (i + 1) % tiles) for i in range(tiles)]
     left = lax.ppermute(last_cols, "tile", up)
-    right = lax.ppermute(first_cols, "tile", [(j, i) for i, j in up])
     (
         taps_one, one, one_turned, bias_one, taps_two, two, bias_two,
-        first, gate, hidden, main_second,
+        first, gate, hidden, hs, first_cols,
     ) = call(
         main_kernel,
         (
@@ -410,7 +414,8 @@
             shape(slab, f32),
             shape(slab, f32),
             shape(slab, f32),
-            shape(slab, f32),
+            shape((slabs + 2, wide, 128), f32),
+            shape((edge_rows, 128), f32),
         ),
         [
             pltpu.VMEM((9, 64), f32),
@@ -421,18 +426,20 @@
             pltpu.VMEM((1, 16), f32),
             pltpu.VMEM((128, 128), f32),
             pltpu.VMEM((slabs + 2, wide, 128), f32),
-            pltpu.VMEM((slabs + 2, wide, 128), f32),
             pltpu.SemaphoreType.DMA((6,)),
         ],
         1 << 28,
         fetched=6,
-        passed=1,
+        passed=2,
     )(
         *in_hbm(
             depth_one.T, point_one, bias_one[None], depth_two.T, point_two, bias_two[None]
         ),
         xt,
-    )
+        first_cols,
+    )
+    right = lax.ppermute(first_cols, "tile", [(j, i) for i, j in up])
+    main_second = call(second_kernel, shape(slab, f32), [], 1 << 27, passed=2)(hs, taps_two)
     edge = (slabs, 16, 128)
     out, send, xs, edge_first, edge_gate, edge_hidden, second = call(
         halo_kernel,

time: 95.7 us -> 97.7 us (1.021)
  blocking collectives: 73.4 us -> 75.3 us
    all_to_all x1, blocking collectives: 16.4 us -> 18.8 us  [local(): seen = lax.all_to_all(send, 'member', 0, 0, tiled=True)]
  transfers between devices with their start and end apart: 2 -> 2, of which waited for: 0 -> 1; matrix products, arithmetic and copies ran while one was open for 0% -> 0% of each run, Pallas kernels for 3% -> 3%
where the time goes in v5:
time: 97.7 us; the launch traced here: 97.3 us
  blocking collectives  75.3 us (77%)
  starting transfers between devices  10.7 us (11%)
  Pallas kernels  10.3 us (11%)
    all_to_all x1, blocking collectives, local(): lax.all_to_all(packed, axes, 0, 0, tiled=True, axis_index_groups=near)  20.4 us
    all_to_all x1, blocking collectives, local(): seen = lax.all_to_all(send, 'member', 0, 0, tiled=True)  18.8 us
    all_to_all x1, blocking collectives, local(): cot = lax.all_to_all(cot, 'member', 0, 0, tiled=True)  12.9 us
    all_to_all x1, blocking collectives, local(): part = lax.all_to_all(part, axes, 0, 0, tiled=True, axis_index_groups=far)  11.8 us
    all_to_all x1, blocking collectives, local(): total = lax.all_to_all(part, axes, 0, 0, tiled=True, axis_index_groups=near)  11.4 us
    ppermute x1, starting transfers between devices, local(): left = lax.ppermute(last_cols, 'tile', up)  5.39 us
    ppermute x1, starting transfers between devices, local(): right = lax.ppermute(first_cols, 'tile', [(j, i) for i, j in up])  5.32 us
    pallas_call x1, Pallas kernels, local(): call(backward_kernel, shape((16, 4, 128), f32), [pltpu.VMEM((16 * chunk_p...  2.84 us
  transfers between devices with their start and end apart: 2, of which 1 were waited for; matrix products, arithmetic and copies ran while one was open for 0% of the time, Pallas kernels for 3%

profile of v5, /device:TPU:1, one launch (start us, length us, event | category | flops | bytes accessed | tf_op | source)
XLA Modules:
  0.0 97.3 jit_solution(9844761421690061024)
XLA Ops:
  0.6 1.5 %shard_map.135 = (f32[16,128,128]{2,1,0:T(8,128)S(1)}, f32[56,128]{1,0:T(8,128)S(1)}, f32[56,128]{1,0:T(8,128)S(1)}) custom-call(bf16[1,64,32,128]{3,2,1,0:T(8,128)(2,1)} %x_hbm.1, f32[16,32,128]{2,1,0:T(8,128)} %target_ref.1), custom_call_target="tpu_custom_call" | custom-call | flops 1048576 | bytes 4194304 | tf_op jit(solution)/shard_map/pallas_call | solution.py:387
  2.2 5.4 %collective-permute-start = (f32[56,128]{1,0:T(8,128)S(1)}, f32[56,128]{1,0:T(8,128)S(1)}, u32[]{:S(2)}, u32[]{:S(2)}) collective-permute-start(f32[56,128]{1,0:T(8,128)S(1)} %get-tuple-element.36), channel_id=1, source_target_pairs={{0,1},{1,2},{2,3},{3,4},{4,5},{5,6},{6,7},{7,8},{8,9},{9,10},{10,1... | collective-permute-start | bytes 86024 | tf_op jit(solution)/shard_map/ppermute | solution.py:400
  7.6 2.1 %shard_map.136 = (f32[16,128]{1,0:T(8,128)S(1)}, bf16[128,128]{1,0:T(8,128)(2,1)S(1)}, bf16[128,128]{1,0:T(8,128)(2,1)S(1)}, f32[8,128]{1,0:T(8,128)S(1)}, f32[1...) custom-call(f32[9,64]{1,0:T(8,128)} %bitcast.8, ...), custom_call_target="tpu_custom_call" | custom-call | flops 268435456 | bytes 4194304 | tf_op jit(solution)/shard_map/pallas_call | solution.py:404
  9.7 5.3 %collective-permute-start.1 = (f32[56,128]{1,0:T(8,128)S(1)}, f32[56,128]{1,0:T(8,128)S(1)}, u32[]{:S(2)}, u32[]{:S(2)}) collective-permute-start(f32[56,128]{1,0:T(8,128)S(1)} %get-tuple-element.38), channel_id=1, source_target_pairs={{1,0},{2,1},{3,2},{4,3},{5,4},{6,5},{7,6},{8,7},{9,8},{10,9},{11,1... | collective-permute-start | bytes 86024 | tf_op jit(solution)/shard_map/ppermute | solution.py:441
  15.0 0.7 shard_map.137.main_second_ref
  15.7 0.0 collective-permute-done.left_ref
  15.7 0.1 collective-permute-done.1.right_ref
  15.9 0.0 copy-start
  15.9 1.7 %shard_map.138 = (bf16[1,16,32,128]{3,2,1,0:T(8,128)(2,1)}, bf16[16,40,128]{2,1,0:T(8,128)(2,1)S(1)}, f32[18,160,128]{2,1,0:T(8,128)S(1)}, f32[16,16,128]{2,1,0:...) custom-call(f32[16,128,128]{2,1,0:T(8,128)S(1)} %get-tuple-element.35.xt_ref, ...), custom_call_target="tpu_custom_call" | custom-call | flops 134217728 | bytes 4194304 | tf_op jit(solution)/shard_map/pallas_call | solution.py:444
  17.6 18.8 %all_to_all.25.x_ref = bf16[16,40,128]{2,1,0:T(8,128)(2,1)S(1)} all-to-all(bf16[16,40,128]{2,1,0:T(8,128)(2,1)S(1)} %get-tuple-element.48), channel_id=1, replica_groups=mesh['member'=16,'tile'=32] {'member'}, dimensions={0} | all-to-all | bytes 327680 | tf_op jit(solution)/shard_map/all_to_all | solution.py:466
  36.3 0.0 copy-done
  36.4 0.7 shard_map.139
  37.1 12.9 %all_to_all.26.cot_ref = bf16[16,40,128]{2,1,0:T(8,128)(2,1)S(1)} all-to-all(bf16[16,40,128]{2,1,0:T(8,128)(2,1)S(1)} %shard_map.139), channel_id=1, replica_groups=mesh['member'=16,'tile'=32] {'member'}, dimensions={0} | all-to-all | bytes 327680 | tf_op jit(solution)/shard_map/all_to_all | solution.py:474
  50.0 2.8 %shard_map.140 = f32[16,4,128]{2,1,0:T(4,128)S(1)} custom-call(bf16[16,40,128]{2,1,0:T(8,128)(2,1)S(1)} %all_to_all.26.cot_ref, f32[18,160,128]{2,1,0:T(8,128)S(1)} %get-tuple-element.49.xs_ref, f32[16,128,128]{2,1,0:T(8,128)S(1)} %get-tuple-element.50.first_ref, f32[16,128,128]{2,1,0:T(8,128)S(1)} %get-tuple-element.51.gate_ref, ...), custom_call_target="tpu_custom_call" | custom-call | flops 268435456 | bytes 4194304 | tf_op jit(solution)/shard_map/pallas_call | solution.py:475
  52.8 20.4 %all_to_all.27 = f32[16,4,128]{2,1,0:T(4,128)S(1)} all-to-all(f32[16,4,128]{2,1,0:T(4,128)S(1)} %shard_map.140), channel_id=1, replica_groups={{0,1,2,3,4,5,6,7,8,9,10,11,12,13,14,15},{16,17,18,19,20,21,22,23,24,25,..., dimensions={0} | all-to-all | bytes 65536 | tf_op jit(solution)/shard_map/all_to_all | solution.py:495
  73.3 11.8 %all_to_all.28 = f32[32,4,128]{2,1,0:T(4,128)S(1)} all-to-all(f32[32,4,128]{2,1,0:T(4,128)S(1)} %broadcast_in_dim.20), channel_id=1, replica_groups={{0,16,32,48,64,80,96,112,128,144,160,176,192,208,224,240,256,272,288,30..., dimensions={0} | all-to-all | bytes 131072 | tf_op jit(solution)/shard_map/all_to_all | solution.py:498
  85.2 11.4 %all_to_all.29.total_ref = f32[16,4,128]{2,1,0:T(4,128)S(1)} all-to-all(f32[16,4,128]{2,1,0:T(4,128)S(1)} %broadcast_in_dim.21), channel_id=1, replica_groups={{0,1,2,3,4,5,6,7,8,9,10,11,12,13,14,15},{16,17,18,19,20,21,22,23,24,25,..., dimensions={0} | all-to-all | bytes 65536 | tf_op jit(solution)/shard_map/all_to_all | solution.py:501
  96.6 0.7 shard_map.141
  (4 shorter events, 0.1 us)
Async XLA Ops:
  2.2 13.6 %collective-permute-start = (f32[56,128]{1,0:T(8,128)S(1)}, f32[56,128]{1,0:T(8,128)S(1)}, u32[]{:S(2)}, u32[]{:S(2)}) collective-permute-start(f32[56,128]{1,0:T(8,128)S(1)} %get-tuple-element.36), channel_id=1, source_target_pairs={{0,1},{1,2},{2,3},{3,4},{4,5},{5,6},{6,7},{7,8},{8,9},{9,10},{10,1... | collective-permute-start | bytes 86024 | tf_op jit(solution)/shard_map/ppermute | solution.py:400
  9.7 6.2 %collective-permute-start.1 = (f32[56,128]{1,0:T(8,128)S(1)}, f32[56,128]{1,0:T(8,128)S(1)}, u32[]{:S(2)}, u32[]{:S(2)}) collective-permute-start(f32[56,128]{1,0:T(8,128)S(1)} %get-tuple-element.38), channel_id=1, source_target_pairs={{1,0},{2,1},{3,2},{4,3},{5,4},{6,5},{7,6},{8,7},{9,8},{10,9},{11,1... | collective-permute-start | bytes 86024 | tf_op jit(solution)/shard_map/ppermute | solution.py:441
  15.9 20.5 %copy-start = (f32[16,32,128]{2,1,0:T(8,128)S(1)}, f32[16,32,128]{2,1,0:T(8,128)}, u32[]{:S(2)}) copy-start(f32[16,32,128]{2,1,0:T(8,128)} %target_ref.1) | copy-start | bytes 786436

commit v6 on v4

--- a/solution.py
+++ b/solution.py
@@ -66,7 +66,14 @@
     return copies
 
 
-def edge_kernel(x_hbm, target_hbm, xt_ref, first_ref, last_ref, x_ref, target_ref, rows_scr, sems):
+def even_tile():
+    return lax.rem(lax.axis_index("tile"), 2) == 0
+
+
+def edge_kernel(
+    x_hbm, target_hbm, xt_ref, outer_ref, inner_ref,
+    x_ref, target_ref, rows_scr, first_ref, last_ref, sems,
+):
     target_copy, x_copy = fetch((target_hbm, x_hbm.at[0]), (target_ref, x_ref), sems)
     target_copy.wait()
     for k in range(4):
@@ -91,6 +98,10 @@
             last_ref[pl.ds(16 * j + p, 1), :] = turned[125 + j : 126 + j]
 
     each_slab(body)
+    even = even_tile()
+    first, last = first_ref[...], last_ref[...]
+    outer_ref[...] = jnp.where(even, first, last)
+    inner_ref[...] = jnp.where(even, last, first)
 
 
 def main_kernel(
@@ -172,12 +183,16 @@
 
 
 def halo_kernel(
-    xt_ref, left_ref, right_ref, hidden_ref, main_second_ref,
+    xt_ref, outer_ref, inner_ref, hidden_ref, main_second_ref,
     taps_one_ref, one_turned_ref, bias_one_ref, taps_two_ref, two_ref, bias_ref,
     out_ref, send_ref, xs_ref, first_ref, gate_ref, edge_hidden_ref, second_ref,
-    hs_ref, first_scr, y_ref, edge_ref,
+    hs_ref, first_scr, y_ref, edge_ref, left_ref, right_ref,
 ):
     two = two_ref[...]
+    even = even_tile()
+    outer, inner = outer_ref[...], inner_ref[...]
+    left_ref[...] = jnp.where(even, outer, inner)
+    right_ref[...] = jnp.where(even, inner, outer)
 
     for k in range(slabs + 2):
         xs_ref[k, 0:16, :] = jnp.zeros((16, 128), f32)
@@ -241,12 +256,15 @@
     return diff * lax.rsqrt(diff * diff + smooth_width * smooth_width)
 
 
-def crps_kernel(cells_all, x_ref, target_ref, left_ref, right_ref, out_ref):
+def crps_kernel(cells_all, x_ref, target_ref, outer_ref, inner_ref, out_ref):
     members = x_ref.shape[0]
     me = lax.axis_index("member")
     turn = lax.rem(4 - lax.rem(me, 4), 4) * 32
-    left = left_ref[pl.ds(48 + me // 4, 1), :]
-    right = right_ref[pl.ds(48 + me // 4, 1), :]
+    even = even_tile()
+    outer = outer_ref[pl.ds(48 + me // 4, 1), :]
+    inner = inner_ref[pl.ds(48 + me // 4, 1), :]
+    left = jnp.where(even, outer, inner)
+    right = jnp.where(even, inner, outer)
     left = pltpu.roll(jnp.broadcast_to(left, (8, 128)), turn, 1)
     right = pltpu.roll(jnp.broadcast_to(right, (8, 128)), turn, 1)
     lane = lanes_of((8, 128))
@@ -379,21 +397,22 @@
     tiles = lax.axis_size("tile")
     _, chans, rows, cols = predictor_inputs.shape
     slab = (slabs, cols, 128)
-    xt, first_cols, last_cols = call(
+    xt, outer, inner = call(
         edge_kernel,
         (shape(slab, f32), shape((edge_rows, 128), f32), shape((edge_rows, 128), f32)),
         [
             pltpu.VMEM((chans, rows, cols), bf16),
             pltpu.VMEM((16, rows, cols), f32),
             pltpu.VMEM((chans * lat_pitch, 128), f32),
+            pltpu.VMEM((edge_rows, 128), f32),
+            pltpu.VMEM((edge_rows, 128), f32),
             pltpu.SemaphoreType.DMA((2,)),
         ],
         1 << 20,
         fetched=2,
     )(*in_hbm(predictor_inputs, target))
-    up = [(i, (i + 1) % tiles) for i in range(tiles)]
-    left = lax.ppermute(last_cols, "tile", up)
-    right = lax.ppermute(first_cols, "tile", [(j, i) for i, j in up])
+    outer = lax.ppermute(outer, "tile", [(i, (i + 2 * (i % 2) - 1) % tiles) for i in range(tiles)])
+    inner = lax.ppermute(inner, "tile", [(i, i + 1 - 2 * (i % 2)) for i in range(tiles)])
     (
         taps_one, one, one_turned, bias_one, taps_two, two, bias_two,
         first, gate, hidden, main_second,
@@ -450,11 +469,13 @@
             pltpu.VMEM((32 * slabs, 128), f32),
             pltpu.VMEM((16 * chunk_pitch, 128), f32),
             pltpu.VMEM((128, 128), f32),
+            pltpu.VMEM((edge_rows, 128), f32),
+            pltpu.VMEM((edge_rows, 128), f32),
         ],
         1 << 27,
         passed=11,
     )(
-        xt, left, right, hidden, main_second, taps_one, one_turned, bias_one, taps_two, two, bias_two
+        xt, outer, inner, hidden, main_second, taps_one, one_turned, bias_one, taps_two, two, bias_two
     )
     seen = lax.all_to_all(send, "member", 0, 0, tiled=True)
     cot = call(
@@ -463,7 +484,7 @@
         [],
         1 << 24,
         passed=4,
-    )(seen, target, left, right)
+    )(seen, target, outer, inner)
     cot = lax.all_to_all(cot, "member", 0, 0, tiled=True)
     packed = call(
         backward_kernel,

time: 95.7 us -> 94.9 us (level)
  blocking collectives: 73.4 us -> 68.6 us
  starting transfers between devices: 10.7 us -> 14.7 us
    all_to_all x1, blocking collectives: 20.9 us -> 12.4 us  [local(): lax.all_to_all(packed, axes, 0, 0, tiled=True, axis_index_groups=near)]
    ppermute x2, starting transfers between devices: 10.7 us -> 14.7 us  [the longest x1 9.34 us: local(): lax.ppermute(inner, 'tile', [(i, i + 1 - 2 * (i % 2)) for i in range(tile...]
    all_to_all x1, blocking collectives: 16.4 us -> 19.9 us  [local(): seen = lax.all_to_all(send, 'member', 0, 0, tiled=True)]
where the time goes in v6:
time: 94.9 us; the launch traced here: 94.5 us
  blocking collectives  68.6 us (72%)
  starting transfers between devices  14.7 us (15%)
  Pallas kernels  10.4 us (11%)
    all_to_all x1, blocking collectives, local(): seen = lax.all_to_all(send, 'member', 0, 0, tiled=True)  19.9 us
    all_to_all x1, blocking collectives, local(): cot = lax.all_to_all(cot, 'member', 0, 0, tiled=True)  13.1 us
    all_to_all x1, blocking collectives, local(): lax.all_to_all(packed, axes, 0, 0, tiled=True, axis_index_groups=near)  12.4 us
    all_to_all x1, blocking collectives, local(): part = lax.all_to_all(part, axes, 0, 0, tiled=True, axis_index_groups=far)  11.8 us
    all_to_all x1, blocking collectives, local(): total = lax.all_to_all(part, axes, 0, 0, tiled=True, axis_index_groups=near)  11.4 us
    ppermute x1, starting transfers between devices, local(): lax.ppermute(inner, 'tile', [(i, i + 1 - 2 * (i % 2)) for i in range(tile...  9.34 us
    ppermute x1, starting transfers between devices, local(): lax.ppermute(outer, 'tile', [(i, (i + 2 * (i % 2) - 1) % tiles) for i in...  5.39 us
    pallas_call x1, Pallas kernels, local(): call(main_kernel, (shape((16, 128), f32), shape((128, 128), bf16), shape(...  2.85 us
  transfers between devices with their start and end apart: 2, of which 0 were waited for; matrix products, arithmetic and copies ran while one was open for 0% of the time, Pallas kernels for 3%

profile of v6, /device:TPU:1, one launch (start us, length us, event | category | flops | bytes accessed | tf_op | source)
XLA Modules:
  0.0 94.5 jit_solution(4184581411955131405)
XLA Ops:
  0.6 1.5 %shard_map.135 = (f32[16,128,128]{2,1,0:T(8,128)S(1)}, f32[56,128]{1,0:T(8,128)S(1)}, f32[56,128]{1,0:T(8,128)S(1)}) custom-call(bf16[1,64,32,128]{3,2,1,0:T(8,128)(2,1)} %x_hbm.1, f32[16,32,128]{2,1,0:T(8,128)} %target_ref.1), custom_call_target="tpu_custom_call" | custom-call | flops 1048576 | bytes 4194304 | tf_op jit(solution)/shard_map/pallas_call | solution.py:400
  2.2 5.4 %collective-permute-start = (f32[56,128]{1,0:T(8,128)S(1)}, f32[56,128]{1,0:T(8,128)S(1)}, u32[]{:S(2)}, u32[]{:S(2)}) collective-permute-start(f32[56,128]{1,0:T(8,128)S(1)} %get-tuple-element.35), channel_id=1, source_target_pairs={{0,31},{1,2},{2,1},{3,4},{4,3},{5,6},{6,5},{7,8},{8,7},{9,10},{10,... | collective-permute-start | bytes 86024 | tf_op jit(solution)/shard_map/ppermute | solution.py:414
  7.6 9.3 %collective-permute-start.1 = (f32[56,128]{1,0:T(8,128)S(1)}, f32[56,128]{1,0:T(8,128)S(1)}, u32[]{:S(2)}, u32[]{:S(2)}) collective-permute-start(f32[56,128]{1,0:T(8,128)S(1)} %get-tuple-element.36), channel_id=1, source_target_pairs={{0,1},{1,0},{2,3},{3,2},{4,5},{5,4},{6,7},{7,6},{8,9},{9,8},{10,11... | collective-permute-start | bytes 86024 | tf_op jit(solution)/shard_map/ppermute | solution.py:415
  16.9 2.9 %shard_map.136 = (f32[16,128]{1,0:T(8,128)S(1)}, bf16[128,128]{1,0:T(8,128)(2,1)S(1)}, bf16[128,128]{1,0:T(8,128)(2,1)S(1)}, f32[8,128]{1,0:T(8,128)S(1)}, f32[1...) custom-call(f32[9,64]{1,0:T(8,128)} %bitcast.8, ...), custom_call_target="tpu_custom_call" | custom-call | flops 268435456 | bytes 4194304 | tf_op jit(solution)/shard_map/pallas_call | solution.py:419
  19.8 0.0 collective-permute-done.outer_ref
  19.8 0.0 collective-permute-done.1.inner_ref
  19.8 0.0 copy-start
  19.8 1.7 %shard_map.137 = (bf16[1,16,32,128]{3,2,1,0:T(8,128)(2,1)}, bf16[16,40,128]{2,1,0:T(8,128)(2,1)S(1)}, f32[18,160,128]{2,1,0:T(8,128)S(1)}, f32[16,16,128]{2,1,0:...) custom-call(f32[16,128,128]{2,1,0:T(8,128)S(1)} %get-tuple-element.34.xt_ref, ...), custom_call_target="tpu_custom_call" | custom-call | flops 134217728 | bytes 4194304 | tf_op jit(solution)/shard_map/pallas_call | solution.py:456
  21.5 19.9 %all_to_all.25.x_ref = bf16[16,40,128]{2,1,0:T(8,128)(2,1)S(1)} all-to-all(bf16[16,40,128]{2,1,0:T(8,128)(2,1)S(1)} %get-tuple-element.46), channel_id=1, replica_groups=mesh['member'=16,'tile'=32] {'member'}, dimensions={0} | all-to-all | bytes 327680 | tf_op jit(solution)/shard_map/all_to_all | solution.py:480
  41.4 0.0 copy-done
  41.4 0.7 shard_map.138
  42.1 13.1 %all_to_all.26.cot_ref = bf16[16,40,128]{2,1,0:T(8,128)(2,1)S(1)} all-to-all(bf16[16,40,128]{2,1,0:T(8,128)(2,1)S(1)} %shard_map.138), channel_id=1, replica_groups=mesh['member'=16,'tile'=32] {'member'}, dimensions={0} | all-to-all | bytes 327680 | tf_op jit(solution)/shard_map/all_to_all | solution.py:488
  55.2 2.9 %shard_map.139 = f32[16,4,128]{2,1,0:T(4,128)S(1)} custom-call(bf16[16,40,128]{2,1,0:T(8,128)(2,1)S(1)} %all_to_all.26.cot_ref, f32[18,160,128]{2,1,0:T(8,128)S(1)} %get-tuple-element.47.xs_ref, f32[16,128,128]{2,1,0:T(8,128)S(1)} %get-tuple-element.48.first_ref, f32[16,128,128]{2,1,0:T(8,128)S(1)} %get-tuple-element.49.gate_ref, ...), custom_call_target="tpu_custom_call" | custom-call | flops 268435456 | bytes 4194304 | tf_op jit(solution)/shard_map/pallas_call | solution.py:489
  58.1 12.4 %all_to_all.27 = f32[16,4,128]{2,1,0:T(4,128)S(1)} all-to-all(f32[16,4,128]{2,1,0:T(4,128)S(1)} %shard_map.139), channel_id=1, replica_groups={{0,1,2,3,4,5,6,7,8,9,10,11,12,13,14,15},{16,17,18,19,20,21,22,23,24,25,..., dimensions={0} | all-to-all | bytes 65536 | tf_op jit(solution)/shard_map/all_to_all | solution.py:509
  70.5 11.8 %all_to_all.28 = f32[32,4,128]{2,1,0:T(4,128)S(1)} all-to-all(f32[32,4,128]{2,1,0:T(4,128)S(1)} %broadcast_in_dim.20), channel_id=1, replica_groups={{0,16,32,48,64,80,96,112,128,144,160,176,192,208,224,240,256,272,288,30..., dimensions={0} | all-to-all | bytes 131072 | tf_op jit(solution)/shard_map/all_to_all | solution.py:512
  82.4 11.4 %all_to_all.29.total_ref = f32[16,4,128]{2,1,0:T(4,128)S(1)} all-to-all(f32[16,4,128]{2,1,0:T(4,128)S(1)} %broadcast_in_dim.21), channel_id=1, replica_groups={{0,1,2,3,4,5,6,7,8,9,10,11,12,13,14,15},{16,17,18,19,20,21,22,23,24,25,..., dimensions={0} | all-to-all | bytes 65536 | tf_op jit(solution)/shard_map/all_to_all | solution.py:515
  93.8 0.7 shard_map.140
  (4 shorter events, 0.1 us)
Async XLA Ops:
  2.2 17.6 %collective-permute-start = (f32[56,128]{1,0:T(8,128)S(1)}, f32[56,128]{1,0:T(8,128)S(1)}, u32[]{:S(2)}, u32[]{:S(2)}) collective-permute-start(f32[56,128]{1,0:T(8,128)S(1)} %get-tuple-element.35), channel_id=1, source_target_pairs={{0,31},{1,2},{2,1},{3,4},{4,3},{5,6},{6,5},{7,8},{8,7},{9,10},{10,... | collective-permute-start | bytes 86024 | tf_op jit(solution)/shard_map/ppermute | solution.py:414
  7.6 12.2 %collective-permute-start.1 = (f32[56,128]{1,0:T(8,128)S(1)}, f32[56,128]{1,0:T(8,128)S(1)}, u32[]{:S(2)}, u32[]{:S(2)}) collective-permute-start(f32[56,128]{1,0:T(8,128)S(1)} %get-tuple-element.36), channel_id=1, source_target_pairs={{0,1},{1,0},{2,3},{3,2},{4,5},{5,4},{6,7},{7,6},{8,9},{9,8},{10,11... | collective-permute-start | bytes 86024 | tf_op jit(solution)/shard_map/ppermute | solution.py:415
  19.8 21.6 %copy-start = (f32[16,32,128]{2,1,0:T(8,128)S(1)}, f32[16,32,128]{2,1,0:T(8,128)}, u32[]{:S(2)}) copy-start(f32[16,32,128]{2,1,0:T(8,128)} %target_ref.1) | copy-start | bytes 786436

commit v7 on v6

--- a/solution.py
+++ b/solution.py
@@ -71,10 +71,17 @@
 
 
 def edge_kernel(
-    x_hbm, target_hbm, xt_ref, outer_ref, inner_ref,
+    x_hbm, target_hbm, depth_one_hbm, point_one_hbm, bias_one_hbm, depth_two_hbm, point_two_hbm,
+    bias_two_hbm,
+    xt_ref, outer_ref, inner_ref, d1_ref, p1_ref, b1_ref, d2_ref, p2_ref, b2_ref,
     x_ref, target_ref, rows_scr, first_ref, last_ref, sems,
 ):
-    target_copy, x_copy = fetch((target_hbm, x_hbm.at[0]), (target_ref, x_ref), sems)
+    sources = (
+        target_hbm, x_hbm.at[0], depth_one_hbm, point_one_hbm, bias_one_hbm, depth_two_hbm,
+        point_two_hbm, bias_two_hbm,
+    )
+    places = (target_ref, x_ref, d1_ref, p1_ref, b1_ref, d2_ref, p2_ref, b2_ref)
+    target_copy, x_copy, *weight_copies = fetch(sources, places, sems)
     target_copy.wait()
     for k in range(4):
         turned = target_ref[4 * k : 4 * k + 4].reshape(128, 128).T
@@ -102,19 +109,16 @@
     first, last = first_ref[...], last_ref[...]
     outer_ref[...] = jnp.where(even, first, last)
     inner_ref[...] = jnp.where(even, last, first)
+    for copy in weight_copies:
+        copy.wait()
 
 
 def main_kernel(
-    depth_one_hbm, point_one_hbm, bias_one_hbm, depth_two_hbm, point_two_hbm, bias_two_hbm, xt_ref,
+    d1_ref, p1_ref, b1_ref, d2_ref, p2_ref, b2_ref, xt_ref,
     taps_one_ref, one_ref, one_turned_ref, bias_one_ref, taps_two_ref, two_ref, bias_two_ref,
     first_ref, gate_ref, hidden_ref, second_ref,
-    d1_ref, p1_ref, b1_ref, d2_ref, p2_ref, b2_ref, turn_ref, xs_ref, hs_ref, sems,
+    turn_ref, xs_ref, hs_ref,
 ):
-    places = (d1_ref, p1_ref, b1_ref, d2_ref, p2_ref, b2_ref)
-    sources = (
-        depth_one_hbm, point_one_hbm, bias_one_hbm, depth_two_hbm, point_two_hbm, bias_two_hbm
-    )
-    copies = fetch(sources, places, sems)
     turn_ref[...] = jnp.zeros((128, 128), f32)
     for ref in (xs_ref, hs_ref):
         for k in range(slabs + 2):
@@ -123,8 +127,6 @@
     for p in range(slabs):
         xs_ref[p + 1, 8:136, :] = xt_ref[p]
     wrap_slabs(xs_ref)
-    for copy in copies:
-        copy.wait()
     zero = jnp.zeros((7, 128), f32)
     taps_one_ref[...] = jnp.concatenate([both_halves(d1_ref[...]), zero], axis=0)
     taps_two_ref[...] = jnp.concatenate([both_halves(d2_ref[...]), zero], axis=0)
@@ -186,7 +188,7 @@
     xt_ref, outer_ref, inner_ref, hidden_ref, main_second_ref,
     taps_one_ref, one_turned_ref, bias_one_ref, taps_two_ref, two_ref, bias_ref,
     out_ref, send_ref, xs_ref, first_ref, gate_ref, edge_hidden_ref, second_ref,
-    hs_ref, first_scr, y_ref, edge_ref, left_ref, right_ref,
+    hs_ref, y_ref, edge_ref, left_ref, right_ref,
 ):
     two = two_ref[...]
     even = even_tile()
@@ -204,27 +206,25 @@
             xs_ref[p + 1, 144 + j : 145 + j, :] = right_ref[16 * j + p : 16 * j + p + 1, :]
     wrap_slabs(xs_ref)
 
-    def first_body(p):
-        first = jnp.concatenate(
-            [depthwise(taps_one_ref, xs_ref, p, 7, 16), depthwise(taps_one_ref, xs_ref, p, 135, 16)],
-            axis=0,
-        )
-        first_scr[pl.ds(32 * p, 32), :] = rounded(first)
-
-    each_slab(first_body)
-    first = first_scr[...]
-    hidden, gate = activation(first, one_turned_ref[...], bias_one_ref)
-    for p in range(slabs):
-        rows = slice(32 * p + 8, 32 * p + 24)
-        first_ref[p] = first[rows]
-        gate_ref[p] = gate[rows]
-        edge_hidden_ref[p] = hidden[rows]
-        hs_ref[p + 1, 0:8, :] = jnp.zeros((8, 128), f32)
-        hs_ref[p + 1, 8:24, :] = hidden[32 * p : 32 * p + 16]
-        hs_ref[p + 1, 24:32, :] = hidden_ref[p, 8:16, :]
-        hs_ref[p + 1, 32:40, :] = hidden_ref[p, 112:120, :]
-        hs_ref[p + 1, 40:56, :] = hidden[32 * p + 16 : 32 * p + 32]
-        hs_ref[p + 1, 56:64, :] = jnp.zeros((8, 128), f32)
+    one_turned = one_turned_ref[...]
+    for k in range(0, slabs, 8):
+        first = [
+            depthwise(taps_one_ref, xs_ref, p, row, 16) for p in range(k, k + 8) for row in (7, 135)
+        ]
+        first = rounded(jnp.concatenate(first, axis=0))
+        hidden, gate = activation(first, one_turned, bias_one_ref)
+        for p in range(k, k + 8):
+            at = 32 * (p - k)
+            rows = slice(at + 8, at + 24)
+            first_ref[p] = first[rows]
+            gate_ref[p] = gate[rows]
+            edge_hidden_ref[p] = hidden[rows]
+            hs_ref[p + 1, 0:8, :] = jnp.zeros((8, 128), f32)
+            hs_ref[p + 1, 8:24, :] = hidden[at : at + 16]
+            hs_ref[p + 1, 24:32, :] = hidden_ref[p, 8:16, :]
+            hs_ref[p + 1, 32:40, :] = hidden_ref[p, 112:120, :]
+            hs_ref[p + 1, 40:56, :] = hidden[at + 16 : at + 32]
+            hs_ref[p + 1, 56:64, :] = jnp.zeros((8, 128), f32)
     wrap_slabs(hs_ref)
     y_ref[...] = jnp.zeros(y_ref.shape, f32)
     edge_ref[...] = jnp.zeros(edge_ref.shape, f32)
@@ -397,20 +397,35 @@
     tiles = lax.axis_size("tile")
     _, chans, rows, cols = predictor_inputs.shape
     slab = (slabs, cols, 128)
-    xt, outer, inner = call(
+    xt, outer, inner, *weights = call(
         edge_kernel,
-        (shape(slab, f32), shape((edge_rows, 128), f32), shape((edge_rows, 128), f32)),
+        (
+            shape(slab, f32),
+            shape((edge_rows, 128), f32),
+            shape((edge_rows, 128), f32),
+            shape((9, 64), f32),
+            shape((64, 64), bf16),
+            shape((1, 64), f32),
+            shape((9, 64), f32),
+            shape((16, 64), bf16),
+            shape((1, 16), f32),
+        ),
         [
             pltpu.VMEM((chans, rows, cols), bf16),
             pltpu.VMEM((16, rows, cols), f32),
             pltpu.VMEM((chans * lat_pitch, 128), f32),
             pltpu.VMEM((edge_rows, 128), f32),
             pltpu.VMEM((edge_rows, 128), f32),
-            pltpu.SemaphoreType.DMA((2,)),
+            pltpu.SemaphoreType.DMA((8,)),
         ],
         1 << 20,
-        fetched=2,
-    )(*in_hbm(predictor_inputs, target))
+        fetched=8,
+    )(
+        *in_hbm(
+            predictor_inputs, target, depth_one.T, point_one, bias_one[None], depth_two.T, point_two,
+            bias_two[None],
+        )
+    )
     outer = lax.ppermute(outer, "tile", [(i, (i + 2 * (i % 2) - 1) % tiles) for i in range(tiles)])
     inner = lax.ppermute(inner, "tile", [(i, i + 1 - 2 * (i % 2)) for i in range(tiles)])
     (
@@ -432,26 +447,13 @@
             shape(slab, f32),
         ),
         [
-            pltpu.VMEM((9, 64), f32),
-            pltpu.VMEM((64, 64), bf16),
-            pltpu.VMEM((1, 64), f32),
-            pltpu.VMEM((9, 64), f32),
-            pltpu.VMEM((16, 64), bf16),
-            pltpu.VMEM((1, 16), f32),
             pltpu.VMEM((128, 128), f32),
             pltpu.VMEM((slabs + 2, wide, 128), f32),
             pltpu.VMEM((slabs + 2, wide, 128), f32),
-            pltpu.SemaphoreType.DMA((6,)),
         ],
         1 << 28,
-        fetched=6,
-        passed=1,
-    )(
-        *in_hbm(
-            depth_one.T, point_one, bias_one[None], depth_two.T, point_two, bias_two[None]
-        ),
-        xt,
-    )
+        passed=7,
+    )(*weights, xt)
     edge = (slabs, 16, 128)
     out, send, xs, edge_first, edge_gate, edge_hidden, second = call(
         halo_kernel,
@@ -466,7 +468,6 @@
         ),
         [
             pltpu.VMEM((slabs + 2, 64, 128), f32),
-            pltpu.VMEM((32 * slabs, 128), f32),
             pltpu.VMEM((16 * chunk_pitch, 128), f32),
             pltpu.VMEM((128, 128), f32),
             pltpu.VMEM((edge_rows, 128), f32),

time: 94.9 us -> 94.1 us (level)
  transfers between devices with their start and end apart: 2 -> 2, of which waited for: 0 -> 0; matrix products, arithmetic and copies ran while one was open for 0% -> 0% of each run, Pallas kernels for 3% -> 2%
where the time goes in v7:
time: 94.1 us; the launch traced here: 93.7 us
  blocking collectives  68.6 us (73%)
  starting transfers between devices  14.7 us (16%)
  Pallas kernels  9.57 us (10%)
    all_to_all x1, blocking collectives, local(): seen = lax.all_to_all(send, 'member', 0, 0, tiled=True)  19.8 us
    all_to_all x1, blocking collectives, local(): cot = lax.all_to_all(cot, 'member', 0, 0, tiled=True)  13.1 us
    all_to_all x1, blocking collectives, local(): lax.all_to_all(packed, axes, 0, 0, tiled=True, axis_index_groups=near)  12.4 us
    all_to_all x1, blocking collectives, local(): part = lax.all_to_all(part, axes, 0, 0, tiled=True, axis_index_groups=far)  11.8 us
    all_to_all x1, blocking collectives, local(): total = lax.all_to_all(part, axes, 0, 0, tiled=True, axis_index_groups=near)  11.4 us
    ppermute x1, starting transfers between devices, local(): lax.ppermute(inner, 'tile', [(i, i + 1 - 2 * (i % 2)) for i in range(tile...  9.34 us
    ppermute x1, starting transfers between devices, local(): lax.ppermute(outer, 'tile', [(i, (i + 2 * (i % 2) - 1) % tiles) for i in...  5.39 us
    pallas_call x1, Pallas kernels, local(): call(backward_kernel, shape((16, 4, 128), f32), [pltpu.VMEM((16 * chunk_p...  2.87 us
  transfers between devices with their start and end apart: 2, of which 0 were waited for; matrix products, arithmetic and copies ran while one was open for 0% of the time, Pallas kernels for 2%

profile of v7, /device:TPU:1, one launch (start us, length us, event | category | flops | bytes accessed | tf_op | source)
XLA Modules:
  0.0 93.7 jit_solution(847499394058582746)
XLA Ops:
  0.6 1.6 %shard_map.135 = (f32[16,128,128]{2,1,0:T(8,128)S(1)}, f32[56,128]{1,0:T(8,128)S(1)}, f32[56,128]{1,0:T(8,128)S(1)}, f32[9,64]{1,0:T(8,128)S(1)}, bf16[64,64]{1,...) custom-call(bf16[1,64,32,128]{3,2,1,0:T(8,128)(2,1)} %x_hbm.1, ...), custom_call_target="tpu_custom_call" | custom-call | flops 1048576 | bytes 4194304 | tf_op jit(solution)/shard_map/pallas_call | solution.py:400
  2.2 5.4 %collective-permute-start = (f32[56,128]{1,0:T(8,128)S(1)}, f32[56,128]{1,0:T(8,128)S(1)}, u32[]{:S(2)}, u32[]{:S(2)}) collective-permute-start(f32[56,128]{1,0:T(8,128)S(1)} %get-tuple-element.41), channel_id=1, source_target_pairs={{0,31},{1,2},{2,1},{3,4},{4,3},{5,6},{6,5},{7,8},{8,7},{9,10},{10,... | collective-permute-start | bytes 86024 | tf_op jit(solution)/shard_map/ppermute | solution.py:429
  7.6 9.3 %collective-permute-start.1 = (f32[56,128]{1,0:T(8,128)S(1)}, f32[56,128]{1,0:T(8,128)S(1)}, u32[]{:S(2)}, u32[]{:S(2)}) collective-permute-start(f32[56,128]{1,0:T(8,128)S(1)} %get-tuple-element.42), channel_id=1, source_target_pairs={{0,1},{1,0},{2,3},{3,2},{4,5},{5,4},{6,7},{7,6},{8,9},{9,8},{10,11... | collective-permute-start | bytes 86024 | tf_op jit(solution)/shard_map/ppermute | solution.py:430
  17.0 2.1 %shard_map.136 = (f32[16,128]{1,0:T(8,128)S(1)}, bf16[128,128]{1,0:T(8,128)(2,1)S(1)}, bf16[128,128]{1,0:T(8,128)(2,1)S(1)}, f32[8,128]{1,0:T(8,128)S(1)}, f32[1...) custom-call(f32[9,64]{1,0:T(8,128)S(1)} %get-tuple-element.43.d1_ref, ...), custom_call_target="tpu_custom_call" | custom-call | flops 268435456 | bytes 4194304 | tf_op jit(solution)/shard_map/pallas_call | solution.py:434
  19.1 0.0 collective-permute-done.outer_ref
  19.1 0.0 collective-permute-done.1.inner_ref
  19.1 0.0 copy-start
  19.1 1.6 %shard_map.137 = (bf16[1,16,32,128]{3,2,1,0:T(8,128)(2,1)}, bf16[16,40,128]{2,1,0:T(8,128)(2,1)S(1)}, f32[18,160,128]{2,1,0:T(8,128)S(1)}, f32[16,16,128]{2,1,0:...) custom-call(f32[16,128,128]{2,1,0:T(8,128)S(1)} %get-tuple-element.40.xt_ref, ...), custom_call_target="tpu_custom_call" | custom-call | flops 134217728 | bytes 4194304 | tf_op jit(solution)/shard_map/pallas_call | solution.py:458
  20.7 19.8 %all_to_all.25.x_ref = bf16[16,40,128]{2,1,0:T(8,128)(2,1)S(1)} all-to-all(bf16[16,40,128]{2,1,0:T(8,128)(2,1)S(1)} %get-tuple-element.58), channel_id=1, replica_groups=mesh['member'=16,'tile'=32] {'member'}, dimensions={0} | all-to-all | bytes 327680 | tf_op jit(solution)/shard_map/all_to_all | solution.py:481
  40.5 0.0 copy-done
  40.5 0.7 shard_map.138
  41.3 13.1 %all_to_all.26.cot_ref = bf16[16,40,128]{2,1,0:T(8,128)(2,1)S(1)} all-to-all(bf16[16,40,128]{2,1,0:T(8,128)(2,1)S(1)} %shard_map.138), channel_id=1, replica_groups=mesh['member'=16,'tile'=32] {'member'}, dimensions={0} | all-to-all | bytes 327680 | tf_op jit(solution)/shard_map/all_to_all | solution.py:489
  54.4 2.9 %shard_map.139 = f32[16,4,128]{2,1,0:T(4,128)S(1)} custom-call(bf16[16,40,128]{2,1,0:T(8,128)(2,1)S(1)} %all_to_all.26.cot_ref, f32[18,160,128]{2,1,0:T(8,128)S(1)} %get-tuple-element.59.xs_ref, f32[16,128,128]{2,1,0:T(8,128)S(1)} %get-tuple-element.60.first_ref, f32[16,128,128]{2,1,0:T(8,128)S(1)} %get-tuple-element.61.gate_ref, ...), custom_call_target="tpu_custom_call" | custom-call | flops 268435456 | bytes 4194304 | tf_op jit(solution)/shard_map/pallas_call | solution.py:490
  57.3 12.4 %all_to_all.27 = f32[16,4,128]{2,1,0:T(4,128)S(1)} all-to-all(f32[16,4,128]{2,1,0:T(4,128)S(1)} %shard_map.139), channel_id=1, replica_groups={{0,1,2,3,4,5,6,7,8,9,10,11,12,13,14,15},{16,17,18,19,20,21,22,23,24,25,..., dimensions={0} | all-to-all | bytes 65536 | tf_op jit(solution)/shard_map/all_to_all | solution.py:510
  69.7 11.8 %all_to_all.28 = f32[32,4,128]{2,1,0:T(4,128)S(1)} all-to-all(f32[32,4,128]{2,1,0:T(4,128)S(1)} %broadcast_in_dim.20), channel_id=1, replica_groups={{0,16,32,48,64,80,96,112,128,144,160,176,192,208,224,240,256,272,288,30..., dimensions={0} | all-to-all | bytes 131072 | tf_op jit(solution)/shard_map/all_to_all | solution.py:513
  81.6 11.4 %all_to_all.29.total_ref = f32[16,4,128]{2,1,0:T(4,128)S(1)} all-to-all(f32[16,4,128]{2,1,0:T(4,128)S(1)} %broadcast_in_dim.21), channel_id=1, replica_groups={{0,1,2,3,4,5,6,7,8,9,10,11,12,13,14,15},{16,17,18,19,20,21,22,23,24,25,..., dimensions={0} | all-to-all | bytes 65536 | tf_op jit(solution)/shard_map/all_to_all | solution.py:516
  93.0 0.7 shard_map.140
  (4 shorter events, 0.1 us)
Async XLA Ops:
  2.2 16.8 %collective-permute-start = (f32[56,128]{1,0:T(8,128)S(1)}, f32[56,128]{1,0:T(8,128)S(1)}, u32[]{:S(2)}, u32[]{:S(2)}) collective-permute-start(f32[56,128]{1,0:T(8,128)S(1)} %get-tuple-element.41), channel_id=1, source_target_pairs={{0,31},{1,2},{2,1},{3,4},{4,3},{5,6},{6,5},{7,8},{8,7},{9,10},{10,... | collective-permute-start | bytes 86024 | tf_op jit(solution)/shard_map/ppermute | solution.py:429
  7.6 11.4 %collective-permute-start.1 = (f32[56,128]{1,0:T(8,128)S(1)}, f32[56,128]{1,0:T(8,128)S(1)}, u32[]{:S(2)}, u32[]{:S(2)}) collective-permute-start(f32[56,128]{1,0:T(8,128)S(1)} %get-tuple-element.42), channel_id=1, source_target_pairs={{0,1},{1,0},{2,3},{3,2},{4,5},{5,4},{6,7},{7,6},{8,9},{9,8},{10,11... | collective-permute-start | bytes 86024 | tf_op jit(solution)/shard_map/ppermute | solution.py:430
  19.1 21.4 %copy-start = (f32[16,32,128]{2,1,0:T(8,128)S(1)}, f32[16,32,128]{2,1,0:T(8,128)}, u32[]{:S(2)}) copy-start(f32[16,32,128]{2,1,0:T(8,128)} %target_ref.1) | copy-start | bytes 786436

commit v8 on v7

--- a/solution.py
+++ b/solution.py
@@ -187,7 +187,7 @@
 def halo_kernel(
     xt_ref, outer_ref, inner_ref, hidden_ref, main_second_ref,
     taps_one_ref, one_turned_ref, bias_one_ref, taps_two_ref, two_ref, bias_ref,
-    out_ref, send_ref, xs_ref, first_ref, gate_ref, edge_hidden_ref, second_ref,
+    send_ref, xs_ref, first_ref, gate_ref, edge_hidden_ref, second_ref,
     hs_ref, y_ref, edge_ref, left_ref, right_ref,
 ):
     two = two_ref[...]
@@ -247,16 +247,18 @@
     y = jnp.where(lane < 32, y[0:16], jnp.where(lane < 64, pltpu.roll(y[16:32], 32, 1), 0.0))
     y_ref[pl.ds(32, 16, stride=chunk_pitch), :] = y
     for o in range(16):
-        send = y_ref[chunk_pitch * o : chunk_pitch * o + chunk, :].astype(bf16)
-        send_ref[o] = send
-        out_ref[0, o] = send[0:32]
+        send_ref[o] = y_ref[chunk_pitch * o : chunk_pitch * o + chunk, :].astype(bf16)
 
 
 def slope(diff):
     return diff * lax.rsqrt(diff * diff + smooth_width * smooth_width)
 
 
-def crps_kernel(cells_all, x_ref, target_ref, outer_ref, inner_ref, out_ref):
+def crps_kernel(
+    cells_all, x_ref, target_ref, outer_ref, inner_ref, send_ref, out_ref, forecast_hbm, sem
+):
+    forecast_copy = pltpu.make_async_copy(send_ref.at[:, 0:32], forecast_hbm.at[0], sem)
+    forecast_copy.start()
     members = x_ref.shape[0]
     me = lax.axis_index("member")
     turn = lax.rem(4 - lax.rem(me, 4), 4) * 32
@@ -289,6 +291,7 @@
         for i in range(members):
             value = slope(x[i] - aim) - pair_weight / (members - 1) * total[i]
             out_ref[i, rows, :] = (value / cells_all).astype(bf16)
+    forecast_copy.wait()
 
 
 def tap_sum(value):
@@ -371,7 +374,7 @@
     point_two_ref[...] = rows_ref[24:40, 64:128]
 
 
-def call(kernel, out_shape, scratch, flops, fetched=0, passed=0):
+def call(kernel, out_shape, scratch, flops, fetched=0, passed=0, **out):
     hbm = pl.BlockSpec(memory_space=pltpu.HBM)
     vmem = pl.BlockSpec(memory_space=pltpu.VMEM)
     return pl.pallas_call(
@@ -379,6 +382,7 @@
         out_shape=out_shape,
         in_specs=[hbm] * fetched + [vmem] * passed,
         scratch_shapes=scratch,
+        **out,
         compiler_params=pltpu.CompilerParams(vmem_limit_bytes=24 * 1024 * 1024),
         cost_estimate=pl.CostEstimate(flops=flops, bytes_accessed=4 << 20, transcendentals=0),
     )
@@ -455,10 +459,9 @@
         passed=7,
     )(*weights, xt)
     edge = (slabs, 16, 128)
-    out, send, xs, edge_first, edge_gate, edge_hidden, second = call(
+    send, xs, edge_first, edge_gate, edge_hidden, second = call(
         halo_kernel,
         (
-            shape((1, 16, rows, cols), bf16),
             shape((16, chunk, 128), bf16),
             shape((slabs + 2, pitch, 128), f32),
             shape(edge, f32),
@@ -479,13 +482,14 @@
         xt, outer, inner, hidden, main_second, taps_one, one_turned, bias_one, taps_two, two, bias_two
     )
     seen = lax.all_to_all(send, "member", 0, 0, tiled=True)
-    cot = call(
+    cot, out = call(
         functools.partial(crps_kernel, rows * cols * tiles),
-        shape((members, chunk, 128), bf16),
-        [],
+        (shape((members, chunk, 128), bf16), shape((1, 16, rows, cols), bf16)),
+        [pltpu.SemaphoreType.DMA],
         1 << 24,
-        passed=4,
-    )(seen, target, outer, inner)
+        passed=5,
+        out_specs=(pl.BlockSpec(memory_space=pltpu.VMEM), pl.BlockSpec(memory_space=pltpu.HBM)),
+    )(seen, target, outer, inner, send)
     cot = lax.all_to_all(cot, "member", 0, 0, tiled=True)
     packed = call(
         backward_kernel,

time: 94.1 us -> 93.5 us (level)
  no operation moved by 1% of the time
where the time goes in v8:
time: 93.5 us; the launch traced here: 93.2 us
  blocking collectives  68.6 us (73%)
  starting transfers between devices  14.7 us (16%)
  Pallas kernels  8.99 us (10%)
    all_to_all x1, blocking collectives, local(): seen = lax.all_to_all(send, 'member', 0, 0, tiled=True)  19.9 us
    all_to_all x1, blocking collectives, local(): cot = lax.all_to_all(cot, 'member', 0, 0, tiled=True)  13.1 us
    all_to_all x1, blocking collectives, local(): lax.all_to_all(packed, axes, 0, 0, tiled=True, axis_index_groups=near)  12.4 us
    all_to_all x1, blocking collectives, local(): part = lax.all_to_all(part, axes, 0, 0, tiled=True, axis_index_groups=far)  11.8 us
    all_to_all x1, blocking collectives, local(): total = lax.all_to_all(part, axes, 0, 0, tiled=True, axis_index_groups=near)  11.4 us
    ppermute x1, starting transfers between devices, local(): lax.ppermute(inner, 'tile', [(i, i + 1 - 2 * (i % 2)) for i in range(tile...  9.34 us
    ppermute x1, starting transfers between devices, local(): lax.ppermute(outer, 'tile', [(i, (i + 2 * (i % 2) - 1) % tiles) for i in...  5.39 us
    pallas_call x1, Pallas kernels, local(): call(backward_kernel, shape((16, 4, 128), f32), [pltpu.VMEM((16 * chunk_p...  2.87 us
  transfers between devices with their start and end apart: 2, of which 0 were waited for; matrix products, arithmetic and copies ran while one was open for 0% of the time, Pallas kernels for 2%

profile of v8, /device:TPU:1, one launch (start us, length us, event | category | flops | bytes accessed | tf_op | source)
XLA Modules:
  0.0 93.2 jit_solution(9234341133356981580)
XLA Ops:
  0.6 1.6 %shard_map.135 = (f32[16,128,128]{2,1,0:T(8,128)S(1)}, f32[56,128]{1,0:T(8,128)S(1)}, f32[56,128]{1,0:T(8,128)S(1)}, f32[9,64]{1,0:T(8,128)S(1)}, bf16[64,64]{1,...) custom-call(bf16[1,64,32,128]{3,2,1,0:T(8,128)(2,1)} %x_hbm.1, ...), custom_call_target="tpu_custom_call" | custom-call | flops 1048576 | bytes 4194304 | tf_op jit(solution)/shard_map/pallas_call | solution.py:404
  2.2 5.4 %collective-permute-start = (f32[56,128]{1,0:T(8,128)S(1)}, f32[56,128]{1,0:T(8,128)S(1)}, u32[]{:S(2)}, u32[]{:S(2)}) collective-permute-start(f32[56,128]{1,0:T(8,128)S(1)} %get-tuple-element.42), channel_id=1, source_target_pairs={{0,31},{1,2},{2,1},{3,4},{4,3},{5,6},{6,5},{7,8},{8,7},{9,10},{10,... | collective-permute-start | bytes 86024 | tf_op jit(solution)/shard_map/ppermute | solution.py:433
  7.6 9.3 %collective-permute-start.1 = (f32[56,128]{1,0:T(8,128)S(1)}, f32[56,128]{1,0:T(8,128)S(1)}, u32[]{:S(2)}, u32[]{:S(2)}) collective-permute-start(f32[56,128]{1,0:T(8,128)S(1)} %get-tuple-element.43), channel_id=1, source_target_pairs={{0,1},{1,0},{2,3},{3,2},{4,5},{5,4},{6,7},{7,6},{8,9},{9,8},{10,11... | collective-permute-start | bytes 86024 | tf_op jit(solution)/shard_map/ppermute | solution.py:434
  17.0 2.1 %shard_map.136 = (f32[16,128]{1,0:T(8,128)S(1)}, bf16[128,128]{1,0:T(8,128)(2,1)S(1)}, bf16[128,128]{1,0:T(8,128)(2,1)S(1)}, f32[8,128]{1,0:T(8,128)S(1)}, f32[1...) custom-call(f32[9,64]{1,0:T(8,128)S(1)} %get-tuple-element.44.d1_ref, ...), custom_call_target="tpu_custom_call" | custom-call | flops 268435456 | bytes 4194304 | tf_op jit(solution)/shard_map/pallas_call | solution.py:438
  19.1 0.0 collective-permute-done.outer_ref
  19.1 0.0 collective-permute-done.1.inner_ref
  19.1 0.0 copy-start
  19.1 1.0 %shard_map.137 = (bf16[16,40,128]{2,1,0:T(8,128)(2,1)S(1)}, f32[18,160,128]{2,1,0:T(8,128)S(1)}, f32[16,16,128]{2,1,0:T(8,128)S(1)}, f32[16,16,128]{2,1,0:T(8,12...) custom-call(f32[16,128,128]{2,1,0:T(8,128)S(1)} %get-tuple-element.41.xt_ref, ...), custom_call_target="tpu_custom_call" | custom-call | flops 134217728 | bytes 4194304 | tf_op jit(solution)/shard_map/pallas_call | solution.py:462
  20.1 19.9 %all_to_all.25.x_ref = bf16[16,40,128]{2,1,0:T(8,128)(2,1)S(1)} all-to-all(bf16[16,40,128]{2,1,0:T(8,128)(2,1)S(1)} %get-tuple-element.58.send_ref), channel_id=1, replica_groups=mesh['member'=16,'tile'=32] {'member'}, dimensions={0} | all-to-all | bytes 327680 | tf_op jit(solution)/shard_map/all_to_all | solution.py:484
  40.0 0.0 copy-done
  40.0 0.8 shard_map.138
  40.7 13.1 %all_to_all.26.cot_ref = bf16[16,40,128]{2,1,0:T(8,128)(2,1)S(1)} all-to-all(bf16[16,40,128]{2,1,0:T(8,128)(2,1)S(1)} %get-tuple-element.60), channel_id=1, replica_groups=mesh['member'=16,'tile'=32] {'member'}, dimensions={0} | all-to-all | bytes 327680 | tf_op jit(solution)/shard_map/all_to_all | solution.py:493
  53.8 2.9 %shard_map.139 = f32[16,4,128]{2,1,0:T(4,128)S(1)} custom-call(bf16[16,40,128]{2,1,0:T(8,128)(2,1)S(1)} %all_to_all.26.cot_ref, f32[18,160,128]{2,1,0:T(8,128)S(1)} %get-tuple-element.61.xs_ref, f32[16,128,128]{2,1,0:T(8,128)S(1)} %get-tuple-element.62.first_ref, f32[16,128,128]{2,1,0:T(8,128)S(1)} %get-tuple-element.63.gate_ref, ...), custom_call_target="tpu_custom_call" | custom-call | flops 268435456 | bytes 4194304 | tf_op jit(solution)/shard_map/pallas_call | solution.py:494
  56.7 12.4 %all_to_all.27 = f32[16,4,128]{2,1,0:T(4,128)S(1)} all-to-all(f32[16,4,128]{2,1,0:T(4,128)S(1)} %shard_map.139), channel_id=1, replica_groups={{0,1,2,3,4,5,6,7,8,9,10,11,12,13,14,15},{16,17,18,19,20,21,22,23,24,25,..., dimensions={0} | all-to-all | bytes 65536 | tf_op jit(solution)/shard_map/all_to_all | solution.py:514
  69.2 11.8 %all_to_all.28 = f32[32,4,128]{2,1,0:T(4,128)S(1)} all-to-all(f32[32,4,128]{2,1,0:T(4,128)S(1)} %broadcast_in_dim.20), channel_id=1, replica_groups={{0,16,32,48,64,80,96,112,128,144,160,176,192,208,224,240,256,272,288,30..., dimensions={0} | all-to-all | bytes 131072 | tf_op jit(solution)/shard_map/all_to_all | solution.py:517
  81.1 11.4 %all_to_all.29.total_ref = f32[16,4,128]{2,1,0:T(4,128)S(1)} all-to-all(f32[16,4,128]{2,1,0:T(4,128)S(1)} %broadcast_in_dim.21), channel_id=1, replica_groups={{0,1,2,3,4,5,6,7,8,9,10,11,12,13,14,15},{16,17,18,19,20,21,22,23,24,25,..., dimensions={0} | all-to-all | bytes 65536 | tf_op jit(solution)/shard_map/all_to_all | solution.py:520
  92.5 0.7 shard_map.140
  (4 shorter events, 0.1 us)
Async XLA Ops:
  2.2 16.8 %collective-permute-start = (f32[56,128]{1,0:T(8,128)S(1)}, f32[56,128]{1,0:T(8,128)S(1)}, u32[]{:S(2)}, u32[]{:S(2)}) collective-permute-start(f32[56,128]{1,0:T(8,128)S(1)} %get-tuple-element.42), channel_id=1, source_target_pairs={{0,31},{1,2},{2,1},{3,4},{4,3},{5,6},{6,5},{7,8},{8,7},{9,10},{10,... | collective-permute-start | bytes 86024 | tf_op jit(solution)/shard_map/ppermute | solution.py:433
  7.6 11.4 %collective-permute-start.1 = (f32[56,128]{1,0:T(8,128)S(1)}, f32[56,128]{1,0:T(8,128)S(1)}, u32[]{:S(2)}, u32[]{:S(2)}) collective-permute-start(f32[56,128]{1,0:T(8,128)S(1)} %get-tuple-element.43), channel_id=1, source_target_pairs={{0,1},{1,0},{2,3},{3,2},{4,5},{5,4},{6,7},{7,6},{8,9},{9,8},{10,11... | collective-permute-start | bytes 86024 | tf_op jit(solution)/shard_map/ppermute | solution.py:434
  19.1 20.9 %copy-start = (f32[16,32,128]{2,1,0:T(8,128)S(1)}, f32[16,32,128]{2,1,0:T(8,128)}, u32[]{:S(2)}) copy-start(f32[16,32,128]{2,1,0:T(8,128)} %target_ref.1) | copy-start | bytes 786436

commit v9 on v8

--- a/solution.py
+++ b/solution.py
@@ -13,7 +13,6 @@
 slabs = 16
 pitch = 160
 own = 16
-wide = 144
 chunk = 40
 chunk_pitch = 50
 lat_pitch = 34
@@ -49,11 +48,18 @@
 
 
 def each_slab(body):
-    def step(p, carry):
+    for p in range(slabs):
         body(p)
-        return carry
-
-    lax.fori_loop(0, slabs, step, 0, unroll=True)
+
+
+def in_turn(make, ref, use):
+    for p in (0, slabs - 1, 1):
+        make(p)
+    wrap_slabs(ref)
+    for p in range(slabs):
+        if p + 2 < slabs - 1:
+            make(p + 2)
+        use(p)
 
 
 def fetch(sources, places, sems):
@@ -120,12 +126,8 @@
     turn_ref, xs_ref, hs_ref,
 ):
     turn_ref[...] = jnp.zeros((128, 128), f32)
-    for ref in (xs_ref, hs_ref):
-        for k in range(slabs + 2):
-            ref[k, 0:8, :] = jnp.zeros((8, 128), f32)
-            ref[k, 136:144, :] = jnp.zeros((8, 128), f32)
     for p in range(slabs):
-        xs_ref[p + 1, 8:136, :] = xt_ref[p]
+        xs_ref[p + 1] = xt_ref[p]
     wrap_slabs(xs_ref)
     zero = jnp.zeros((7, 128), f32)
     taps_one_ref[...] = jnp.concatenate([both_halves(d1_ref[...]), zero], axis=0)
@@ -149,19 +151,17 @@
     ).astype(bf16)
 
     def first_body(p):
-        first = rounded(depthwise(taps_one_ref, xs_ref, p, 7, 128))
+        first = rounded(depthwise(taps_one_ref, xs_ref, p, 7, 112))
         first_ref[p] = first
         hidden, gate = activation(first, one_turned, bias_one_ref)
         hidden_ref[p] = hidden
-        hs_ref[p + 1, 8:136, :] = hidden
+        hs_ref[p + 1] = hidden
         gate_ref[p] = gate
 
     def second_body(p):
-        second_ref[p] = depthwise(taps_two_ref, hs_ref, p, 7, 128)
-
-    each_slab(first_body)
-    wrap_slabs(hs_ref)
-    each_slab(second_body)
+        second_ref[p] = depthwise(taps_two_ref, hs_ref, p, 7, 96).astype(bf16)
+
+    in_turn(first_body, hs_ref, second_body)
 
 
 def depthwise(taps_ref, ref, p, row, count):
@@ -181,7 +181,7 @@
 
 
 def with_edges(main, edge):
-    return jnp.concatenate([edge[0:8], main[8:120], edge[8:16]], axis=0)
+    return jnp.concatenate([edge[0:8], main, edge[8:16]], axis=0)
 
 
 def halo_kernel(
@@ -221,21 +221,22 @@
             edge_hidden_ref[p] = hidden[rows]
             hs_ref[p + 1, 0:8, :] = jnp.zeros((8, 128), f32)
             hs_ref[p + 1, 8:24, :] = hidden[at : at + 16]
-            hs_ref[p + 1, 24:32, :] = hidden_ref[p, 8:16, :]
-            hs_ref[p + 1, 32:40, :] = hidden_ref[p, 112:120, :]
-            hs_ref[p + 1, 40:56, :] = hidden[at + 16 : at + 32]
-            hs_ref[p + 1, 56:64, :] = jnp.zeros((8, 128), f32)
+            hs_ref[p + 1, 24:40, :] = hidden_ref[p, 0:16, :]
+            hs_ref[p + 1, 40:56, :] = hidden_ref[p, 96:112, :]
+            hs_ref[p + 1, 56:72, :] = hidden[at + 16 : at + 32]
+            hs_ref[p + 1, 72:80, :] = jnp.zeros((8, 128), f32)
     wrap_slabs(hs_ref)
     y_ref[...] = jnp.zeros(y_ref.shape, f32)
     edge_ref[...] = jnp.zeros(edge_ref.shape, f32)
 
     def second_body(p):
-        before = depthwise(taps_two_ref, hs_ref, p, 7, 16)
-        after = depthwise(taps_two_ref, hs_ref, p, 39, 16)
+        before = depthwise(taps_two_ref, hs_ref, p, 7, 24)
+        after = depthwise(taps_two_ref, hs_ref, p, 47, 24)
         edge_ref[pl.ds(p, 1), :] = before[7:8]
-        edge_ref[pl.ds(16 + p, 1), :] = after[8:9]
-        edge = jnp.concatenate([before[8:16], after[0:8]], axis=0)
-        second = with_edges(main_second_ref[p], edge).astype(bf16)
+        edge_ref[pl.ds(16 + p, 1), :] = after[16:17]
+        second = jnp.concatenate(
+            [before[8:24].astype(bf16), main_second_ref[p], after[0:16].astype(bf16)], axis=0
+        )
         second_ref[p] = second
         y = dot(two, second, 1, 1) + bias_ref[...]
         y_ref[pl.ds(p, 16, stride=chunk_pitch), :] = y[0:16]
@@ -417,7 +418,7 @@
         [
             pltpu.VMEM((chans, rows, cols), bf16),
             pltpu.VMEM((16, rows, cols), f32),
-            pltpu.VMEM((chans * lat_pitch, 128), f32),
+            pltpu.VMEM((chans * lat_pitch + 32, 128), f32),
             pltpu.VMEM((edge_rows, 128), f32),
             pltpu.VMEM((edge_rows, 128), f32),
             pltpu.SemaphoreType.DMA((8,)),
@@ -445,15 +446,15 @@
             shape((16, 128), f32),
             shape((32, 128), bf16),
             shape((32, 128), f32),
-            shape(slab, f32),
-            shape(slab, f32),
-            shape(slab, f32),
-            shape(slab, f32),
+            shape((slabs, 112, 128), f32),
+            shape((slabs, 112, 128), f32),
+            shape((slabs, 112, 128), f32),
+            shape((slabs, 96, 128), bf16),
         ),
         [
             pltpu.VMEM((128, 128), f32),
-            pltpu.VMEM((slabs + 2, wide, 128), f32),
-            pltpu.VMEM((slabs + 2, wide, 128), f32),
+            pltpu.VMEM((slabs + 2, cols, 128), f32),
+            pltpu.VMEM((slabs + 2, 112, 128), f32),
         ],
         1 << 28,
         passed=7,
@@ -470,8 +471,8 @@
             shape(slab, bf16),
         ),
         [
-            pltpu.VMEM((slabs + 2, 64, 128), f32),
-            pltpu.VMEM((16 * chunk_pitch, 128), f32),
+            pltpu.VMEM((slabs + 2, 80, 128), f32),
+            pltpu.VMEM((16 * chunk_pitch + 40, 128), f32),
             pltpu.VMEM((128, 128), f32),
             pltpu.VMEM((edge_rows, 128), f32),
             pltpu.VMEM((edge_rows, 128), f32),
@@ -495,7 +496,7 @@
         backward_kernel,
         shape((16, 4, 128), f32),
         [
-            pltpu.VMEM((16 * chunk_pitch, 128), f32),
+            pltpu.VMEM((16 * chunk_pitch + 40, 128), f32),
             pltpu.VMEM((slabs + 2, pitch, 128), f32),
             pltpu.VMEM((19, 8, 128), f32),
             pltpu.VMEM((128, 128), f32),

time: 93.5 us -> 93.5 us (level)
  no operation moved by 1% of the time
where the time goes in v9:
time: 93.5 us; the launch traced here: 93.1 us
  blocking collectives  68.9 us (74%)
  starting transfers between devices  14.7 us (16%)
  Pallas kernels  8.63 us (9%)
    all_to_all x1, blocking collectives, local(): seen = lax.all_to_all(send, 'member', 0, 0, tiled=True)  19.9 us
    all_to_all x1, blocking collectives, local(): cot = lax.all_to_all(cot, 'member', 0, 0, tiled=True)  13.1 us
    all_to_all x1, blocking collectives, local(): lax.all_to_all(packed, axes, 0, 0, tiled=True, axis_index_groups=near)  12.7 us
    all_to_all x1, blocking collectives, local(): part = lax.all_to_all(part, axes, 0, 0, tiled=True, axis_index_groups=far)  11.8 us
    all_to_all x1, blocking collectives, local(): total = lax.all_to_all(part, axes, 0, 0, tiled=True, axis_index_groups=near)  11.4 us
    ppermute x1, starting transfers between devices, local(): lax.ppermute(inner, 'tile', [(i, i + 1 - 2 * (i % 2)) for i in range(tile...  9.34 us
    ppermute x1, starting transfers between devices, local(): lax.ppermute(outer, 'tile', [(i, (i + 2 * (i % 2) - 1) % tiles) for i in...  5.39 us
    pallas_call x1, Pallas kernels, local(): call(backward_kernel, shape((16, 4, 128), f32), [pltpu.VMEM((16 * chunk_p...  2.83 us
  transfers between devices with their start and end apart: 2, of which 0 were waited for; matrix products, arithmetic and copies ran while one was open for 0% of the time, Pallas kernels for 2%

profile of v9, /device:TPU:1, one launch (start us, length us, event | category | flops | bytes accessed | tf_op | source)
XLA Modules:
  0.0 93.1 jit_solution(4361856185460570964)
XLA Ops:
  0.6 1.6 %shard_map.135 = (f32[16,128,128]{2,1,0:T(8,128)S(1)}, f32[56,128]{1,0:T(8,128)S(1)}, f32[56,128]{1,0:T(8,128)S(1)}, f32[9,64]{1,0:T(8,128)S(1)}, bf16[64,64]{1,...) custom-call(bf16[1,64,32,128]{3,2,1,0:T(8,128)(2,1)} %x_hbm.1, ...), custom_call_target="tpu_custom_call" | custom-call | flops 1048576 | bytes 4194304 | tf_op jit(solution)/shard_map/pallas_call | solution.py:405
  2.2 5.4 %collective-permute-start = (f32[56,128]{1,0:T(8,128)S(1)}, f32[56,128]{1,0:T(8,128)S(1)}, u32[]{:S(2)}, u32[]{:S(2)}) collective-permute-start(f32[56,128]{1,0:T(8,128)S(1)} %get-tuple-element.42), channel_id=1, source_target_pairs={{0,31},{1,2},{2,1},{3,4},{4,3},{5,6},{6,5},{7,8},{8,7},{9,10},{10,... | collective-permute-start | bytes 86024 | tf_op jit(solution)/shard_map/ppermute | solution.py:434
  7.6 9.3 %collective-permute-start.1 = (f32[56,128]{1,0:T(8,128)S(1)}, f32[56,128]{1,0:T(8,128)S(1)}, u32[]{:S(2)}, u32[]{:S(2)}) collective-permute-start(f32[56,128]{1,0:T(8,128)S(1)} %get-tuple-element.43), channel_id=1, source_target_pairs={{0,1},{1,0},{2,3},{3,2},{4,5},{5,4},{6,7},{7,6},{8,9},{9,8},{10,11... | collective-permute-start | bytes 86024 | tf_op jit(solution)/shard_map/ppermute | solution.py:435
  17.0 1.7 %shard_map.136 = (f32[16,128]{1,0:T(8,128)S(1)}, bf16[128,128]{1,0:T(8,128)(2,1)S(1)}, bf16[128,128]{1,0:T(8,128)(2,1)S(1)}, f32[8,128]{1,0:T(8,128)S(1)}, f32[1...) custom-call(f32[9,64]{1,0:T(8,128)S(1)} %get-tuple-element.44.d1_ref, ...), custom_call_target="tpu_custom_call" | custom-call | flops 268435456 | bytes 4194304 | tf_op jit(solution)/shard_map/pallas_call | solution.py:439
  18.7 0.0 copy-start
  18.7 0.0 collective-permute-done.outer_ref
  18.7 0.0 collective-permute-done.1.inner_ref
  18.7 1.0 %shard_map.137 = (bf16[16,40,128]{2,1,0:T(8,128)(2,1)S(1)}, f32[18,160,128]{2,1,0:T(8,128)S(1)}, f32[16,16,128]{2,1,0:T(8,128)S(1)}, f32[16,16,128]{2,1,0:T(8,12...) custom-call(f32[16,128,128]{2,1,0:T(8,128)S(1)} %get-tuple-element.41.xt_ref, ...), custom_call_target="tpu_custom_call" | custom-call | flops 134217728 | bytes 4194304 | tf_op jit(solution)/shard_map/pallas_call | solution.py:463
  19.8 19.9 %all_to_all.25.x_ref = bf16[16,40,128]{2,1,0:T(8,128)(2,1)S(1)} all-to-all(bf16[16,40,128]{2,1,0:T(8,128)(2,1)S(1)} %get-tuple-element.58.send_ref), channel_id=1, replica_groups=mesh['member'=16,'tile'=32] {'member'}, dimensions={0} | all-to-all | bytes 327680 | tf_op jit(solution)/shard_map/all_to_all | solution.py:485
  39.6 0.0 copy-done
  39.6 0.8 shard_map.138
  40.4 13.1 %all_to_all.26.cot_ref = bf16[16,40,128]{2,1,0:T(8,128)(2,1)S(1)} all-to-all(bf16[16,40,128]{2,1,0:T(8,128)(2,1)S(1)} %get-tuple-element.60), channel_id=1, replica_groups=mesh['member'=16,'tile'=32] {'member'}, dimensions={0} | all-to-all | bytes 327680 | tf_op jit(solution)/shard_map/all_to_all | solution.py:494
  53.5 2.8 %shard_map.139 = f32[16,4,128]{2,1,0:T(4,128)S(1)} custom-call(bf16[16,40,128]{2,1,0:T(8,128)(2,1)S(1)} %all_to_all.26.cot_ref, f32[18,160,128]{2,1,0:T(8,128)S(1)} %get-tuple-element.61.xs_ref, f32[16,112,128]{2,1,0:T(8,128)S(1)} %get-tuple-element.62.first_ref, f32[16,112,128]{2,1,0:T(8,128)S(1)} %get-tuple-element.63.gate_ref, ...), custom_call_target="tpu_custom_call" | custom-call | flops 268435456 | bytes 4194304 | tf_op jit(solution)/shard_map/pallas_call | solution.py:495
  56.4 12.7 %all_to_all.27 = f32[16,4,128]{2,1,0:T(4,128)S(1)} all-to-all(f32[16,4,128]{2,1,0:T(4,128)S(1)} %shard_map.139), channel_id=1, replica_groups={{0,1,2,3,4,5,6,7,8,9,10,11,12,13,14,15},{16,17,18,19,20,21,22,23,24,25,..., dimensions={0} | all-to-all | bytes 65536 | tf_op jit(solution)/shard_map/all_to_all | solution.py:515
  69.1 11.8 %all_to_all.28 = f32[32,4,128]{2,1,0:T(4,128)S(1)} all-to-all(f32[32,4,128]{2,1,0:T(4,128)S(1)} %broadcast_in_dim.20), channel_id=1, replica_groups={{0,16,32,48,64,80,96,112,128,144,160,176,192,208,224,240,256,272,288,30..., dimensions={0} | all-to-all | bytes 131072 | tf_op jit(solution)/shard_map/all_to_all | solution.py:518
  81.0 11.4 %all_to_all.29.total_ref = f32[16,4,128]{2,1,0:T(4,128)S(1)} all-to-all(f32[16,4,128]{2,1,0:T(4,128)S(1)} %broadcast_in_dim.21), channel_id=1, replica_groups={{0,1,2,3,4,5,6,7,8,9,10,11,12,13,14,15},{16,17,18,19,20,21,22,23,24,25,..., dimensions={0} | all-to-all | bytes 65536 | tf_op jit(solution)/shard_map/all_to_all | solution.py:521
  92.4 0.7 shard_map.140
  (4 shorter events, 0.1 us)
Async XLA Ops:
  2.2 16.5 %collective-permute-start = (f32[56,128]{1,0:T(8,128)S(1)}, f32[56,128]{1,0:T(8,128)S(1)}, u32[]{:S(2)}, u32[]{:S(2)}) collective-permute-start(f32[56,128]{1,0:T(8,128)S(1)} %get-tuple-element.42), channel_id=1, source_target_pairs={{0,31},{1,2},{2,1},{3,4},{4,3},{5,6},{6,5},{7,8},{8,7},{9,10},{10,... | collective-permute-start | bytes 86024 | tf_op jit(solution)/shard_map/ppermute | solution.py:434
  7.6 11.1 %collective-permute-start.1 = (f32[56,128]{1,0:T(8,128)S(1)}, f32[56,128]{1,0:T(8,128)S(1)}, u32[]{:S(2)}, u32[]{:S(2)}) collective-permute-start(f32[56,128]{1,0:T(8,128)S(1)} %get-tuple-element.43), channel_id=1, source_target_pairs={{0,1},{1,0},{2,3},{3,2},{4,5},{5,4},{6,7},{7,6},{8,9},{9,8},{10,11... | collective-permute-start | bytes 86024 | tf_op jit(solution)/shard_map/ppermute | solution.py:435
  18.7 20.9 %copy-start = (f32[16,32,128]{2,1,0:T(8,128)S(1)}, f32[16,32,128]{2,1,0:T(8,128)}, u32[]{:S(2)}) copy-start(f32[16,32,128]{2,1,0:T(8,128)} %target_ref.1) | copy-start | bytes 786436

commit v10 on v9

--- a/solution.py
+++ b/solution.py
@@ -510,7 +510,11 @@
         cot, xs, first, gate, hidden, edge_first, edge_gate, edge_hidden, second, one, two, taps_two
     )
     axes = ("member", "tile")
-    near = [[16 * g + k for k in range(16)] for g in range(members * tiles // 16)]
+    near = [
+        [32 * (2 * y + x_hi) + 2 * pair + core for y in range(8) for core in range(2)]
+        for x_hi in range(2)
+        for pair in range(16)
+    ]
     far = [list(group) for group in zip(*near)]
     part = lax.all_to_all(packed, axes, 0, 0, tiled=True, axis_index_groups=near)
     part = jnp.sum(part, axis=0)

time: 93.5 us -> 93.4 us (level)
  no operation moved by 1% of the time
where the time goes in v10:
time: 93.4 us; the launch traced here: 93 us
  blocking collectives  68.8 us (74%)
  starting transfers between devices  14.7 us (16%)
  Pallas kernels  8.63 us (9%)
    all_to_all x1, blocking collectives, local(): seen = lax.all_to_all(send, 'member', 0, 0, tiled=True)  19.9 us
    all_to_all x1, blocking collectives, local(): cot = lax.all_to_all(cot, 'member', 0, 0, tiled=True)  13.1 us
    all_to_all x1, blocking collectives, local(): lax.all_to_all(packed, axes, 0, 0, tiled=True, axis_index_groups=near)  12.4 us
    all_to_all x1, blocking collectives, local(): part = lax.all_to_all(part, axes, 0, 0, tiled=True, axis_index_groups=far)  11.9 us
    all_to_all x1, blocking collectives, local(): total = lax.all_to_all(part, axes, 0, 0, tiled=True, axis_index_groups=near)  11.6 us
    ppermute x1, starting transfers between devices, local(): lax.ppermute(inner, 'tile', [(i, i + 1 - 2 * (i % 2)) for i in range(tile...  9.34 us
    ppermute x1, starting transfers between devices, local(): lax.ppermute(outer, 'tile', [(i, (i + 2 * (i % 2) - 1) % tiles) for i in...  5.39 us
    pallas_call x1, Pallas kernels, local(): call(backward_kernel, shape((16, 4, 128), f32), [pltpu.VMEM((16 * chunk_p...  2.83 us
  transfers between devices with their start and end apart: 2, of which 0 were waited for; matrix products, arithmetic and copies ran while one was open for 0% of the time, Pallas kernels for 2%

profile of v10, /device:TPU:1, one launch (start us, length us, event | category | flops | bytes accessed | tf_op | source)
XLA Modules:
  0.0 93.0 jit_solution(1855296490455471498)
XLA Ops:
  0.6 1.6 %shard_map.135 = (f32[16,128,128]{2,1,0:T(8,128)S(1)}, f32[56,128]{1,0:T(8,128)S(1)}, f32[56,128]{1,0:T(8,128)S(1)}, f32[9,64]{1,0:T(8,128)S(1)}, bf16[64,64]{1,...) custom-call(bf16[1,64,32,128]{3,2,1,0:T(8,128)(2,1)} %x_hbm.1, ...), custom_call_target="tpu_custom_call" | custom-call | flops 1048576 | bytes 4194304 | tf_op jit(solution)/shard_map/pallas_call | solution.py:405
  2.2 5.4 %collective-permute-start = (f32[56,128]{1,0:T(8,128)S(1)}, f32[56,128]{1,0:T(8,128)S(1)}, u32[]{:S(2)}, u32[]{:S(2)}) collective-permute-start(f32[56,128]{1,0:T(8,128)S(1)} %get-tuple-element.42), channel_id=1, source_target_pairs={{0,31},{1,2},{2,1},{3,4},{4,3},{5,6},{6,5},{7,8},{8,7},{9,10},{10,... | collective-permute-start | bytes 86024 | tf_op jit(solution)/shard_map/ppermute | solution.py:434
  7.6 9.3 %collective-permute-start.1 = (f32[56,128]{1,0:T(8,128)S(1)}, f32[56,128]{1,0:T(8,128)S(1)}, u32[]{:S(2)}, u32[]{:S(2)}) collective-permute-start(f32[56,128]{1,0:T(8,128)S(1)} %get-tuple-element.43), channel_id=1, source_target_pairs={{0,1},{1,0},{2,3},{3,2},{4,5},{5,4},{6,7},{7,6},{8,9},{9,8},{10,11... | collective-permute-start | bytes 86024 | tf_op jit(solution)/shard_map/ppermute | solution.py:435
  17.0 1.7 %shard_map.136 = (f32[16,128]{1,0:T(8,128)S(1)}, bf16[128,128]{1,0:T(8,128)(2,1)S(1)}, bf16[128,128]{1,0:T(8,128)(2,1)S(1)}, f32[8,128]{1,0:T(8,128)S(1)}, f32[1...) custom-call(f32[9,64]{1,0:T(8,128)S(1)} %get-tuple-element.44.d1_ref, ...), custom_call_target="tpu_custom_call" | custom-call | flops 268435456 | bytes 4194304 | tf_op jit(solution)/shard_map/pallas_call | solution.py:439
  18.7 0.0 copy-start
  18.7 0.0 collective-permute-done.outer_ref
  18.7 0.0 collective-permute-done.1.inner_ref
  18.7 1.0 %shard_map.137 = (bf16[16,40,128]{2,1,0:T(8,128)(2,1)S(1)}, f32[18,160,128]{2,1,0:T(8,128)S(1)}, f32[16,16,128]{2,1,0:T(8,128)S(1)}, f32[16,16,128]{2,1,0:T(8,12...) custom-call(f32[16,128,128]{2,1,0:T(8,128)S(1)} %get-tuple-element.41.xt_ref, ...), custom_call_target="tpu_custom_call" | custom-call | flops 134217728 | bytes 4194304 | tf_op jit(solution)/shard_map/pallas_call | solution.py:463
  19.8 19.9 %all_to_all.25.x_ref = bf16[16,40,128]{2,1,0:T(8,128)(2,1)S(1)} all-to-all(bf16[16,40,128]{2,1,0:T(8,128)(2,1)S(1)} %get-tuple-element.58.send_ref), channel_id=1, replica_groups=mesh['member'=16,'tile'=32] {'member'}, dimensions={0} | all-to-all | bytes 327680 | tf_op jit(solution)/shard_map/all_to_all | solution.py:485
  39.6 0.0 copy-done
  39.6 0.8 shard_map.138
  40.4 13.1 %all_to_all.26.cot_ref = bf16[16,40,128]{2,1,0:T(8,128)(2,1)S(1)} all-to-all(bf16[16,40,128]{2,1,0:T(8,128)(2,1)S(1)} %get-tuple-element.60), channel_id=1, replica_groups=mesh['member'=16,'tile'=32] {'member'}, dimensions={0} | all-to-all | bytes 327680 | tf_op jit(solution)/shard_map/all_to_all | solution.py:494
  53.5 2.8 %shard_map.139 = f32[16,4,128]{2,1,0:T(4,128)S(1)} custom-call(bf16[16,40,128]{2,1,0:T(8,128)(2,1)S(1)} %all_to_all.26.cot_ref, f32[18,160,128]{2,1,0:T(8,128)S(1)} %get-tuple-element.61.xs_ref, f32[16,112,128]{2,1,0:T(8,128)S(1)} %get-tuple-element.62.first_ref, f32[16,112,128]{2,1,0:T(8,128)S(1)} %get-tuple-element.63.gate_ref, ...), custom_call_target="tpu_custom_call" | custom-call | flops 268435456 | bytes 4194304 | tf_op jit(solution)/shard_map/pallas_call | solution.py:495
  56.4 12.4 %all_to_all.27 = f32[16,4,128]{2,1,0:T(4,128)S(1)} all-to-all(f32[16,4,128]{2,1,0:T(4,128)S(1)} %shard_map.139), channel_id=1, replica_groups={{0,1,64,65,128,129,192,193,256,257,320,321,384,385,448,449},{2,3,66,67,..., dimensions={0} | all-to-all | bytes 65536 | tf_op jit(solution)/shard_map/all_to_all | solution.py:519
  68.8 11.9 %all_to_all.28 = f32[32,4,128]{2,1,0:T(4,128)S(1)} all-to-all(f32[32,4,128]{2,1,0:T(4,128)S(1)} %broadcast_in_dim.20), channel_id=1, replica_groups={{0,2,4,6,8,10,12,14,16,18,20,22,24,26,28,30,32,34,36,38,40,42,44,46,48,..., dimensions={0} | all-to-all | bytes 131072 | tf_op jit(solution)/shard_map/all_to_all | solution.py:522
  80.8 11.6 %all_to_all.29.total_ref = f32[16,4,128]{2,1,0:T(4,128)S(1)} all-to-all(f32[16,4,128]{2,1,0:T(4,128)S(1)} %broadcast_in_dim.21), channel_id=1, replica_groups={{0,1,64,65,128,129,192,193,256,257,320,321,384,385,448,449},{2,3,66,67,..., dimensions={0} | all-to-all | bytes 65536 | tf_op jit(solution)/shard_map/all_to_all | solution.py:525
  92.3 0.7 shard_map.140
  (4 shorter events, 0.1 us)
Async XLA Ops:
  2.2 16.5 %collective-permute-start = (f32[56,128]{1,0:T(8,128)S(1)}, f32[56,128]{1,0:T(8,128)S(1)}, u32[]{:S(2)}, u32[]{:S(2)}) collective-permute-start(f32[56,128]{1,0:T(8,128)S(1)} %get-tuple-element.42), channel_id=1, source_target_pairs={{0,31},{1,2},{2,1},{3,4},{4,3},{5,6},{6,5},{7,8},{8,7},{9,10},{10,... | collective-permute-start | bytes 86024 | tf_op jit(solution)/shard_map/ppermute | solution.py:434
  7.6 11.1 %collective-permute-start.1 = (f32[56,128]{1,0:T(8,128)S(1)}, f32[56,128]{1,0:T(8,128)S(1)}, u32[]{:S(2)}, u32[]{:S(2)}) collective-permute-start(f32[56,128]{1,0:T(8,128)S(1)} %get-tuple-element.43), channel_id=1, source_target_pairs={{0,1},{1,0},{2,3},{3,2},{4,5},{5,4},{6,7},{7,6},{8,9},{9,8},{10,11... | collective-permute-start | bytes 86024 | tf_op jit(solution)/shard_map/ppermute | solution.py:435
  18.7 20.9 %copy-start = (f32[16,32,128]{2,1,0:T(8,128)S(1)}, f32[16,32,128]{2,1,0:T(8,128)}, u32[]{:S(2)}) copy-start(f32[16,32,128]{2,1,0:T(8,128)} %target_ref.1) | copy-start | bytes 786436

commit v11 on v9

--- a/solution.py
+++ b/solution.py
@@ -256,7 +256,8 @@
 
 
 def crps_kernel(
-    cells_all, x_ref, target_ref, outer_ref, inner_ref, send_ref, out_ref, forecast_hbm, sem
+    cells_all, x_ref, target_ref, outer_ref, inner_ref, send_ref, out_ref, forecast_hbm,
+    value_ref, sem,
 ):
     forecast_copy = pltpu.make_async_copy(send_ref.at[:, 0:32], forecast_hbm.at[0], sem)
     forecast_copy.start()
@@ -281,7 +282,7 @@
         ),
     )
     for rows in (slice(0, 16), slice(16, 32), slice(32, 40)):
-        x = [x_ref[i, rows, :].astype(f32) for i in range(members)]
+        x = [x_ref[i].astype(f32)[rows] for i in range(members)]
         total = [None] * members
         for i in range(members):
             for j in range(i + 1, members):
@@ -291,7 +292,9 @@
         aim = halo if rows.start == 32 else target_ref[me, rows, :]
         for i in range(members):
             value = slope(x[i] - aim) - pair_weight / (members - 1) * total[i]
-            out_ref[i, rows, :] = (value / cells_all).astype(bf16)
+            value_ref[i, rows, :] = value / cells_all
+    for i in range(members):
+        out_ref[i] = value_ref[i].astype(bf16)
     forecast_copy.wait()
 
 
@@ -486,7 +489,7 @@
     cot, out = call(
         functools.partial(crps_kernel, rows * cols * tiles),
         (shape((members, chunk, 128), bf16), shape((1, 16, rows, cols), bf16)),
-        [pltpu.SemaphoreType.DMA],
+        [pltpu.VMEM((members, chunk, 128), f32), pltpu.SemaphoreType.DMA],
         1 << 24,
         passed=5,
         out_specs=(pl.BlockSpec(memory_space=pltpu.VMEM), pl.BlockSpec(memory_space=pltpu.HBM)),

time: 93.5 us -> 93.5 us (level)
  no operation moved by 1% of the time
where the time goes in v11:
time: 93.5 us; the launch traced here: 93.1 us
  blocking collectives  68.9 us (74%)
  starting transfers between devices  14.7 us (16%)
  Pallas kernels  8.63 us (9%)
    all_to_all x1, blocking collectives, local(): seen = lax.all_to_all(send, 'member', 0, 0, tiled=True)  19.9 us
    all_to_all x1, blocking collectives, local(): cot = lax.all_to_all(cot, 'member', 0, 0, tiled=True)  13.1 us
    all_to_all x1, blocking collectives, local(): lax.all_to_all(packed, axes, 0, 0, tiled=True, axis_index_groups=near)  12.7 us
    all_to_all x1, blocking collectives, local(): part = lax.all_to_all(part, axes, 0, 0, tiled=True, axis_index_groups=far)  11.8 us
    all_to_all x1, blocking collectives, local(): total = lax.all_to_all(part, axes, 0, 0, tiled=True, axis_index_groups=near)  11.4 us
    ppermute x1, starting transfers between devices, local(): lax.ppermute(inner, 'tile', [(i, i + 1 - 2 * (i % 2)) for i in range(tile...  9.34 us
    ppermute x1, starting transfers between devices, local(): lax.ppermute(outer, 'tile', [(i, (i + 2 * (i % 2) - 1) % tiles) for i in...  5.39 us
    pallas_call x1, Pallas kernels, local(): call(backward_kernel, shape((16, 4, 128), f32), [pltpu.VMEM((16 * chunk_p...  2.83 us
  transfers between devices with their start and end apart: 2, of which 0 were waited for; matrix products, arithmetic and copies ran while one was open for 0% of the time, Pallas kernels for 2%

profile of v11, /device:TPU:1, one launch (start us, length us, event | category | flops | bytes accessed | tf_op | source)
XLA Modules:
  0.0 93.1 jit_solution(6999443702421067444)
XLA Ops:
  0.6 1.6 %shard_map.135 = (f32[16,128,128]{2,1,0:T(8,128)S(1)}, f32[56,128]{1,0:T(8,128)S(1)}, f32[56,128]{1,0:T(8,128)S(1)}, f32[9,64]{1,0:T(8,128)S(1)}, bf16[64,64]{1,...) custom-call(bf16[1,64,32,128]{3,2,1,0:T(8,128)(2,1)} %x_hbm.1, ...), custom_call_target="tpu_custom_call" | custom-call | flops 1048576 | bytes 4194304 | tf_op jit(solution)/shard_map/pallas_call | solution.py:408
  2.2 5.4 %collective-permute-start = (f32[56,128]{1,0:T(8,128)S(1)}, f32[56,128]{1,0:T(8,128)S(1)}, u32[]{:S(2)}, u32[]{:S(2)}) collective-permute-start(f32[56,128]{1,0:T(8,128)S(1)} %get-tuple-element.42), channel_id=1, source_target_pairs={{0,31},{1,2},{2,1},{3,4},{4,3},{5,6},{6,5},{7,8},{8,7},{9,10},{10,... | collective-permute-start | bytes 86024 | tf_op jit(solution)/shard_map/ppermute | solution.py:437
  7.6 9.3 %collective-permute-start.1 = (f32[56,128]{1,0:T(8,128)S(1)}, f32[56,128]{1,0:T(8,128)S(1)}, u32[]{:S(2)}, u32[]{:S(2)}) collective-permute-start(f32[56,128]{1,0:T(8,128)S(1)} %get-tuple-element.43), channel_id=1, source_target_pairs={{0,1},{1,0},{2,3},{3,2},{4,5},{5,4},{6,7},{7,6},{8,9},{9,8},{10,11... | collective-permute-start | bytes 86024 | tf_op jit(solution)/shard_map/ppermute | solution.py:438
  17.0 1.7 %shard_map.136 = (f32[16,128]{1,0:T(8,128)S(1)}, bf16[128,128]{1,0:T(8,128)(2,1)S(1)}, bf16[128,128]{1,0:T(8,128)(2,1)S(1)}, f32[8,128]{1,0:T(8,128)S(1)}, f32[1...) custom-call(f32[9,64]{1,0:T(8,128)S(1)} %get-tuple-element.44.d1_ref, ...), custom_call_target="tpu_custom_call" | custom-call | flops 268435456 | bytes 4194304 | tf_op jit(solution)/shard_map/pallas_call | solution.py:442
  18.7 0.0 copy-start
  18.7 0.0 collective-permute-done.outer_ref
  18.7 0.0 collective-permute-done.1.inner_ref
  18.7 1.0 %shard_map.137 = (bf16[16,40,128]{2,1,0:T(8,128)(2,1)S(1)}, f32[18,160,128]{2,1,0:T(8,128)S(1)}, f32[16,16,128]{2,1,0:T(8,128)S(1)}, f32[16,16,128]{2,1,0:T(8,12...) custom-call(f32[16,128,128]{2,1,0:T(8,128)S(1)} %get-tuple-element.41.xt_ref, ...), custom_call_target="tpu_custom_call" | custom-call | flops 134217728 | bytes 4194304 | tf_op jit(solution)/shard_map/pallas_call | solution.py:466
  19.8 19.9 %all_to_all.25.x_ref = bf16[16,40,128]{2,1,0:T(8,128)(2,1)S(1)} all-to-all(bf16[16,40,128]{2,1,0:T(8,128)(2,1)S(1)} %get-tuple-element.58.send_ref), channel_id=1, replica_groups=mesh['member'=16,'tile'=32] {'member'}, dimensions={0} | all-to-all | bytes 327680 | tf_op jit(solution)/shard_map/all_to_all | solution.py:488
  39.6 0.0 copy-done
  39.6 0.8 shard_map.138
  40.4 13.1 %all_to_all.26.cot_ref = bf16[16,40,128]{2,1,0:T(8,128)(2,1)S(1)} all-to-all(bf16[16,40,128]{2,1,0:T(8,128)(2,1)S(1)} %get-tuple-element.60), channel_id=1, replica_groups=mesh['member'=16,'tile'=32] {'member'}, dimensions={0} | all-to-all | bytes 327680 | tf_op jit(solution)/shard_map/all_to_all | solution.py:497
  53.5 2.8 %shard_map.139 = f32[16,4,128]{2,1,0:T(4,128)S(1)} custom-call(bf16[16,40,128]{2,1,0:T(8,128)(2,1)S(1)} %all_to_all.26.cot_ref, f32[18,160,128]{2,1,0:T(8,128)S(1)} %get-tuple-element.61.xs_ref, f32[16,112,128]{2,1,0:T(8,128)S(1)} %get-tuple-element.62.first_ref, f32[16,112,128]{2,1,0:T(8,128)S(1)} %get-tuple-element.63.gate_ref, ...), custom_call_target="tpu_custom_call" | custom-call | flops 268435456 | bytes 4194304 | tf_op jit(solution)/shard_map/pallas_call | solution.py:498
  56.4 12.7 %all_to_all.27 = f32[16,4,128]{2,1,0:T(4,128)S(1)} all-to-all(f32[16,4,128]{2,1,0:T(4,128)S(1)} %shard_map.139), channel_id=1, replica_groups={{0,1,2,3,4,5,6,7,8,9,10,11,12,13,14,15},{16,17,18,19,20,21,22,23,24,25,..., dimensions={0} | all-to-all | bytes 65536 | tf_op jit(solution)/shard_map/all_to_all | solution.py:518
  69.1 11.8 %all_to_all.28 = f32[32,4,128]{2,1,0:T(4,128)S(1)} all-to-all(f32[32,4,128]{2,1,0:T(4,128)S(1)} %broadcast_in_dim.20), channel_id=1, replica_groups={{0,16,32,48,64,80,96,112,128,144,160,176,192,208,224,240,256,272,288,30..., dimensions={0} | all-to-all | bytes 131072 | tf_op jit(solution)/shard_map/all_to_all | solution.py:521
  81.0 11.4 %all_to_all.29.total_ref = f32[16,4,128]{2,1,0:T(4,128)S(1)} all-to-all(f32[16,4,128]{2,1,0:T(4,128)S(1)} %broadcast_in_dim.21), channel_id=1, replica_groups={{0,1,2,3,4,5,6,7,8,9,10,11,12,13,14,15},{16,17,18,19,20,21,22,23,24,25,..., dimensions={0} | all-to-all | bytes 65536 | tf_op jit(solution)/shard_map/all_to_all | solution.py:524
  92.4 0.7 shard_map.140
  (4 shorter events, 0.1 us)
Async XLA Ops:
  2.2 16.5 %collective-permute-start = (f32[56,128]{1,0:T(8,128)S(1)}, f32[56,128]{1,0:T(8,128)S(1)}, u32[]{:S(2)}, u32[]{:S(2)}) collective-permute-start(f32[56,128]{1,0:T(8,128)S(1)} %get-tuple-element.42), channel_id=1, source_target_pairs={{0,31},{1,2},{2,1},{3,4},{4,3},{5,6},{6,5},{7,8},{8,7},{9,10},{10,... | collective-permute-start | bytes 86024 | tf_op jit(solution)/shard_map/ppermute | solution.py:437
  7.6 11.1 %collective-permute-start.1 = (f32[56,128]{1,0:T(8,128)S(1)}, f32[56,128]{1,0:T(8,128)S(1)}, u32[]{:S(2)}, u32[]{:S(2)}) collective-permute-start(f32[56,128]{1,0:T(8,128)S(1)} %get-tuple-element.43), channel_id=1, source_target_pairs={{0,1},{1,0},{2,3},{3,2},{4,5},{5,4},{6,7},{7,6},{8,9},{9,8},{10,11... | collective-permute-start | bytes 86024 | tf_op jit(solution)/shard_map/ppermute | solution.py:438
  18.7 20.9 %copy-start = (f32[16,32,128]{2,1,0:T(8,128)S(1)}, f32[16,32,128]{2,1,0:T(8,128)}, u32[]{:S(2)}) copy-start(f32[16,32,128]{2,1,0:T(8,128)} %target_ref.1) | copy-start | bytes 786436

commit v12 on v11

--- a/solution.py
+++ b/solution.py
@@ -318,16 +318,21 @@
     point_one_ref[...] = jnp.zeros(point_one_ref.shape, f32)
     other_ref[...] = jnp.zeros(other_ref.shape, f32)
 
-    def cot_body(p):
+    parts = []
+    for p in range(slabs):
         cot = jnp.concatenate(
-            [cf_ref[pl.ds(p, 16, stride=chunk_pitch), :], cf_ref[pl.ds(16 + p, 16, stride=chunk_pitch), :]], axis=0
+            [
+                cf_ref[pl.ds(p, 16, stride=chunk_pitch), :],
+                cf_ref[pl.ds(16 + p, 16, stride=chunk_pitch), :],
+            ],
+            axis=0,
         )
         cot_sum_ref[0:32] += cot
-        cot = cot.astype(bf16)
-        bs_ref[p + 1, own : own + 128, :] = rounded(dot(cot, two, 0, 0))
-        point_two_ref[...] += dot(cot, second_ref[p], 1, 0)
-
-    each_slab(cot_body)
+        parts.append(cot.astype(bf16))
+    for p in range(slabs):
+        bs_ref[p + 1, own : own + 128, :] = rounded(dot(parts[p], two, 0, 0))
+    cot = jnp.concatenate(parts, axis=1)
+    point_two_ref[...] = dot(cot, second_ref[...].reshape(128 * slabs, 128), 1, 0)
     halo = cf_ref[pl.ds(32, 16, stride=chunk_pitch), :]
     halo = jnp.concatenate([halo, pltpu.roll(halo, 96, 1)], axis=0).astype(bf16)
     halo = rounded(dot(halo, two, 0, 0))
@@ -513,7 +518,12 @@
         cot, xs, first, gate, hidden, edge_first, edge_gate, edge_hidden, second, one, two, taps_two
     )
     axes = ("member", "tile")
-    near = [[16 * g + k for k in range(16)] for g in range(members * tiles // 16)]
+    near = [
+        [16 * (2 * (2 * y + x_hi) + x_lo) + 2 * z + core for core in range(2) for z in range(8)]
+        for x_hi in range(2)
+        for x_lo in range(2)
+        for y in range(8)
+    ]
     far = [list(group) for group in zip(*near)]
     part = lax.all_to_all(packed, axes, 0, 0, tiled=True, axis_index_groups=near)
     part = jnp.sum(part, axis=0)

time: 93.5 us -> 93 us (level)
  no operation moved by 1% of the time
where the time goes in v12:
time: 93 us; the launch traced here: 92.7 us
  blocking collectives  68.5 us (74%)
  starting transfers between devices  14.7 us (16%)
  Pallas kernels  8.64 us (9%)
    all_to_all x1, blocking collectives, local(): seen = lax.all_to_all(send, 'member', 0, 0, tiled=True)  19.9 us
    all_to_all x1, blocking collectives, local(): cot = lax.all_to_all(cot, 'member', 0, 0, tiled=True)  13.1 us
    all_to_all x1, blocking collectives, local(): lax.all_to_all(packed, axes, 0, 0, tiled=True, axis_index_groups=near)  12.4 us
    all_to_all x1, blocking collectives, local(): part = lax.all_to_all(part, axes, 0, 0, tiled=True, axis_index_groups=far)  11.8 us
    all_to_all x1, blocking collectives, local(): total = lax.all_to_all(part, axes, 0, 0, tiled=True, axis_index_groups=near)  11.3 us
    ppermute x1, starting transfers between devices, local(): lax.ppermute(inner, 'tile', [(i, i + 1 - 2 * (i % 2)) for i in range(tile...  9.34 us
    ppermute x1, starting transfers between devices, local(): lax.ppermute(outer, 'tile', [(i, (i + 2 * (i % 2) - 1) % tiles) for i in...  5.39 us
    pallas_call x1, Pallas kernels, local(): call(backward_kernel, shape((16, 4, 128), f32), [pltpu.VMEM((16 * chunk_p...  2.84 us
  transfers between devices with their start and end apart: 2, of which 0 were waited for; matrix products, arithmetic and copies ran while one was open for 0% of the time, Pallas kernels for 2%

profile of v12, /device:TPU:1, one launch (start us, length us, event | category | flops | bytes accessed | tf_op | source)
XLA Modules:
  0.0 92.7 jit_solution(11502527738685812127)
XLA Ops:
  0.6 1.6 %shard_map.135 = (f32[16,128,128]{2,1,0:T(8,128)S(1)}, f32[56,128]{1,0:T(8,128)S(1)}, f32[56,128]{1,0:T(8,128)S(1)}, f32[9,64]{1,0:T(8,128)S(1)}, bf16[64,64]{1,...) custom-call(bf16[1,64,32,128]{3,2,1,0:T(8,128)(2,1)} %x_hbm.1, ...), custom_call_target="tpu_custom_call" | custom-call | flops 1048576 | bytes 4194304 | tf_op jit(solution)/shard_map/pallas_call | solution.py:413
  2.2 5.4 %collective-permute-start = (f32[56,128]{1,0:T(8,128)S(1)}, f32[56,128]{1,0:T(8,128)S(1)}, u32[]{:S(2)}, u32[]{:S(2)}) collective-permute-start(f32[56,128]{1,0:T(8,128)S(1)} %get-tuple-element.42), channel_id=1, source_target_pairs={{0,31},{1,2},{2,1},{3,4},{4,3},{5,6},{6,5},{7,8},{8,7},{9,10},{10,... | collective-permute-start | bytes 86024 | tf_op jit(solution)/shard_map/ppermute | solution.py:442
  7.6 9.3 %collective-permute-start.1 = (f32[56,128]{1,0:T(8,128)S(1)}, f32[56,128]{1,0:T(8,128)S(1)}, u32[]{:S(2)}, u32[]{:S(2)}) collective-permute-start(f32[56,128]{1,0:T(8,128)S(1)} %get-tuple-element.43), channel_id=1, source_target_pairs={{0,1},{1,0},{2,3},{3,2},{4,5},{5,4},{6,7},{7,6},{8,9},{9,8},{10,11... | collective-permute-start | bytes 86024 | tf_op jit(solution)/shard_map/ppermute | solution.py:443
  17.0 1.7 %shard_map.136 = (f32[16,128]{1,0:T(8,128)S(1)}, bf16[128,128]{1,0:T(8,128)(2,1)S(1)}, bf16[128,128]{1,0:T(8,128)(2,1)S(1)}, f32[8,128]{1,0:T(8,128)S(1)}, f32[1...) custom-call(f32[9,64]{1,0:T(8,128)S(1)} %get-tuple-element.44.d1_ref, ...), custom_call_target="tpu_custom_call" | custom-call | flops 268435456 | bytes 4194304 | tf_op jit(solution)/shard_map/pallas_call | solution.py:447
  18.7 0.0 copy-start
  18.7 0.0 collective-permute-done.outer_ref
  18.7 0.0 collective-permute-done.1.inner_ref
  18.7 1.0 %shard_map.137 = (bf16[16,40,128]{2,1,0:T(8,128)(2,1)S(1)}, f32[18,160,128]{2,1,0:T(8,128)S(1)}, f32[16,16,128]{2,1,0:T(8,128)S(1)}, f32[16,16,128]{2,1,0:T(8,12...) custom-call(f32[16,128,128]{2,1,0:T(8,128)S(1)} %get-tuple-element.41.xt_ref, ...), custom_call_target="tpu_custom_call" | custom-call | flops 134217728 | bytes 4194304 | tf_op jit(solution)/shard_map/pallas_call | solution.py:471
  19.8 19.9 %all_to_all.25.x_ref = bf16[16,40,128]{2,1,0:T(8,128)(2,1)S(1)} all-to-all(bf16[16,40,128]{2,1,0:T(8,128)(2,1)S(1)} %get-tuple-element.58.send_ref), channel_id=1, replica_groups=mesh['member'=16,'tile'=32] {'member'}, dimensions={0} | all-to-all | bytes 327680 | tf_op jit(solution)/shard_map/all_to_all | solution.py:493
  39.6 0.0 copy-done
  39.6 0.8 shard_map.138
  40.4 13.1 %all_to_all.26.cot_ref = bf16[16,40,128]{2,1,0:T(8,128)(2,1)S(1)} all-to-all(bf16[16,40,128]{2,1,0:T(8,128)(2,1)S(1)} %get-tuple-element.60), channel_id=1, replica_groups=mesh['member'=16,'tile'=32] {'member'}, dimensions={0} | all-to-all | bytes 327680 | tf_op jit(solution)/shard_map/all_to_all | solution.py:502
  53.5 2.8 %shard_map.139 = f32[16,4,128]{2,1,0:T(4,128)S(1)} custom-call(bf16[16,40,128]{2,1,0:T(8,128)(2,1)S(1)} %all_to_all.26.cot_ref, f32[18,160,128]{2,1,0:T(8,128)S(1)} %get-tuple-element.61.xs_ref, f32[16,112,128]{2,1,0:T(8,128)S(1)} %get-tuple-element.62.first_ref, f32[16,112,128]{2,1,0:T(8,128)S(1)} %get-tuple-element.63.gate_ref, ...), custom_call_target="tpu_custom_call" | custom-call | flops 268435456 | bytes 4194304 | tf_op jit(solution)/shard_map/pallas_call | solution.py:503
  56.4 12.4 %all_to_all.27 = f32[16,4,128]{2,1,0:T(4,128)S(1)} all-to-all(f32[16,4,128]{2,1,0:T(4,128)S(1)} %shard_map.139), channel_id=1, replica_groups={{0,2,4,6,8,10,12,14,1,3,5,7,9,11,13,15},{64,66,68,70,72,74,76,78,65,67,..., dimensions={0} | all-to-all | bytes 65536 | tf_op jit(solution)/shard_map/all_to_all | solution.py:528
  68.8 11.8 %all_to_all.28 = f32[32,4,128]{2,1,0:T(4,128)S(1)} all-to-all(f32[32,4,128]{2,1,0:T(4,128)S(1)} %broadcast_in_dim.20), channel_id=1, replica_groups={{0,64,128,192,256,320,384,448,16,80,144,208,272,336,400,464,32,96,160,2..., dimensions={0} | all-to-all | bytes 131072 | tf_op jit(solution)/shard_map/all_to_all | solution.py:531
  80.6 11.3 %all_to_all.29.total_ref = f32[16,4,128]{2,1,0:T(4,128)S(1)} all-to-all(f32[16,4,128]{2,1,0:T(4,128)S(1)} %broadcast_in_dim.21), channel_id=1, replica_groups={{0,2,4,6,8,10,12,14,1,3,5,7,9,11,13,15},{64,66,68,70,72,74,76,78,65,67,..., dimensions={0} | all-to-all | bytes 65536 | tf_op jit(solution)/shard_map/all_to_all | solution.py:534
  92.0 0.7 shard_map.140
  (4 shorter events, 0.1 us)
Async XLA Ops:
  2.2 16.5 %collective-permute-start = (f32[56,128]{1,0:T(8,128)S(1)}, f32[56,128]{1,0:T(8,128)S(1)}, u32[]{:S(2)}, u32[]{:S(2)}) collective-permute-start(f32[56,128]{1,0:T(8,128)S(1)} %get-tuple-element.42), channel_id=1, source_target_pairs={{0,31},{1,2},{2,1},{3,4},{4,3},{5,6},{6,5},{7,8},{8,7},{9,10},{10,... | collective-permute-start | bytes 86024 | tf_op jit(solution)/shard_map/ppermute | solution.py:442
  7.6 11.1 %collective-permute-start.1 = (f32[56,128]{1,0:T(8,128)S(1)}, f32[56,128]{1,0:T(8,128)S(1)}, u32[]{:S(2)}, u32[]{:S(2)}) collective-permute-start(f32[56,128]{1,0:T(8,128)S(1)} %get-tuple-element.43), channel_id=1, source_target_pairs={{0,1},{1,0},{2,3},{3,2},{4,5},{5,4},{6,7},{7,6},{8,9},{9,8},{10,11... | collective-permute-start | bytes 86024 | tf_op jit(solution)/shard_map/ppermute | solution.py:443
  18.7 20.9 %copy-start = (f32[16,32,128]{2,1,0:T(8,128)S(1)}, f32[16,32,128]{2,1,0:T(8,128)}, u32[]{:S(2)}) copy-start(f32[16,32,128]{2,1,0:T(8,128)} %target_ref.1) | copy-start | bytes 786436

commit v13 on v12

--- a/solution.py
+++ b/solution.py
@@ -263,6 +263,7 @@
     forecast_copy.start()
     members = x_ref.shape[0]
     me = lax.axis_index("member")
+    me = lax.rem(me, 2) * (members // 2) + me // 2
     turn = lax.rem(4 - lax.rem(me, 4), 4) * 32
     even = even_tile()
     outer = outer_ref[pl.ds(48 + me // 4, 1), :]
@@ -490,7 +491,12 @@
     )(
         xt, outer, inner, hidden, main_second, taps_one, one_turned, bias_one, taps_two, two, bias_two
     )
-    seen = lax.all_to_all(send, "member", 0, 0, tiled=True)
+    axes = ("member", "tile")
+    ring = [
+        [tiles * (2 * y + x_hi) + t for x_hi in range(2) for y in range(members // 2)]
+        for t in range(tiles)
+    ]
+    seen = lax.all_to_all(send, axes, 0, 0, tiled=True, axis_index_groups=ring)
     cot, out = call(
         functools.partial(crps_kernel, rows * cols * tiles),
         (shape((members, chunk, 128), bf16), shape((1, 16, rows, cols), bf16)),
@@ -499,7 +505,7 @@
         passed=5,
         out_specs=(pl.BlockSpec(memory_space=pltpu.VMEM), pl.BlockSpec(memory_space=pltpu.HBM)),
     )(seen, target, outer, inner, send)
-    cot = lax.all_to_all(cot, "member", 0, 0, tiled=True)
+    cot = lax.all_to_all(cot, axes, 0, 0, tiled=True, axis_index_groups=ring)
     packed = call(
         backward_kernel,
         shape((16, 4, 128), f32),
@@ -517,7 +523,6 @@
     )(
         cot, xs, first, gate, hidden, edge_first, edge_gate, edge_hidden, second, one, two, taps_two
     )
-    axes = ("member", "tile")
     near = [
         [16 * (2 * (2 * y + x_hi) + x_lo) + 2 * z + core for core in range(2) for z in range(8)]
         for x_hi in range(2)

time: 93 us -> 91.9 us (0.988)
  blocking collectives: 68.5 us -> 67.3 us
    all_to_all x2, blocking collectives: 33 us -> 31.6 us  [the longest x1 17.9 us: local(): seen = lax.all_to_all(send, axes, 0, 0, tiled=True, axis_index_groups=ring)]
where the time goes in v13:
time: 91.9 us; the launch traced here: 91.5 us
  blocking collectives  67.3 us (73%)
  starting transfers between devices  14.7 us (16%)
  Pallas kernels  8.64 us (9%)
    all_to_all x1, blocking collectives, local(): seen = lax.all_to_all(send, axes, 0, 0, tiled=True, axis_index_groups=ring)  17.9 us
    all_to_all x1, blocking collectives, local(): cot = lax.all_to_all(cot, axes, 0, 0, tiled=True, axis_index_groups=ring)  13.6 us
    all_to_all x1, blocking collectives, local(): part = lax.all_to_all(part, axes, 0, 0, tiled=True, axis_index_groups=far)  12.2 us
    all_to_all x1, blocking collectives, local(): lax.all_to_all(packed, axes, 0, 0, tiled=True, axis_index_groups=near)  11.9 us
    all_to_all x1, blocking collectives, local(): total = lax.all_to_all(part, axes, 0, 0, tiled=True, axis_index_groups=near)  11.6 us
    ppermute x1, starting transfers between devices, local(): lax.ppermute(inner, 'tile', [(i, i + 1 - 2 * (i % 2)) for i in range(tile...  9.34 us
    ppermute x1, starting transfers between devices, local(): lax.ppermute(outer, 'tile', [(i, (i + 2 * (i % 2) - 1) % tiles) for i in...  5.39 us
    pallas_call x1, Pallas kernels, local(): call(backward_kernel, shape((16, 4, 128), f32), [pltpu.VMEM((16 * chunk_p...  2.83 us
  transfers between devices with their start and end apart: 2, of which 0 were waited for; matrix products, arithmetic and copies ran while one was open for 0% of the time, Pallas kernels for 2%

profile of v13, /device:TPU:1, one launch (start us, length us, event | category | flops | bytes accessed | tf_op | source)
XLA Modules:
  0.0 91.5 jit_solution(10069006500033879095)
XLA Ops:
  0.6 1.6 %shard_map.135 = (f32[16,128,128]{2,1,0:T(8,128)S(1)}, f32[56,128]{1,0:T(8,128)S(1)}, f32[56,128]{1,0:T(8,128)S(1)}, f32[9,64]{1,0:T(8,128)S(1)}, bf16[64,64]{1,...) custom-call(bf16[1,64,32,128]{3,2,1,0:T(8,128)(2,1)} %x_hbm.1, ...), custom_call_target="tpu_custom_call" | custom-call | flops 1048576 | bytes 4194304 | tf_op jit(solution)/shard_map/pallas_call | solution.py:414
  2.2 5.4 %collective-permute-start = (f32[56,128]{1,0:T(8,128)S(1)}, f32[56,128]{1,0:T(8,128)S(1)}, u32[]{:S(2)}, u32[]{:S(2)}) collective-permute-start(f32[56,128]{1,0:T(8,128)S(1)} %get-tuple-element.42), channel_id=1, source_target_pairs={{0,31},{1,2},{2,1},{3,4},{4,3},{5,6},{6,5},{7,8},{8,7},{9,10},{10,... | collective-permute-start | bytes 86024 | tf_op jit(solution)/shard_map/ppermute | solution.py:443
  7.6 9.3 %collective-permute-start.1 = (f32[56,128]{1,0:T(8,128)S(1)}, f32[56,128]{1,0:T(8,128)S(1)}, u32[]{:S(2)}, u32[]{:S(2)}) collective-permute-start(f32[56,128]{1,0:T(8,128)S(1)} %get-tuple-element.43), channel_id=1, source_target_pairs={{0,1},{1,0},{2,3},{3,2},{4,5},{5,4},{6,7},{7,6},{8,9},{9,8},{10,11... | collective-permute-start | bytes 86024 | tf_op jit(solution)/shard_map/ppermute | solution.py:444
  17.0 1.7 %shard_map.136 = (f32[16,128]{1,0:T(8,128)S(1)}, bf16[128,128]{1,0:T(8,128)(2,1)S(1)}, bf16[128,128]{1,0:T(8,128)(2,1)S(1)}, f32[8,128]{1,0:T(8,128)S(1)}, f32[1...) custom-call(f32[9,64]{1,0:T(8,128)S(1)} %get-tuple-element.44.d1_ref, ...), custom_call_target="tpu_custom_call" | custom-call | flops 268435456 | bytes 4194304 | tf_op jit(solution)/shard_map/pallas_call | solution.py:448
  18.7 0.0 copy-start
  18.7 0.0 collective-permute-done.outer_ref
  18.7 0.0 collective-permute-done.1.inner_ref
  18.7 1.0 %shard_map.137 = (bf16[16,40,128]{2,1,0:T(8,128)(2,1)S(1)}, f32[18,160,128]{2,1,0:T(8,128)S(1)}, f32[16,16,128]{2,1,0:T(8,128)S(1)}, f32[16,16,128]{2,1,0:T(8,12...) custom-call(f32[16,128,128]{2,1,0:T(8,128)S(1)} %get-tuple-element.41.xt_ref, ...), custom_call_target="tpu_custom_call" | custom-call | flops 134217728 | bytes 4194304 | tf_op jit(solution)/shard_map/pallas_call | solution.py:472
  19.8 17.9 %all_to_all.25.x_ref = bf16[16,40,128]{2,1,0:T(8,128)(2,1)S(1)} all-to-all(bf16[16,40,128]{2,1,0:T(8,128)(2,1)S(1)} %get-tuple-element.58.send_ref), channel_id=1, replica_groups={{0,64,128,192,256,320,384,448,32,96,160,224,288,352,416,480},{1,65,129,..., dimensions={0} | all-to-all | bytes 327680 | tf_op jit(solution)/shard_map/all_to_all | solution.py:499
  37.7 0.0 copy-done
  37.7 0.8 shard_map.138
  38.5 13.6 %all_to_all.26.cot_ref = bf16[16,40,128]{2,1,0:T(8,128)(2,1)S(1)} all-to-all(bf16[16,40,128]{2,1,0:T(8,128)(2,1)S(1)} %get-tuple-element.60), channel_id=1, replica_groups={{0,64,128,192,256,320,384,448,32,96,160,224,288,352,416,480},{1,65,129,..., dimensions={0} | all-to-all | bytes 327680 | tf_op jit(solution)/shard_map/all_to_all | solution.py:508
  52.1 2.8 %shard_map.139 = f32[16,4,128]{2,1,0:T(4,128)S(1)} custom-call(bf16[16,40,128]{2,1,0:T(8,128)(2,1)S(1)} %all_to_all.26.cot_ref, f32[18,160,128]{2,1,0:T(8,128)S(1)} %get-tuple-element.61.xs_ref, f32[16,112,128]{2,1,0:T(8,128)S(1)} %get-tuple-element.62.first_ref, f32[16,112,128]{2,1,0:T(8,128)S(1)} %get-tuple-element.63.gate_ref, ...), custom_call_target="tpu_custom_call" | custom-call | flops 268435456 | bytes 4194304 | tf_op jit(solution)/shard_map/pallas_call | solution.py:509
  55.0 11.9 %all_to_all.27 = f32[16,4,128]{2,1,0:T(4,128)S(1)} all-to-all(f32[16,4,128]{2,1,0:T(4,128)S(1)} %shard_map.139), channel_id=1, replica_groups={{0,2,4,6,8,10,12,14,1,3,5,7,9,11,13,15},{64,66,68,70,72,74,76,78,65,67,..., dimensions={0} | all-to-all | bytes 65536 | tf_op jit(solution)/shard_map/all_to_all | solution.py:533
  66.9 12.2 %all_to_all.28 = f32[32,4,128]{2,1,0:T(4,128)S(1)} all-to-all(f32[32,4,128]{2,1,0:T(4,128)S(1)} %broadcast_in_dim.20), channel_id=1, replica_groups={{0,64,128,192,256,320,384,448,16,80,144,208,272,336,400,464,32,96,160,2..., dimensions={0} | all-to-all | bytes 131072 | tf_op jit(solution)/shard_map/all_to_all | solution.py:536
  79.2 11.6 %all_to_all.29.total_ref = f32[16,4,128]{2,1,0:T(4,128)S(1)} all-to-all(f32[16,4,128]{2,1,0:T(4,128)S(1)} %broadcast_in_dim.21), channel_id=1, replica_groups={{0,2,4,6,8,10,12,14,1,3,5,7,9,11,13,15},{64,66,68,70,72,74,76,78,65,67,..., dimensions={0} | all-to-all | bytes 65536 | tf_op jit(solution)/shard_map/all_to_all | solution.py:539
  90.8 0.7 shard_map.140
  (4 shorter events, 0.1 us)
Async XLA Ops:
  2.2 16.5 %collective-permute-start = (f32[56,128]{1,0:T(8,128)S(1)}, f32[56,128]{1,0:T(8,128)S(1)}, u32[]{:S(2)}, u32[]{:S(2)}) collective-permute-start(f32[56,128]{1,0:T(8,128)S(1)} %get-tuple-element.42), channel_id=1, source_target_pairs={{0,31},{1,2},{2,1},{3,4},{4,3},{5,6},{6,5},{7,8},{8,7},{9,10},{10,... | collective-permute-start | bytes 86024 | tf_op jit(solution)/shard_map/ppermute | solution.py:443
  7.6 11.1 %collective-permute-start.1 = (f32[56,128]{1,0:T(8,128)S(1)}, f32[56,128]{1,0:T(8,128)S(1)}, u32[]{:S(2)}, u32[]{:S(2)}) collective-permute-start(f32[56,128]{1,0:T(8,128)S(1)} %get-tuple-element.43), channel_id=1, source_target_pairs={{0,1},{1,0},{2,3},{3,2},{4,5},{5,4},{6,7},{7,6},{8,9},{9,8},{10,11... | collective-permute-start | bytes 86024 | tf_op jit(solution)/shard_map/ppermute | solution.py:444
  18.7 19.0 %copy-start = (f32[16,32,128]{2,1,0:T(8,128)S(1)}, f32[16,32,128]{2,1,0:T(8,128)}, u32[]{:S(2)}) copy-start(f32[16,32,128]{2,1,0:T(8,128)} %target_ref.1) | copy-start | bytes 786436
